TPU v7x, 128 devices: a whole 4x4x4 slice. The times are simulated.
128 devices in a mesh: seq: 16 (over x, y), dp: 4 (over z), rep: 2 (over core).
Axes of the slice: x: 4, y: 4, z: 4, core: 2. Of those that a mesh axis runs over, the one named last changes fastest.
Arguments:
- hidden: bfloat16 [4, 8192, 8192], P('dp', 'seq'), may hold values from -6 to 6
- kept: int32 [4, 16, 192], P('dp'), may hold values from 0 to 511, as said below
- counts: int32 [4, 16], P('dp'), may hold values from 48 to 192, as said below
- queries: bfloat16 [4, 3072, 4096], P('dp', 'seq', 'rep'), may hold values from -6 to 6
- keys: bfloat16 [4, 3072, 512], P('dp', 'seq', 'rep'), may hold values from -6 to 6
- values: bfloat16 [4, 3072, 512], P('dp', 'seq', 'rep'), may hold values from -6 to 6
- out_grad: bfloat16 [4, 3072, 4096], P('dp', 'seq', 'rep'), may hold values from -6 to 6
- kv_weight: bfloat16 [8192, 2, 512], P('dp', None, 'rep'), may hold values from -0.0625 to 0.0625
Outputs:
- grad_queries: bfloat16 [4, 3072, 4096], P('dp', 'seq', 'rep')
- grad_hidden: bfloat16 [4, 8192, 8192], P('dp', 'seq', 'rep')
- grad_kv_weight: float32 [8192, 2, 512], P(('seq', 'dp'), None, 'rep')
Inputs may be any that keep to these rules, and one draw needn't show every extreme that they name: `counts`: in every sequence some shard keeps exactly 192 tokens. `kept`: the first counts[b, s] entries of a shard's list are distinct token indices of that shard in rising order; the other entries are arbitrary token indices.
All inputs are finite; a program needn't handle non-finite values.
Results may differ from a plain program's by a relative error of at most 0.012.
Values may be sent and summed in bfloat16 or wider, within the bound.
No kernel may reach another device: no remote copies, remote signals or barrier semaphores. Data moves between devices by JAX's collectives and lax.ppermute only.
A program may use at most 128 MiB of HBM per device.

v0:
```python
import functools

import jax
import jax.numpy as jnp
from jax import lax
from jax.experimental import pallas as pl
from jax.experimental.pallas import tpu as pltpu
from jax.sharding import PartitionSpec as P

HEAD = 128
MASKED = -1e30
LOG2E = 1.4426950408889634
ROWS_ROWS = (((1,), (1,)), ((), ()))
ROWS_COLS = (((1,), (0,)), ((), ()))
QT = 512
KT = 512
VMEM_BYTES = 56 * 1024 * 1024
SIDE = 4


def gather_kernel(place, rows_ref, hidden_ref, out_ref, pick_ref):
    capacity, tokens = rows_ref.shape[0], hidden_ref.shape[0]

    @pl.when(pl.program_id(0) == 0)
    def _():
        token = lax.broadcasted_iota(jnp.int32, (capacity, tokens), 1)
        pick_ref[...] = (token == rows_ref[...]).astype(jnp.bfloat16)

    picked = lax.dot_general(
        pick_ref[...], hidden_ref[...], ROWS_COLS, preferred_element_type=jnp.float32
    ).astype(jnp.bfloat16)
    parts = out_ref.shape[0]
    for part in range(parts):
        for block in range(out_ref.shape[2] // HEAD):
            first = (block * parts + part) * HEAD
            out_ref[part, :, block * HEAD : (block + 1) * HEAD] = picked[:, first : first + HEAD]


def gather_columns(place, rows, hidden, parts, cores):
    capacity = rows.shape[0]
    tokens, width = hidden.shape
    half = width // cores
    steps = 4
    block = half // steps
    return pl.pallas_call(
        gather_kernel,
        grid_spec=pltpu.PrefetchScalarGridSpec(
            num_scalar_prefetch=1,
            grid=(steps,),
            in_specs=[
                pl.BlockSpec((capacity, 1), lambda s, place: (0, 0)),
                pl.BlockSpec((tokens, block), lambda s, place: (0, place[4] * steps + s)),
            ],
            out_specs=pl.BlockSpec((parts, capacity, block // parts), lambda s, place: (0, 0, s)),
            scratch_shapes=[pltpu.VMEM((capacity, tokens), jnp.bfloat16)],
        ),
        out_shape=jax.ShapeDtypeStruct((parts, capacity, half // parts), hidden.dtype),
        cost_estimate=pl.CostEstimate(
            flops=800_000_000, bytes_accessed=6_000_000, transcendentals=0
        ),
        name="gather_columns",
    )(place, rows[:, None], hidden)


def y_sum_kernel(place, *refs):
    parts, outs = refs[:4], refs[4:]
    cap = outs[0].shape[0]
    for step, out in enumerate(outs):
        at = pl.ds(pl.multiple_of(((place[0] + step) % len(outs)) * cap, 64), cap)
        total = parts[0][at, :].astype(jnp.float32)
        for part in parts[1:]:
            total = total + part[at, :].astype(jnp.float32)
        out[...] = total.astype(jnp.bfloat16)


def y_sum(place, parts):
    rows, width = parts[0].shape
    vmem = pl.BlockSpec(memory_space=pltpu.VMEM)
    return pl.pallas_call(
        y_sum_kernel,
        in_specs=[pl.BlockSpec(memory_space=pltpu.SMEM)] + [vmem] * len(parts),
        out_specs=[vmem] * len(parts),
        out_shape=[jax.ShapeDtypeStruct((rows // len(parts), width), jnp.bfloat16)] * len(parts),
        cost_estimate=pl.CostEstimate(
            flops=1_000_000, bytes_accessed=2_000_000, transcendentals=0
        ),
        name="y_sum",
    )(place, *parts)


def x_sum_kernel(place, *refs):
    parts, out_ref, by_x = refs[:-2], refs[-2], refs[-1]
    cap = out_ref.shape[0]
    count = len(parts)
    groups = out_ref.shape[1] // (2 * HEAD)
    for step, part in enumerate(parts):
        at = pl.ds(pl.multiple_of(((place[0] - step) % count) * cap, 64), cap)
        by_x[at, :] = part[...].astype(jnp.float32)
    size = count // groups
    for group in range(groups):
        total = by_x[group * size * cap : (group * size + 1) * cap, :]
        for x in range(group * size + 1, (group + 1) * size):
            total = total + by_x[x * cap : (x + 1) * cap, :]
        total = total.astype(jnp.bfloat16)
        for kind in range(2):
            first = (kind * groups + group) * HEAD
            out_ref[:, first : first + HEAD] = total[:, kind * HEAD : (kind + 1) * HEAD]


def x_sum(place, parts, groups):
    rows, width = parts[0].shape
    vmem = pl.BlockSpec(memory_space=pltpu.VMEM)
    return pl.pallas_call(
        x_sum_kernel,
        in_specs=[pl.BlockSpec(memory_space=pltpu.SMEM)] + [vmem] * len(parts),
        out_specs=vmem,
        out_shape=jax.ShapeDtypeStruct((rows, groups * width), jnp.bfloat16),
        scratch_shapes=[pltpu.VMEM((rows * len(parts), width), jnp.float32)],
        cost_estimate=pl.CostEstimate(
            flops=1_000_000, bytes_accessed=1_000_000, transcendentals=0
        ),
        name="x_sum",
    )(place, *parts)


def terms_kernel(place, own_ref, other_ref, *refs):
    kv, (out_ref, columns_s, kv_s) = refs[:-3], refs[-3:]
    count, cap = len(kv), kv[0].shape[0]
    step = pl.program_id(0)

    def collect(columns_ref):
        for index in range(count):
            held = (place[3] - index) % count
            columns_s[index * cap : (index + 1) * cap, :] = columns_ref[held]

    @pl.when(step == 0)
    def _():
        collect(own_ref)
        for index, part in enumerate(kv):
            kv_s[index * cap : (index + 1) * cap, :] = part[...]

    @pl.when(step == 1)
    def _():
        collect(other_ref)

    out_ref[...] = lax.dot_general(
        columns_s[...], kv_s[...], (((0,), (0,)), ((), ())), preferred_element_type=jnp.float32
    ).astype(jnp.bfloat16)


def weight_terms(place, own, other, kv):
    count, cap, half = own.shape
    width = kv[0].shape[1]
    columns = pl.BlockSpec((count, cap, half), lambda s, place: (0, 0, 0))
    return pl.pallas_call(
        terms_kernel,
        grid_spec=pltpu.PrefetchScalarGridSpec(
            num_scalar_prefetch=1,
            grid=(2,),
            in_specs=[columns] * 2
            + [pl.BlockSpec((cap, width), lambda s, place: (0, 0))] * len(kv),
            out_specs=pl.BlockSpec((half, width), lambda s, place: ((s + place[4]) % 2, 0)),
            scratch_shapes=[
                pltpu.VMEM((count * cap, half), jnp.bfloat16),
                pltpu.VMEM((count * cap, width), jnp.bfloat16),
            ],
        ),
        out_shape=jax.ShapeDtypeStruct((2 * half, width), jnp.bfloat16),
        compiler_params=pltpu.CompilerParams(vmem_limit_bytes=VMEM_BYTES),
        cost_estimate=pl.CostEstimate(
            flops=1_600_000_000, bytes_accessed=6_000_000, transcendentals=0
        ),
        name="weight_terms",
    )(place, own, other, *kv)


def products_kernel(place, *refs):
    w_own, w_other, out_s, kv_s = refs[-4:]
    count = (len(refs) - 4) // 3
    own, other, parts = refs[:count], refs[count : 2 * count], refs[2 * count : 3 * count]
    cap, half = own[0].shape
    for index in range(count):
        kv_s[index * cap : (index + 1) * cap, :half] = own[index][...]
        kv_s[index * cap : (index + 1) * cap, half:] = other[index][...]
    chunk = 256
    for first in range(0, out_s.shape[1], chunk):
        here = slice(first, first + chunk)
        total = lax.dot_general(
            kv_s[:, :half], w_own[here, :], ROWS_ROWS, preferred_element_type=jnp.float32
        ) + lax.dot_general(
            kv_s[:, half:], w_other[here, :], ROWS_ROWS, preferred_element_type=jnp.float32
        )
        out_s[:, here] = total.astype(jnp.bfloat16)
    for step, part in enumerate(parts):
        held = (place[3] - place[5] - step) % count
        part[...] = out_s[pl.ds(pl.multiple_of(held * cap, 64), cap), :]


def input_products(place, own, other, w_own, w_other):
    cap, half = own[0].shape
    count, width = len(own), w_own.shape[0]
    vmem = pl.BlockSpec(memory_space=pltpu.VMEM)

    def body(place, *refs):
        ins, outs, scratch = refs[: 2 * count + 2], refs[2 * count + 2 : 3 * count + 2], refs[3 * count + 2 :]
        products_kernel(place, *ins[: 2 * count], *outs, ins[-2], ins[-1], *scratch)

    return pl.pallas_call(
        body,
        in_specs=[pl.BlockSpec(memory_space=pltpu.SMEM)] + [vmem] * (2 * count + 2),
        out_specs=[vmem] * count,
        out_shape=[jax.ShapeDtypeStruct((cap, width), jnp.bfloat16)] * count,
        scratch_shapes=[
            pltpu.VMEM((count * cap, width), jnp.bfloat16),
            pltpu.VMEM((count * cap, 2 * half), jnp.bfloat16),
        ],
        compiler_params=pltpu.CompilerParams(vmem_limit_bytes=VMEM_BYTES),
        cost_estimate=pl.CostEstimate(
            flops=1_600_000_000, bytes_accessed=6_000_000, transcendentals=0
        ),
        name="input_products",
    )(place, *own, *other, w_own, w_other)


def attention_kernel(counts, place, q_own, do_own, far, kv0, kv1, kv2, kv3,
                     dq_own, dq_far, out0, out1, out2, out3,
                     kv_s, k_s, kt_s, v_s, q_s, do_s, tri_s, s_s, g_s, so_s, go_s, dq_s, dk_s, dv_s, off_s):
    bf, f32 = jnp.bfloat16, jnp.float32
    cap = q_own.shape[0]
    far_heads = far.shape[1] // (2 * HEAD)
    shards = counts.shape[0]
    side = 4
    scale = HEAD**-0.5
    x_at, y_at, group = place[0], place[1], place[2]
    row = lax.broadcasted_iota(jnp.int32, (cap, HEAD), 0)
    lane = lax.broadcasted_iota(jnp.int32, (cap, HEAD), 1)
    zero = jnp.zeros((cap, HEAD), bf)

    def up16(value):
        return ((value + 15) // 16) * 16

    block = side * cap
    for index, ref in enumerate((kv0, kv1, kv2, kv3)):
        kv_s[index * block : (index + 1) * block, :] = ref[...]
    total = jnp.int32(0)
    for s in range(shards):
        off_s[s] = total
        at = pl.ds(pl.multiple_of(total, 16), cap)
        held = ((y_at - s % side) % side) * side + (x_at - s // side) % side
        pair = kv_s[pl.ds(pl.multiple_of(held * cap, 64), cap), :]
        live = row < counts[s]
        k_s[at, :HEAD] = jnp.where(live, pair[:, :HEAD], zero)
        k_s[at, HEAD:] = jnp.where(live, 0.0, jnp.where(lane == 0, MASKED, 0.0)).astype(bf)
        v_s[at, :] = jnp.where(live, pair[:, HEAD:], zero)
        total = total + up16(counts[s])
    end = pl.ds(pl.multiple_of(total, 16), KT)
    k_s[end, :HEAD] = jnp.zeros((KT, HEAD), bf)
    k_s[end, HEAD:] = jnp.zeros((KT, HEAD), bf)
    v_s[end, :] = jnp.zeros((KT, HEAD), bf)

    def k_at(index):
        return pl.ds(pl.multiple_of(index * KT, KT), KT)

    def prepare(j, carry):
        at = k_at(j)
        kt_s[:, at] = k_s[at, :HEAD].T
        dk_s[at, :] = jnp.zeros((KT, HEAD), f32)
        dv_s[at, :] = jnp.zeros((KT, HEAD), f32)
        return carry

    lax.fori_loop(0, (total + cap + KT - 1) // KT, prepare, 0)
    one_lane = lax.broadcasted_iota(jnp.int32, (QT, HEAD), 1)
    ones = jnp.where(one_lane == 0, 1.0, 0.0).astype(bf)
    slot = lax.broadcasted_iota(jnp.int32, (cap, 2 * HEAD), 0)
    key_slot = lax.broadcasted_iota(jnp.int32, (cap, 2 * HEAD), 1)
    later = jnp.where(key_slot > slot, MASKED, 0.0).astype(bf)
    same = jnp.where(key_slot == slot, 1.0, 0.0).astype(bf)
    key_row = lax.broadcasted_iota(jnp.int32, (KT, QT), 0)

    def one_shard(shard, q_ref, do_ref, q_first, do_first, dq_ref):
        count = counts[shard]
        before = pl.multiple_of(off_s[shard], 16)
        rows = up16(count)
        live = row < count
        for h in range(far_heads):
            at = pl.ds(pl.multiple_of(h * rows, 16), cap)
            q_here = pl.ds(pl.multiple_of(q_first + h * HEAD, HEAD), HEAD)
            do_here = pl.ds(pl.multiple_of(do_first + h * HEAD, HEAD), HEAD)
            q_s[at, :] = jnp.where(live, q_ref[:, q_here], zero)
            do_s[at, :] = jnp.where(live, do_ref[:, do_here], zero)
            tri_s[at, :] = later
        tail = pl.ds(pl.multiple_of(far_heads * rows, 16), QT)
        q_s[tail, :] = jnp.zeros((QT, HEAD), bf)
        do_s[tail, :] = jnp.zeros((QT, HEAD), bf)
        tri_s[tail, :] = jnp.zeros((QT, 2 * HEAD), bf)
        own = pl.ds(before, cap)
        full = before // KT
        rest = before - full * KT
        tiles = (far_heads * rows + QT - 1) // QT

        def query_step(i, carry):
            q_at = pl.ds(pl.multiple_of(i * QT, QT), QT)
            q = q_s[q_at, :]
            do = do_s[q_at, :]
            q_one = jnp.concatenate([q, ones], axis=1)
            own_k = k_s[own, :HEAD]
            scores = lax.dot_general(own_k, q, ROWS_ROWS, preferred_element_type=f32) * (scale * LOG2E)
            scores = scores + lax.dot_general(same, tri_s[q_at, :], ROWS_ROWS, preferred_element_type=f32)
            grads = lax.dot_general(v_s[own, :], do, ROWS_ROWS, preferred_element_type=f32)
            so_s[...] = scores
            go_s[...] = grads
            high = jnp.max(scores, axis=0, keepdims=True)
            e = jnp.exp2(scores - high)
            state = (high, jnp.sum(e, axis=0, keepdims=True), jnp.sum(e * grads, axis=0, keepdims=True))

            def scan(j, state, partial):
                high, total_e, total_w = state
                at = k_at(j)
                scores = lax.dot_general(k_s[at, :], q_one, ROWS_ROWS, preferred_element_type=f32)
                grads = lax.dot_general(v_s[at, :], do, ROWS_ROWS, preferred_element_type=f32)
                scores = scores * (scale * LOG2E)
                if partial:
                    scores = jnp.where(key_row < rest, scores, MASKED)
                s_s[at, :] = scores
                g_s[at, :] = grads
                new = jnp.maximum(high, jnp.max(scores, axis=0, keepdims=True))
                e = jnp.exp2(scores - new)
                shrink = jnp.exp2(high - new)
                return (
                    new,
                    total_e * shrink + jnp.sum(e, axis=0, keepdims=True),
                    total_w * shrink + jnp.sum(e * grads, axis=0, keepdims=True),
                )

            state = lax.fori_loop(0, full, functools.partial(scan, partial=False), state)
            ends = full + (rest > 0).astype(jnp.int32)
            high, total_e, total_w = lax.fori_loop(full, ends, functools.partial(scan, partial=True), state)
            delta = total_w / total_e
            log_total = high + jnp.log2(total_e)

            def spread(at, key_t, scores, grads):
                probs = jnp.exp2(scores - log_total)
                dscore = (probs * (grads - delta)).astype(bf)
                dv_s[at, :] += lax.dot_general(probs.astype(bf), do, ROWS_COLS, preferred_element_type=f32)
                dk_s[at, :] += lax.dot_general(dscore, q, ROWS_COLS, preferred_element_type=f32)
                return lax.dot_general(key_t, dscore, ROWS_COLS, preferred_element_type=f32)

            dq = spread(own, own_k.T, so_s[...], go_s[...])
            dq = lax.fori_loop(
                0, ends, lambda j, dq: dq + spread(k_at(j), kt_s[:, k_at(j)], s_s[k_at(j), :], g_s[k_at(j), :]), dq
            )
            dq_s[q_at, :] = (dq * scale).T.astype(bf)
            return carry

        lax.fori_loop(0, tiles, query_step, 0)
        for h in range(far_heads):
            at = pl.ds(pl.multiple_of(h * rows, 16), cap)
            dq_ref[:, h * HEAD : (h + 1) * HEAD] = jnp.where(live, dq_s[at, :], zero)

    span = far_heads * HEAD
    one_shard(x_at * side + y_at, q_own, do_own, group * span, group * span, dq_own)
    one_shard((side - 1 - x_at) * side + y_at, far, far, 0, span, dq_far)

    for step, ref in enumerate((out0, out1, out2, out3)):
        for x in range(side):
            shard = x * side + (y_at + step) % side
            at = pl.ds(pl.multiple_of(off_s[shard], 16), cap)
            here = slice(x * cap, (x + 1) * cap)
            live = row < counts[shard]
            ref[here, :HEAD] = jnp.where(live, dk_s[at, :] * scale, 0.0).astype(bf)
            ref[here, HEAD:] = jnp.where(live, dv_s[at, :], 0.0).astype(bf)


def attention_backward(counts, place, q_own, do_own, far, kvs):
    cap, width = far.shape[0], far.shape[1] // 2
    shards = counts.shape[0]
    rows = shards * cap
    keys = -(-(rows + KT) // KT) * KT
    queries = -(-(cap * (width // HEAD) + max(QT, cap)) // QT) * QT
    bf, f32 = jnp.bfloat16, jnp.float32
    vmem = pl.BlockSpec(memory_space=pltpu.VMEM)
    smem = pl.BlockSpec(memory_space=pltpu.SMEM)
    block = kvs[0].shape
    return pl.pallas_call(
        attention_kernel,
        out_shape=[jax.ShapeDtypeStruct((cap, width), bf)] * 2 + [jax.ShapeDtypeStruct(block, bf)] * 4,
        in_specs=[smem, smem] + [vmem] * 7,
        out_specs=[vmem] * 6,
        scratch_shapes=[
            pltpu.VMEM((rows, 2 * HEAD), bf),
            pltpu.VMEM((keys, 2 * HEAD), bf),
            pltpu.VMEM((HEAD, keys), bf),
            pltpu.VMEM((keys, HEAD), bf),
            pltpu.VMEM((queries, HEAD), bf),
            pltpu.VMEM((queries, HEAD), bf),
            pltpu.VMEM((queries, 2 * HEAD), bf),
            pltpu.VMEM((keys, QT), f32),
            pltpu.VMEM((keys, QT), f32),
            pltpu.VMEM((cap, QT), f32),
            pltpu.VMEM((cap, QT), f32),
            pltpu.VMEM((queries, HEAD), bf),
            pltpu.VMEM((keys, HEAD), f32),
            pltpu.VMEM((keys, HEAD), f32),
            pltpu.SMEM((shards,), jnp.int32),
        ],
        compiler_params=pltpu.CompilerParams(vmem_limit_bytes=VMEM_BYTES),
        cost_estimate=pl.CostEstimate(flops=6_000_000_000, bytes_accessed=6_000_000, transcendentals=10_000_000),
        name="attention_backward",
    )(counts, place, q_own, do_own, far, *kvs)


def spread_kernel(order, target_ref, *refs):
    parts, out_ref = refs[:-1], refs[-1]
    step = pl.program_id(0)
    tokens, capacity = out_ref.shape[0], parts[0].shape[0]
    token = lax.broadcasted_iota(jnp.int32, (tokens, capacity), 0)
    pick = (token == target_ref[...]).astype(jnp.bfloat16)
    for index, part in enumerate(parts):

        @pl.when(step == index)
        def _(part=part):
            out_ref[...] = lax.dot_general(
                pick, part[...], ROWS_COLS, preferred_element_type=jnp.float32
            ).astype(jnp.bfloat16)


def spread_rows(order, target, parts, tokens):
    capacity, width = parts[0].shape
    whole = pl.BlockSpec((capacity, width), lambda s, order: (0, 0))
    return pl.pallas_call(
        spread_kernel,
        grid_spec=pltpu.PrefetchScalarGridSpec(
            num_scalar_prefetch=1,
            grid=(len(parts),),
            in_specs=[pl.BlockSpec((1, capacity), lambda s, order: (0, 0))] + [whole] * len(parts),
            out_specs=pl.BlockSpec((tokens, width), lambda s, order: (0, order[s])),
        ),
        out_shape=jax.ShapeDtypeStruct((tokens, width * len(parts)), jnp.bfloat16),
        cost_estimate=pl.CostEstimate(
            flops=800_000_000, bytes_accessed=6_000_000, transcendentals=0
        ),
        name="spread_rows",
    )(order, target[None, :], *parts)


def shards(hidden, kept, counts, queries, keys, values, out_grad, kv_weight):
    f32 = jnp.float32
    seq_devices = lax.axis_size("seq")
    dp_devices = lax.axis_size("dp")
    rep_devices = lax.axis_size("rep")
    seq_index = lax.axis_index("seq")
    dp_index = lax.axis_index("dp")
    rep_index = lax.axis_index("rep")
    capacity = queries.shape[1]
    tokens_local = hidden.shape[1]
    local_groups = keys.shape[2] // HEAD
    group_columns = queries.shape[2] // local_groups
    width = kv_weight.shape[2]
    part_rows = kv_weight.shape[0] // rep_devices
    dp_per_rep = dp_devices // rep_devices
    lane_of = (dp_index % dp_per_rep) * rep_devices + rep_index
    x_at, y_at = seq_index // SIDE, seq_index % SIDE
    group = x_at // (SIDE // local_groups)
    place = jnp.stack([x_at, y_at, group, dp_index, rep_index, lane_of]).astype(jnp.int32)
    swap = [(i, (i + 1) % rep_devices) for i in range(rep_devices)]
    mirror = [(i, (SIDE - 1 - i // SIDE) * SIDE + i % SIDE) for i in range(seq_devices)]

    def shift_dp(array, step):
        return lax.ppermute(array, "dp", [(i, (i + step) % dp_devices) for i in range(dp_devices)])

    def shift_x(array, step):
        pairs = [(i, ((i // SIDE + step) % SIDE) * SIDE + i % SIDE) for i in range(seq_devices)]
        return lax.ppermute(array, "seq", pairs)

    def shift_y(array, step):
        pairs = [(i, (i // SIDE) * SIDE + (i % SIDE + step) % SIDE) for i in range(seq_devices)]
        return lax.ppermute(array, "seq", pairs)

    by_group = [
        jnp.concatenate([keys[0][:, g * HEAD : (g + 1) * HEAD], values[0][:, g * HEAD : (g + 1) * HEAD]], axis=1)
        for g in range(local_groups)
    ]

    def pair_for(step):
        wanted = ((x_at + step) % SIDE) // (SIDE // local_groups)
        chosen = by_group[0]
        for g in range(1, local_groups):
            chosen = jnp.where(wanted == g, by_group[g], chosen)
        return chosen

    kv_x = [pair_for(0)] + [shift_x(pair_for(step), step) for step in range(1, SIDE)]
    kv_x = jnp.concatenate(kv_x, axis=0)
    sent = (1 - group) * group_columns
    far = jnp.concatenate(
        [lax.dynamic_slice_in_dim(array[0], sent, group_columns, 1) for array in (queries, out_grad)], axis=1
    )
    halves = kv_weight.reshape(rep_devices, part_rows, 2 * width)
    kept_half = lax.dynamic_index_in_dim(halves, rep_index, 0, keepdims=False)
    sent_half = lax.dynamic_index_in_dim(halves, 1 - rep_index, 0, keepdims=False)
    kv_x, far, hidden, kept_half, sent_half = lax.optimization_barrier(
        (kv_x, far, hidden, kept_half, sent_half)
    )
    kv_y = [kv_x] + [shift_y(kv_x, step) for step in range(1, SIDE)]

    far = lax.ppermute(far, "seq", mirror)

    own_rows = lax.dynamic_index_in_dim(kept[0], seq_index, 0, keepdims=False)
    own_count = lax.dynamic_index_in_dim(counts[0], seq_index, 0, keepdims=False)
    columns = gather_columns(place, own_rows, hidden[0], dp_devices, rep_devices)
    other_half = lax.ppermute(sent_half, "rep", swap)
    slot_index = jnp.arange(capacity, dtype=jnp.int32)
    target = jnp.where(slot_index < own_count, own_rows, tokens_local)
    kv_y[1:], columns, kept_half, other_half, target = lax.optimization_barrier(
        (kv_y[1:], columns, kept_half, other_half, target)
    )
    columns = lax.all_to_all(columns, "dp", split_axis=0, concat_axis=0, tiled=True)

    grads = attention_backward(counts[0], place, queries[0], out_grad[0], far, kv_y)
    (dq_own, dq_far, *kv_back), columns = lax.optimization_barrier((tuple(grads), columns))
    kv_back = [kv_back[0]] + [shift_y(kv_back[step], step) for step in range(1, SIDE)]
    dq_back = lax.ppermute(dq_far, "seq", mirror)
    columns_far = lax.ppermute(columns, "rep", swap)
    kv_back[-1], columns_far = lax.optimization_barrier((kv_back[-1], columns_far))

    pieces = y_sum(place, kv_back)
    pieces = [pieces[0]] + [shift_x(pieces[step], step) for step in range(1, SIDE)]
    pieces, dq_back = lax.optimization_barrier((pieces, dq_back))
    kv_grad = x_sum(place, pieces, local_groups)
    dq_first = jnp.where(group == 0, dq_own, dq_back)
    dq_last = jnp.where(group == 0, dq_back, dq_own)
    back_query = jnp.concatenate([dq_first, dq_last], axis=1)

    kv_all = [kv_grad] + [shift_dp(kv_grad, step) for step in range(1, dp_devices)]
    kv_far = [lax.ppermute(part, "rep", swap) for part in kv_all]
    kv_all, kv_far[:-1], back_query = lax.optimization_barrier((kv_all, kv_far[:-1], back_query))

    terms = weight_terms(place, columns, columns_far, kv_all)
    terms = lax.all_to_all(
        terms.reshape(seq_devices, -1, 2 * width), "seq", split_axis=0, concat_axis=0, tiled=True
    )
    grad_weight = jnp.sum(terms.astype(f32), axis=0).reshape(-1, 2, width)

    products = input_products(place, kv_all, kv_far, kept_half, other_half)
    received = []
    for step in range(dp_devices):
        pairs = []
        for dp in range(dp_devices):
            for rep in range(rep_devices):
                lane = (dp % dp_per_rep) * rep_devices + rep
                to_dp = (lane + step) % dp_devices
                pairs.append((dp * rep_devices + rep, to_dp * rep_devices + dp // dp_per_rep))
        received.append(lax.ppermute(products[step], ("dp", "rep"), pairs))
    order = jnp.stack([(dp_index - step) % dp_devices for step in range(dp_devices)]).astype(jnp.int32)
    grad_hidden = spread_rows(order, target, received, tokens_local)
    return (back_query[None], grad_hidden[None], grad_weight)


def solution(mesh):
    placed = (
        P("dp", "seq", None),
        P("dp", None, None),
        P("dp", None),
        P("dp", "seq", "rep"),
        P("dp", "seq", "rep"),
        P("dp", "seq", "rep"),
        P("dp", "seq", "rep"),
        P("dp", None, "rep"),
    )
    return jax.shard_map(
        shards,
        mesh=mesh,
        in_specs=placed,
        out_specs=(P("dp", "seq", "rep"), P("dp", "seq", "rep"), P(("seq", "dp"), None, "rep")),
        check_vma=False,
    )
```

profile of v0, /device:TPU:1, one launch (start us, length us, event | category | flops | bytes accessed | tf_op | source)
XLA Modules:
  0.0 169.9 jit_solution(5930267807653533825)
XLA Ops:
  2.4 2.0 %collective-permute-start = (bf16[192,256]{1,0:T(8,128)(2,1)}, bf16[192,256]{1,0:T(8,128)(2,1)S(1)}, u32[]{:S(2)}, u32[]{:S(2)}) collective-permute-start(bf16[192,256]{1,0:T(8,128)(2,1)} %get-tuple-element.104), channel_id=1, source_target_pairs={{0,32},{8,40},{16,48},{24,56},{32,64},{40,72},{48,80},{56,88},{64,... | collective-permute-start | bytes 294920 | tf_op jit(solution)/shard_map/ppermute | solution.py:473
  4.5 2.5 %collective-permute-start.1 = (bf16[192,256]{1,0:T(8,128)(2,1)}, bf16[192,256]{1,0:T(8,128)(2,1)S(1)}, u32[]{:S(2)}, u32[]{:S(2)}) collective-permute-start(bf16[192,256]{1,0:T(8,128)(2,1)} %get-tuple-element.105), channel_id=1, source_target_pairs={{0,64},{8,72},{16,80},{24,88},{32,96},{40,104},{48,112},{56,120},{... | collective-permute-start | bytes 294920 | tf_op jit(solution)/shard_map/ppermute | solution.py:473
  7.6 1.2 collective-permute-start.2
  8.7 3.2 %reshape.22 = bf16[2,1024,512]{2,1,0:T(8,128)(2,1)S(1)} reshape(bf16[2048,2,256]{2,1,0:T(2,128)(2,1)} %param.15) | data formatting | bytes 4194304 | tf_op jit(solution)/shard_map/reshape | solution.py:497
  12.0 1.1 dynamic-slice_bitcast_fusion.2
  13.0 0.9 pad_maximum_fusion
  14.0 1.1 dynamic-slice_bitcast_fusion
  15.2 1.6 collective-permute-start.7
  16.8 1.2 constant_dynamic-slice_fusion
  18.0 1.4 collective-permute-start.4
  19.4 2.6 %collective-permute-start.5 = (bf16[768,256]{1,0:T(8,128)(2,1)S(1)}, bf16[768,256]{1,0:T(8,128)(2,1)S(1)}, u32[]{:S(2)}, u32[]{:S(2)}) collective-permute-start(bf16[768,256]{1,0:T(8,128)(2,1)S(1)} %pad_maximum_fusion.2.kv0), channel_id=1, source_target_pairs={{0,16},{8,24},{16,0},{24,8},{32,48},{40,56},{48,32},{56,40},{64,80... | collective-permute-start | bytes 1179656 | tf_op jit(solution)/shard_map/ppermute | solution.py:477
  22.0 1.1 collective-permute-start.6
  23.1 1.2 compare_select_fusion
  25.7 5.6 %gather_columns.1 = bf16[4,192,1024]{2,1,0:T(8,128)(2,1)} custom-call(s32[6]{0:T(128)} %stack.42.place, s32[192,1]{1,0:T(8,128)} %copy.11.rows_ref, bf16[512,8192]{1,0:T(8,128)(2,1)} %bitcast.33), custom_call_target="tpu_custom_call" | custom-call | flops 800000000 | bytes 6000000 | tf_op jit(solution)/shard_map/gather_columns/pallas_call | solution.py:45
  31.3 8.4 %collective-permute-done.5.kv2 = bf16[768,256]{1,0:T(8,128)(2,1)S(1)} collective-permute-done((bf16[768,256]{1,0:T(8,128)(2,1)S(1)}, bf16[768,256]{1,0:T(8,128)(2,1)S(1)}, u32[]{:S(2)}, u32[]{:S(2)}) %collective-permute-start.5) | collective-permute-done | bytes 393248 | tf_op jit(solution)/shard_map/ppermute | solution.py:477
  40.4 5.0 %all-to-all-start = ((bf16[4,192,1024]{2,1,0:T(8,128)(2,1)}), bf16[4,192,1024]{2,1,0:T(8,128)(2,1)S(1)}, u32[]{:S(2)}, u32[]{:S(2)}) async-start(bf16[4,192,1024]{2,1,0:T(8,128)(2,1)} %gather_columns.1), calls=%async_computation | async-start | bytes 3145728 | tf_op jit(solution)/shard_map/all_to_all | solution.py:516
  45.4 22.9 %attention_backward.1 = (bf16[192,1024]{1,0:T(8,128)(2,1)}, bf16[192,1024]{1,0:T(8,128)(2,1)}, bf16[768,256]{1,0:T(8,128)(2,1)}, bf16[768,256]{1,0:T(8,128)(2,1)...) custom-call(s32[16]{0:T(128)} %bitcast.42, s32[6]{0:T(128)} %stack.42.place, bf16[192,2048]{1,0:T(8,128)(2,1)} %bitcast.36, ...), custom_call_target="tpu_custom_call" | custom-call | flops 6000000000 | bytes 6000000 | tf_op jit(solution)/shard_map/attention_backward/pallas_call | solution.py:384
  68.3 1.2 collective-permute-start.11
  69.6 1.5 collective-permute-start.8
  71.0 5.8 %collective-permute-start.9 = (bf16[768,256]{1,0:T(8,128)(2,1)}, bf16[768,256]{1,0:T(8,128)(2,1)}, u32[]{:S(2)}, u32[]{:S(2)}) collective-permute-start(bf16[768,256]{1,0:T(8,128)(2,1)} %get-tuple-element.68), channel_id=1, source_target_pairs={{0,16},{8,24},{16,0},{24,8},{32,48},{40,56},{48,32},{56,40},{64,80... | collective-permute-start | bytes 1179656 | tf_op jit(solution)/shard_map/ppermute | solution.py:477
  76.8 3.6 %collective-permute-done.10.refs_3_ = bf16[768,256]{1,0:T(8,128)(2,1)S(1)} collective-permute-done((bf16[768,256]{1,0:T(8,128)(2,1)}, bf16[768,256]{1,0:T(8,128)(2,1)S(1)}, u32[]{:S(2)}, u32[]{:S(2)}) %collective-permute-start.10) | collective-permute-done | bytes 393248 | tf_op jit(solution)/shard_map/ppermute | solution.py:477
  81.2 3.9 %collective-permute-done.8.refs_1_ = bf16[768,256]{1,0:T(8,128)(2,1)S(1)} collective-permute-done((bf16[768,256]{1,0:T(8,128)(2,1)}, bf16[768,256]{1,0:T(8,128)(2,1)S(1)}, u32[]{:S(2)}, u32[]{:S(2)}) %collective-permute-start.8) | collective-permute-done | bytes 393248 | tf_op jit(solution)/shard_map/ppermute | solution.py:477
  85.9 8.5 %collective-permute-done.9.refs_2_ = bf16[768,256]{1,0:T(8,128)(2,1)} collective-permute-done((bf16[768,256]{1,0:T(8,128)(2,1)}, bf16[768,256]{1,0:T(8,128)(2,1)}, u32[]{:S(2)}, u32[]{:S(2)}) %collective-permute-start.9) | collective-permute-done | bytes 393248 | tf_op jit(solution)/shard_map/ppermute | solution.py:477
  94.4 2.2 %y_sum.1 = (bf16[192,256]{1,0:T(8,128)(2,1)}, bf16[192,256]{1,0:T(8,128)(2,1)}, bf16[192,256]{1,0:T(8,128)(2,1)}, bf16[192,256]{1,0:T(8,128)(2,1)}) custom-call(s32[6]{0:T(128)} %stack.42.place, bf16[768,256]{1,0:T(8,128)(2,1)} %get-tuple-element.66.refs_0_, bf16[768,256]{1,0:T(8,128)(2,1)} %copy-done.9, bf16[768,256]{1,0:T(8,128)(2,1)} %collective-permute-done.9.refs_2_, ...), custom_call_target="tpu_custom_call" | custom-call | flops 1000000 | bytes 2000000 | tf_op jit(solution)/shard_map/y_sum/pallas_call | solution.py:79
  96.7 1.8 %collective-permute-start.12 = (bf16[192,256]{1,0:T(8,128)(2,1)}, bf16[192,256]{1,0:T(8,128)(2,1)}, u32[]{:S(2)}, u32[]{:S(2)}) collective-permute-start(bf16[192,256]{1,0:T(8,128)(2,1)} %get-tuple-element.73), channel_id=1, source_target_pairs={{0,32},{8,40},{16,48},{24,56},{32,64},{40,72},{48,80},{56,88},{64,... | collective-permute-start | bytes 294920 | tf_op jit(solution)/shard_map/ppermute | solution.py:473
  98.5 2.4 %collective-permute-start.14 = (bf16[192,256]{1,0:T(8,128)(2,1)}, bf16[192,256]{1,0:T(8,128)(2,1)}, u32[]{:S(2)}, u32[]{:S(2)}) collective-permute-start(bf16[192,256]{1,0:T(8,128)(2,1)} %get-tuple-element.75), channel_id=1, source_target_pairs={{0,96},{8,104},{16,112},{24,120},{32,0},{40,8},{48,16},{56,24},{64... | collective-permute-start | bytes 294920 | tf_op jit(solution)/shard_map/ppermute | solution.py:473
  101.7 2.2 %collective-permute-done.13.refs_2_ = bf16[192,256]{1,0:T(8,128)(2,1)} collective-permute-done((bf16[192,256]{1,0:T(8,128)(2,1)}, bf16[192,256]{1,0:T(8,128)(2,1)}, u32[]{:S(2)}, u32[]{:S(2)}) %collective-permute-start.13) | collective-permute-done | bytes 98336 | tf_op jit(solution)/shard_map/ppermute | solution.py:473
  103.9 1.8 %x_sum.1.refs_0_ = bf16[192,512]{1,0:T(8,128)(2,1)} custom-call(s32[6]{0:T(128)} %stack.42.place, bf16[192,256]{1,0:T(8,128)(2,1)} %get-tuple-element.77.refs_0_, bf16[192,256]{1,0:T(8,128)(2,1)} %collective-permute-done.12.refs_1_, bf16[192,256]{1,0:T(8,128)(2,1)} %collective-permute-done.13.refs_2_, bf16[192,256]{1,0:T(8,128)(2,1)} %collective-permute-done.14.refs_3_), custom_call_target="tpu_custom_call" | custom-call | flops 1000000 | bytes 1000000 | tf_op jit(solution)/shard_map/x_sum/pallas_call | solution.py:113
  105.7 1.6 collective-permute-start.16
  107.3 1.6 collective-permute-start.17
  108.9 2.0 %collective-permute-start.18 = (bf16[192,512]{1,0:T(8,128)(2,1)}, bf16[192,512]{1,0:T(8,128)(2,1)S(1)}, u32[]{:S(2)}, u32[]{:S(2)}) collective-permute-start(bf16[192,512]{1,0:T(8,128)(2,1)} %x_sum.1.refs_0_), channel_id=1, source_target_pairs={{0,6},{2,0},{4,2},{6,4},{1,7},{3,1},{5,3},{7,5},{8,14},{10,8},{12,... | collective-permute-start | bytes 589832 | tf_op jit(solution)/shard_map/ppermute | solution.py:469
  110.9 2.5 %collective-permute-start.19 = (bf16[192,512]{1,0:T(8,128)(2,1)}, bf16[192,512]{1,0:T(8,128)(2,1)S(1)}, u32[]{:S(2)}, u32[]{:S(2)}) collective-permute-start(bf16[192,512]{1,0:T(8,128)(2,1)} %x_sum.1.refs_0_), channel_id=1, source_target_pairs={{0,1},{1,0},{2,3},{3,2},{4,5},{5,4},{6,7},{7,6},{8,9},{9,8},{10,11... | collective-permute-start | bytes 589832 | tf_op jit(solution)/shard_map/ppermute | solution.py:534
  113.4 1.1 broadcast_select_fusion.1
  114.5 2.6 %collective-permute-start.20 = (bf16[192,512]{1,0:T(8,128)(2,1)S(1)}, bf16[192,512]{1,0:T(8,128)(2,1)S(1)}, u32[]{:S(2)}, u32[]{:S(2)}) collective-permute-start(bf16[192,512]{1,0:T(8,128)(2,1)S(1)} %collective-permute-done.16.refs_1_), channel_id=1, source_target_pairs={{0,1},{1,0},{2,3},{3,2},{4,5},{5,4},{6,7},{7,6},{8,9},{9,8},{10,11... | collective-permute-start | bytes 589832 | tf_op jit(solution)/shard_map/ppermute | solution.py:534
  117.0 2.1 %collective-permute-start.21 = (bf16[192,512]{1,0:T(8,128)(2,1)S(1)}, bf16[192,512]{1,0:T(8,128)(2,1)S(1)}, u32[]{:S(2)}, u32[]{:S(2)}) collective-permute-start(bf16[192,512]{1,0:T(8,128)(2,1)S(1)} %collective-permute-done.17.refs_2_), channel_id=1, source_target_pairs={{0,1},{1,0},{2,3},{3,2},{4,5},{5,4},{6,7},{7,6},{8,9},{9,8},{10,11... | collective-permute-start | bytes 589832 | tf_op jit(solution)/shard_map/ppermute | solution.py:534
  119.1 0.9 pad_maximum_fusion.1
  120.8 6.1 %weight_terms.1 = bf16[2048,512]{1,0:T(8,128)(2,1)} custom-call(s32[6]{0:T(128)} %stack.42.place, bf16[4,192,1024]{2,1,0:T(8,128)(2,1)} %copy-done.1, bf16[4,192,1024]{2,1,0:T(8,128)(2,1)} %copy-done.2, bf16[192,512]{1,0:T(8,128)(2,1)} %x_sum.1.refs_0_, bf16[192,512]{1,0:T(8,128)(2,1)} %copy-done.10, bf16[192,512]{1,0:T(8,128)(2,1)} %copy-done.11, ...), custom_call_target="tpu_custom_call" | custom-call | flops 1600000000 | bytes 6000000 | tf_op jit(solution)/shard_map/weight_terms/pallas_call | solution.py:155
  126.9 5.2 %all-to-all-start.1 = ((bf16[16,128,512]{2,1,0:T(8,128)(2,1)}), bf16[16,128,512]{2,1,0:T(8,128)(2,1)S(1)}, u32[]{:S(2)}, u32[]{:S(2)}) async-start(bf16[16,128,512]{2,1,0:T(8,128)(2,1)} %bitcast.32), calls=%async_computation.1 | async-start | bytes 4194304 | tf_op jit(solution)/shard_map/all_to_all | solution.py:538
  132.7 1.1 collective-permute-done.22.refs_7_
  134.5 5.1 %input_products.1 = (bf16[192,1024]{1,0:T(8,128)(2,1)}, bf16[192,1024]{1,0:T(8,128)(2,1)}, bf16[192,1024]{1,0:T(8,128)(2,1)}, bf16[192,1024]{1,0:T(8,128)(2,1)}) custom-call(s32[6]{0:T(128)} %stack.42.place, bf16[192,512]{1,0:T(8,128)(2,1)} %x_sum.1.refs_0_, bf16[192,512]{1,0:T(8,128)(2,1)} %copy-done.10, bf16[192,512]{1,0:T(8,128)(2,1)} %copy-done.11, ...), custom_call_target="tpu_custom_call" | custom-call | flops 1600000000 | bytes 6000000 | tf_op jit(solution)/shard_map/input_products/pallas_call | solution.py:208
  139.6 2.2 %collective-permute-start.23 = (bf16[192,1024]{1,0:T(8,128)(2,1)}, bf16[192,1024]{1,0:T(8,128)(2,1)S(1)}, u32[]{:S(2)}, u32[]{:S(2)}) collective-permute-start(bf16[192,1024]{1,0:T(8,128)(2,1)} %get-tuple-element.94), channel_id=1, source_target_pairs={{0,0},{1,2},{2,4},{3,6},{4,1},{5,3},{6,5},{7,7},{8,8},{9,10},{10,1... | collective-permute-start | bytes 1179656 | tf_op jit(solution)/shard_map/ppermute | solution.py:552
  141.8 4.8 %collective-permute-start.24 = (bf16[192,1024]{1,0:T(8,128)(2,1)}, bf16[192,1024]{1,0:T(8,128)(2,1)S(1)}, u32[]{:S(2)}, u32[]{:S(2)}) collective-permute-start(bf16[192,1024]{1,0:T(8,128)(2,1)} %get-tuple-element.95), channel_id=1, source_target_pairs={{0,2},{1,4},{2,6},{3,0},{4,3},{5,5},{6,7},{7,1},{8,10},{9,12},{10,... | collective-permute-start | bytes 1179656 | tf_op jit(solution)/shard_map/ppermute | solution.py:552
  146.8 3.4 %collective-permute-start.26 = (bf16[192,1024]{1,0:T(8,128)(2,1)}, bf16[192,1024]{1,0:T(8,128)(2,1)}, u32[]{:S(2)}, u32[]{:S(2)}) collective-permute-start(bf16[192,1024]{1,0:T(8,128)(2,1)} %get-tuple-element.97), channel_id=1, source_target_pairs={{0,6},{1,0},{2,2},{3,4},{4,7},{5,1},{6,3},{7,5},{8,14},{9,8},{10,1... | collective-permute-start | bytes 1179656 | tf_op jit(solution)/shard_map/ppermute | solution.py:552
  150.8 1.4 collective-permute-done.23.refs_0_
  152.2 7.2 %collective-permute-done.24.refs_1_ = bf16[192,1024]{1,0:T(8,128)(2,1)S(1)} collective-permute-done((bf16[192,1024]{1,0:T(8,128)(2,1)}, bf16[192,1024]{1,0:T(8,128)(2,1)S(1)}, u32[]{:S(2)}, u32[]{:S(2)}) %collective-permute-start.24) | collective-permute-done | bytes 393248 | tf_op jit(solution)/shard_map/ppermute | solution.py:552
  159.4 2.2 %collective-permute-done.25.refs_2_ = bf16[192,1024]{1,0:T(8,128)(2,1)S(1)} collective-permute-done((bf16[192,1024]{1,0:T(8,128)(2,1)}, bf16[192,1024]{1,0:T(8,128)(2,1)S(1)}, u32[]{:S(2)}, u32[]{:S(2)}) %collective-permute-start.25) | collective-permute-done | bytes 393248 | tf_op jit(solution)/shard_map/ppermute | solution.py:552
  161.7 1.5 collective-permute-done.26.refs_3_
  163.2 5.6 %spread_rows.1 = bf16[512,4096]{1,0:T(8,128)(2,1)} custom-call(s32[4]{0:T(128)} %pad_add_fusion.order, s32[1,192]{1,0:T(1,128)} %bitcast.40, bf16[192,1024]{1,0:T(8,128)(2,1)} %copy-done.3, bf16[192,1024]{1,0:T(8,128)(2,1)} %copy-done.4, bf16[192,1024]{1,0:T(8,128)(2,1)} %copy-done.5, bf16[192,1024]{1,0:T(8,128)(2,1)} %collective-permute-done.26.refs_3_), custom_call_target="tpu_custom_call" | custom-call | flops 800000000 | bytes 6000000 | tf_op jit(solution)/shard_map/spread_rows/pallas_call | solution.py:430
  (80 shorter events, 10.6 us)
Async XLA Ops:
  0.6 17.4 %copy-start = (s32[1,16,192]{2,1,0:T(8,128)S(1)}, s32[1,16,192]{2,1,0:T(8,128)}, u32[]{:S(2)}) copy-start(s32[1,16,192]{2,1,0:T(8,128)} %param.9) | copy-start | bytes 36868
  2.4 12.7 %collective-permute-start = (bf16[192,256]{1,0:T(8,128)(2,1)}, bf16[192,256]{1,0:T(8,128)(2,1)S(1)}, u32[]{:S(2)}, u32[]{:S(2)}) collective-permute-start(bf16[192,256]{1,0:T(8,128)(2,1)} %get-tuple-element.104), channel_id=1, source_target_pairs={{0,32},{8,40},{16,48},{24,56},{32,64},{40,72},{48,80},{56,88},{64,... | collective-permute-start | bytes 294920 | tf_op jit(solution)/shard_map/ppermute | solution.py:473
  4.5 10.7 %collective-permute-start.1 = (bf16[192,256]{1,0:T(8,128)(2,1)}, bf16[192,256]{1,0:T(8,128)(2,1)S(1)}, u32[]{:S(2)}, u32[]{:S(2)}) collective-permute-start(bf16[192,256]{1,0:T(8,128)(2,1)} %get-tuple-element.105), channel_id=1, source_target_pairs={{0,64},{8,72},{16,80},{24,88},{32,96},{40,104},{48,112},{56,120},{... | collective-permute-start | bytes 294920 | tf_op jit(solution)/shard_map/ppermute | solution.py:473
  7.6 7.6 %collective-permute-start.2 = (bf16[192,256]{1,0:T(8,128)(2,1)}, bf16[192,256]{1,0:T(8,128)(2,1)S(1)}, u32[]{:S(2)}, u32[]{:S(2)}) collective-permute-start(bf16[192,256]{1,0:T(8,128)(2,1)} %broadcast_select_fusion.2), channel_id=1, source_target_pairs={{0,96},{8,104},{16,112},{24,120},{32,0},{40,8},{48,16},{56,24},{64... | collective-permute-start | bytes 294920 | tf_op jit(solution)/shard_map/ppermute | solution.py:473
  8.7 3.2 %copy-start.14 = (bf16[1,192,2048]{2,1,0:T(8,128)(2,1)S(1)}, bf16[1,192,2048]{2,1,0:T(8,128)(2,1)}, u32[]{:S(2)}) copy-start(bf16[1,192,2048]{2,1,0:T(8,128)(2,1)} %param.11) | copy-start | bytes 2359300
  15.2 16.1 %copy-start.6 = (bf16[768,256]{1,0:T(8,128)(2,1)}, bf16[768,256]{1,0:T(8,128)(2,1)S(1)}, u32[]{:S(2)}) copy-start(bf16[768,256]{1,0:T(8,128)(2,1)S(1)} %pad_maximum_fusion.2.kv0) | copy-start | bytes 1179652
  15.2 24.5 %collective-permute-start.7 = (bf16[1024,512]{1,0:T(8,128)(2,1)S(1)}, bf16[1024,512]{1,0:T(8,128)(2,1)S(1)}, u32[]{:S(2)}, u32[]{:S(2)}) collective-permute-start(bf16[1024,512]{1,0:T(8,128)(2,1)S(1)} %get-tuple-element.55), channel_id=1, source_target_pairs={{0,1},{1,0},{2,3},{3,2},{4,5},{5,4},{6,7},{7,6},{8,9},{9,8},{10,11... | collective-permute-start | bytes 3145736 | tf_op jit(solution)/shard_map/ppermute | solution.py:510
  18.0 13.3 %collective-permute-start.4 = (bf16[768,256]{1,0:T(8,128)(2,1)S(1)}, bf16[768,256]{1,0:T(8,128)(2,1)S(1)}, u32[]{:S(2)}, u32[]{:S(2)}) collective-permute-start(bf16[768,256]{1,0:T(8,128)(2,1)S(1)} %pad_maximum_fusion.2.kv0), channel_id=1, source_target_pairs={{0,8},{8,16},{16,24},{24,0},{32,40},{40,48},{48,56},{56,32},{64,72... | collective-permute-start | bytes 1179656 | tf_op jit(solution)/shard_map/ppermute | solution.py:477
  19.4 20.3 %collective-permute-start.5 = (bf16[768,256]{1,0:T(8,128)(2,1)S(1)}, bf16[768,256]{1,0:T(8,128)(2,1)S(1)}, u32[]{:S(2)}, u32[]{:S(2)}) collective-permute-start(bf16[768,256]{1,0:T(8,128)(2,1)S(1)} %pad_maximum_fusion.2.kv0), channel_id=1, source_target_pairs={{0,16},{8,24},{16,0},{24,8},{32,48},{40,56},{48,32},{56,40},{64,80... | collective-permute-start | bytes 1179656 | tf_op jit(solution)/shard_map/ppermute | solution.py:477
  22.0 17.6 %collective-permute-start.6 = (bf16[768,256]{1,0:T(8,128)(2,1)S(1)}, bf16[768,256]{1,0:T(8,128)(2,1)}, u32[]{:S(2)}, u32[]{:S(2)}) collective-permute-start(bf16[768,256]{1,0:T(8,128)(2,1)S(1)} %pad_maximum_fusion.2.kv0), channel_id=1, source_target_pairs={{0,24},{8,0},{16,8},{24,16},{32,56},{40,32},{48,40},{56,48},{64,88... | collective-permute-start | bytes 1179656 | tf_op jit(solution)/shard_map/ppermute | solution.py:477
  24.3 21.1 %collective-permute-start.3 = (bf16[192,2048]{1,0:T(8,128)(2,1)}, bf16[192,2048]{1,0:T(8,128)(2,1)}, u32[]{:S(2)}, u32[]{:S(2)}) collective-permute-start(bf16[192,2048]{1,0:T(8,128)(2,1)} %pad_maximum_fusion), channel_id=1, source_target_pairs={{0,96},{8,104},{16,112},{24,120},{32,64},{40,72},{48,80},{56,88},{... | collective-permute-start | bytes 2359304 | tf_op jit(solution)/shard_map/ppermute | solution.py:505
  31.3 14.1 %copy-start.16 = (bf16[768,256]{1,0:T(8,128)(2,1)}, bf16[768,256]{1,0:T(8,128)(2,1)S(1)}, u32[]{:S(2)}) copy-start(bf16[768,256]{1,0:T(8,128)(2,1)S(1)} %collective-permute-done.4.kv1) | copy-start | bytes 1179652
  39.7 28.6 %copy-start.15 = (bf16[1024,512]{1,0:T(8,128)(2,1)}, bf16[1024,512]{1,0:T(8,128)(2,1)S(1)}, u32[]{:S(2)}) copy-start(bf16[1024,512]{1,0:T(8,128)(2,1)S(1)} %collective-permute-done.7.refs_9_) | copy-start | bytes 3145732
  40.4 27.9 %all-to-all-start = ((bf16[4,192,1024]{2,1,0:T(8,128)(2,1)}), bf16[4,192,1024]{2,1,0:T(8,128)(2,1)S(1)}, u32[]{:S(2)}, u32[]{:S(2)}) async-start(bf16[4,192,1024]{2,1,0:T(8,128)(2,1)} %gather_columns.1), calls=%async_computation | async-start | bytes 3145728 | tf_op jit(solution)/shard_map/all_to_all | solution.py:516
  68.3 45.1 %copy-start.7 = (bf16[192,1024]{1,0:T(8,128)(2,1)S(1)}, bf16[192,1024]{1,0:T(8,128)(2,1)}, u32[]{:S(2)}) copy-start(bf16[192,1024]{1,0:T(8,128)(2,1)} %get-tuple-element.81) | copy-start | bytes 1179652
  68.3 51.8 %copy-start.1 = (bf16[4,192,1024]{2,1,0:T(8,128)(2,1)}, bf16[4,192,1024]{2,1,0:T(8,128)(2,1)S(1)}, u32[]{:S(2)}) copy-start(bf16[4,192,1024]{2,1,0:T(8,128)(2,1)S(1)} %all-to-all-done.own_ref) | copy-start | bytes 4718596
  68.3 12.1 %collective-permute-start.11 = (bf16[4,192,1024]{2,1,0:T(8,128)(2,1)S(1)}, bf16[4,192,1024]{2,1,0:T(8,128)(2,1)S(1)}, u32[]{:S(2)}, u32[]{:S(2)}) collective-permute-start(bf16[4,192,1024]{2,1,0:T(8,128)(2,1)S(1)} %all-to-all-done.own_ref), channel_id=1, source_target_pairs={{0,1},{1,0},{2,3},{3,2},{4,5},{5,4},{6,7},{7,6},{8,9},{9,8},{10,11... | collective-permute-start | bytes 4718600 | tf_op jit(solution)/shard_map/ppermute | solution.py:522
  69.6 10.9 %collective-permute-start.10 = (bf16[768,256]{1,0:T(8,128)(2,1)}, bf16[768,256]{1,0:T(8,128)(2,1)S(1)}, u32[]{:S(2)}, u32[]{:S(2)}) collective-permute-start(bf16[768,256]{1,0:T(8,128)(2,1)} %get-tuple-element.69), channel_id=1, source_target_pairs={{0,24},{8,0},{16,8},{24,16},{32,56},{40,32},{48,40},{56,48},{64,88... | collective-permute-start | bytes 1179656 | tf_op jit(solution)/shard_map/ppermute | solution.py:477
  69.6 15.6 %collective-permute-start.8 = (bf16[768,256]{1,0:T(8,128)(2,1)}, bf16[768,256]{1,0:T(8,128)(2,1)S(1)}, u32[]{:S(2)}, u32[]{:S(2)}) collective-permute-start(bf16[768,256]{1,0:T(8,128)(2,1)} %get-tuple-element.67), channel_id=1, source_target_pairs={{0,8},{8,16},{16,24},{24,0},{32,40},{40,48},{48,56},{56,32},{64,72... | collective-permute-start | bytes 1179656 | tf_op jit(solution)/shard_map/ppermute | solution.py:477
  71.0 23.4 %collective-permute-start.9 = (bf16[768,256]{1,0:T(8,128)(2,1)}, bf16[768,256]{1,0:T(8,128)(2,1)}, u32[]{:S(2)}, u32[]{:S(2)}) collective-permute-start(bf16[768,256]{1,0:T(8,128)(2,1)} %get-tuple-element.68), channel_id=1, source_target_pairs={{0,16},{8,24},{16,0},{24,8},{32,48},{40,56},{48,32},{56,40},{64,80... | collective-permute-start | bytes 1179656 | tf_op jit(solution)/shard_map/ppermute | solution.py:477
  76.8 24.1 %collective-permute-start.15 = (bf16[192,1024]{1,0:T(8,128)(2,1)}, bf16[192,1024]{1,0:T(8,128)(2,1)}, u32[]{:S(2)}, u32[]{:S(2)}) collective-permute-start(bf16[192,1024]{1,0:T(8,128)(2,1)} %get-tuple-element.76), channel_id=1, source_target_pairs={{0,96},{8,104},{16,112},{24,120},{32,64},{40,72},{48,80},{56,88},{... | collective-permute-start | bytes 1179656 | tf_op jit(solution)/shard_map/ppermute | solution.py:521
  80.5 0.7 copy-start.8
  81.2 38.9 %copy-start.2 = (bf16[4,192,1024]{2,1,0:T(8,128)(2,1)}, bf16[4,192,1024]{2,1,0:T(8,128)(2,1)S(1)}, u32[]{:S(2)}) copy-start(bf16[4,192,1024]{2,1,0:T(8,128)(2,1)S(1)} %collective-permute-done.11.other_ref) | copy-start | bytes 4718596
  85.2 0.8 copy-start.9
  96.7 5.0 %collective-permute-start.12 = (bf16[192,256]{1,0:T(8,128)(2,1)}, bf16[192,256]{1,0:T(8,128)(2,1)}, u32[]{:S(2)}, u32[]{:S(2)}) collective-permute-start(bf16[192,256]{1,0:T(8,128)(2,1)} %get-tuple-element.73), channel_id=1, source_target_pairs={{0,32},{8,40},{16,48},{24,56},{32,64},{40,72},{48,80},{56,88},{64,... | collective-permute-start | bytes 294920 | tf_op jit(solution)/shard_map/ppermute | solution.py:473
  98.5 5.4 %collective-permute-start.13 = (bf16[192,256]{1,0:T(8,128)(2,1)}, bf16[192,256]{1,0:T(8,128)(2,1)}, u32[]{:S(2)}, u32[]{:S(2)}) collective-permute-start(bf16[192,256]{1,0:T(8,128)(2,1)} %get-tuple-element.74), channel_id=1, source_target_pairs={{0,64},{8,72},{16,80},{24,88},{32,96},{40,104},{48,112},{56,120},{... | collective-permute-start | bytes 294920 | tf_op jit(solution)/shard_map/ppermute | solution.py:473
  98.5 5.4 %collective-permute-start.14 = (bf16[192,256]{1,0:T(8,128)(2,1)}, bf16[192,256]{1,0:T(8,128)(2,1)}, u32[]{:S(2)}, u32[]{:S(2)}) collective-permute-start(bf16[192,256]{1,0:T(8,128)(2,1)} %get-tuple-element.75), channel_id=1, source_target_pairs={{0,96},{8,104},{16,112},{24,120},{32,0},{40,8},{48,16},{56,24},{64... | collective-permute-start | bytes 294920 | tf_op jit(solution)/shard_map/ppermute | solution.py:473
  105.7 8.8 %collective-permute-start.16 = (bf16[192,512]{1,0:T(8,128)(2,1)}, bf16[192,512]{1,0:T(8,128)(2,1)S(1)}, u32[]{:S(2)}, u32[]{:S(2)}) collective-permute-start(bf16[192,512]{1,0:T(8,128)(2,1)} %x_sum.1.refs_0_), channel_id=1, source_target_pairs={{0,2},{2,4},{4,6},{6,0},{1,3},{3,5},{5,7},{7,1},{8,10},{10,12},{12... | collective-permute-start | bytes 589832 | tf_op jit(solution)/shard_map/ppermute | solution.py:469
  107.3 9.7 %collective-permute-start.17 = (bf16[192,512]{1,0:T(8,128)(2,1)}, bf16[192,512]{1,0:T(8,128)(2,1)S(1)}, u32[]{:S(2)}, u32[]{:S(2)}) collective-permute-start(bf16[192,512]{1,0:T(8,128)(2,1)} %x_sum.1.refs_0_), channel_id=1, source_target_pairs={{0,4},{2,6},{4,0},{6,2},{1,5},{3,7},{5,1},{7,3},{8,12},{10,14},{12... | collective-permute-start | bytes 589832 | tf_op jit(solution)/shard_map/ppermute | solution.py:469
  108.9 11.2 %collective-permute-start.18 = (bf16[192,512]{1,0:T(8,128)(2,1)}, bf16[192,512]{1,0:T(8,128)(2,1)S(1)}, u32[]{:S(2)}, u32[]{:S(2)}) collective-permute-start(bf16[192,512]{1,0:T(8,128)(2,1)} %x_sum.1.refs_0_), channel_id=1, source_target_pairs={{0,6},{2,0},{4,2},{6,4},{1,7},{3,1},{5,3},{7,5},{8,14},{10,8},{12,... | collective-permute-start | bytes 589832 | tf_op jit(solution)/shard_map/ppermute | solution.py:469
  110.9 9.2 %collective-permute-start.19 = (bf16[192,512]{1,0:T(8,128)(2,1)}, bf16[192,512]{1,0:T(8,128)(2,1)S(1)}, u32[]{:S(2)}, u32[]{:S(2)}) collective-permute-start(bf16[192,512]{1,0:T(8,128)(2,1)} %x_sum.1.refs_0_), channel_id=1, source_target_pairs={{0,1},{1,0},{2,3},{3,2},{4,5},{5,4},{6,7},{7,6},{8,9},{9,8},{10,11... | collective-permute-start | bytes 589832 | tf_op jit(solution)/shard_map/ppermute | solution.py:534
  114.5 5.7 %copy-start.10 = (bf16[192,512]{1,0:T(8,128)(2,1)}, bf16[192,512]{1,0:T(8,128)(2,1)S(1)}, u32[]{:S(2)}) copy-start(bf16[192,512]{1,0:T(8,128)(2,1)S(1)} %collective-permute-done.16.refs_1_) | copy-start | bytes 589828
  114.5 5.6 %collective-permute-start.20 = (bf16[192,512]{1,0:T(8,128)(2,1)S(1)}, bf16[192,512]{1,0:T(8,128)(2,1)S(1)}, u32[]{:S(2)}, u32[]{:S(2)}) collective-permute-start(bf16[192,512]{1,0:T(8,128)(2,1)S(1)} %collective-permute-done.16.refs_1_), channel_id=1, source_target_pairs={{0,1},{1,0},{2,3},{3,2},{4,5},{5,4},{6,7},{7,6},{8,9},{9,8},{10,11... | collective-permute-start | bytes 589832 | tf_op jit(solution)/shard_map/ppermute | solution.py:534
  117.0 3.2 %copy-start.11 = (bf16[192,512]{1,0:T(8,128)(2,1)}, bf16[192,512]{1,0:T(8,128)(2,1)S(1)}, u32[]{:S(2)}) copy-start(bf16[192,512]{1,0:T(8,128)(2,1)S(1)} %collective-permute-done.17.refs_2_) | copy-start | bytes 589828
  117.0 3.2 %collective-permute-start.21 = (bf16[192,512]{1,0:T(8,128)(2,1)S(1)}, bf16[192,512]{1,0:T(8,128)(2,1)S(1)}, u32[]{:S(2)}, u32[]{:S(2)}) collective-permute-start(bf16[192,512]{1,0:T(8,128)(2,1)S(1)} %collective-permute-done.17.refs_2_), channel_id=1, source_target_pairs={{0,1},{1,0},{2,3},{3,2},{4,5},{5,4},{6,7},{7,6},{8,9},{9,8},{10,11... | collective-permute-start | bytes 589832 | tf_op jit(solution)/shard_map/ppermute | solution.py:534
  120.1 6.8 %copy-start.18 = (bf16[192,512]{1,0:T(8,128)(2,1)}, bf16[192,512]{1,0:T(8,128)(2,1)S(1)}, u32[]{:S(2)}) copy-start(bf16[192,512]{1,0:T(8,128)(2,1)S(1)} %collective-permute-done.19.refs_4_) | copy-start | bytes 589828
  120.1 6.8 %copy-start.19 = (bf16[192,512]{1,0:T(8,128)(2,1)}, bf16[192,512]{1,0:T(8,128)(2,1)S(1)}, u32[]{:S(2)}) copy-start(bf16[192,512]{1,0:T(8,128)(2,1)S(1)} %collective-permute-done.20.refs_5_) | copy-start | bytes 589828
  120.8 6.1 %copy-start.20 = (bf16[192,512]{1,0:T(8,128)(2,1)}, bf16[192,512]{1,0:T(8,128)(2,1)S(1)}, u32[]{:S(2)}) copy-start(bf16[192,512]{1,0:T(8,128)(2,1)S(1)} %collective-permute-done.21.refs_6_) | copy-start | bytes 589828
  126.9 5.2 %copy-start.13 = (bf16[192,512]{1,0:T(8,128)(2,1)S(1)}, bf16[192,512]{1,0:T(8,128)(2,1)}, u32[]{:S(2)}) copy-start(bf16[192,512]{1,0:T(8,128)(2,1)} %copy-done.12) | copy-start | bytes 589828
  126.9 41.8 %all-to-all-start.1 = ((bf16[16,128,512]{2,1,0:T(8,128)(2,1)}), bf16[16,128,512]{2,1,0:T(8,128)(2,1)S(1)}, u32[]{:S(2)}, u32[]{:S(2)}) async-start(bf16[16,128,512]{2,1,0:T(8,128)(2,1)} %bitcast.32), calls=%async_computation.1 | async-start | bytes 4194304 | tf_op jit(solution)/shard_map/all_to_all | solution.py:538
  132.1 1.7 collective-permute-start.22
  139.6 12.6 %collective-permute-start.23 = (bf16[192,1024]{1,0:T(8,128)(2,1)}, bf16[192,1024]{1,0:T(8,128)(2,1)S(1)}, u32[]{:S(2)}, u32[]{:S(2)}) collective-permute-start(bf16[192,1024]{1,0:T(8,128)(2,1)} %get-tuple-element.94), channel_id=1, source_target_pairs={{0,0},{1,2},{2,4},{3,6},{4,1},{5,3},{6,5},{7,7},{8,8},{9,10},{10,1... | collective-permute-start | bytes 1179656 | tf_op jit(solution)/shard_map/ppermute | solution.py:552
  141.8 17.6 %collective-permute-start.24 = (bf16[192,1024]{1,0:T(8,128)(2,1)}, bf16[192,1024]{1,0:T(8,128)(2,1)S(1)}, u32[]{:S(2)}, u32[]{:S(2)}) collective-permute-start(bf16[192,1024]{1,0:T(8,128)(2,1)} %get-tuple-element.95), channel_id=1, source_target_pairs={{0,2},{1,4},{2,6},{3,0},{4,3},{5,5},{6,7},{7,1},{8,10},{9,12},{10,... | collective-permute-start | bytes 1179656 | tf_op jit(solution)/shard_map/ppermute | solution.py:552
  146.7 15.0 %collective-permute-start.25 = (bf16[192,1024]{1,0:T(8,128)(2,1)}, bf16[192,1024]{1,0:T(8,128)(2,1)S(1)}, u32[]{:S(2)}, u32[]{:S(2)}) collective-permute-start(bf16[192,1024]{1,0:T(8,128)(2,1)} %get-tuple-element.96), channel_id=1, source_target_pairs={{0,4},{1,6},{2,0},{3,2},{4,5},{5,7},{6,1},{7,3},{8,12},{9,14},{10,... | collective-permute-start | bytes 1179656 | tf_op jit(solution)/shard_map/ppermute | solution.py:552
  146.8 16.4 %collective-permute-start.26 = (bf16[192,1024]{1,0:T(8,128)(2,1)}, bf16[192,1024]{1,0:T(8,128)(2,1)}, u32[]{:S(2)}, u32[]{:S(2)}) collective-permute-start(bf16[192,1024]{1,0:T(8,128)(2,1)} %get-tuple-element.97), channel_id=1, source_target_pairs={{0,6},{1,0},{2,2},{3,4},{4,7},{5,1},{6,3},{7,5},{8,14},{9,8},{10,1... | collective-permute-start | bytes 1179656 | tf_op jit(solution)/shard_map/ppermute | solution.py:552
  152.2 10.9 %copy-start.3 = (bf16[192,1024]{1,0:T(8,128)(2,1)}, bf16[192,1024]{1,0:T(8,128)(2,1)S(1)}, u32[]{:S(2)}) copy-start(bf16[192,1024]{1,0:T(8,128)(2,1)S(1)} %collective-permute-done.23.refs_0_) | copy-start | bytes 1179652
  159.4 3.7 %copy-start.4 = (bf16[192,1024]{1,0:T(8,128)(2,1)}, bf16[192,1024]{1,0:T(8,128)(2,1)S(1)}, u32[]{:S(2)}) copy-start(bf16[192,1024]{1,0:T(8,128)(2,1)S(1)} %collective-permute-done.24.refs_1_) | copy-start | bytes 1179652
  161.7 1.5 copy-start.5
  (3 other events, 2.1 us)
where the time goes:
time: 173 us; the launch traced here: 170 us
  starting transfers between devices  58.7 us (34%)
  Pallas kernels  49.3 us (28%)
  waiting for transfers between devices  40.9 us (24%)
  local copies, waits for them, and re-layouts  13.4 us (8%)
  other arithmetic  6.47 us (4%)
    ppermute x6, waiting for transfers between devices, shift_y(): return lax.ppermute(array, 'seq', pairs)  24.5 us
    pallas_call x1, Pallas kernels, attention_backward(): pl.pallas_call(attention_kernel, out_shape=[jax.ShapeDtypeStruct((cap, wi...  22.9 us
    ppermute x6, starting transfers between devices, shift_y(): return lax.ppermute(array, 'seq', pairs)  12.3 us
    ppermute x4, waiting for transfers between devices, shards(): received.append(lax.ppermute(products[step], ('dp', 'rep'), pairs))  12.3 us
    ppermute x4, starting transfers between devices, shards(): received.append(lax.ppermute(products[step], ('dp', 'rep'), pairs))  10.6 us
    ppermute x6, starting transfers between devices, shift_x(): return lax.ppermute(array, 'seq', pairs)  9.86 us
    ppermute x4, starting transfers between devices, shards(): kv_far = [lax.ppermute(part, 'rep', swap) for part in kv_all]  7.78 us
    pallas_call x1, Pallas kernels, weight_terms(): pl.pallas_call(terms_kernel, grid_spec=pltpu.PrefetchScalarGridSpec(num_s...  6.12 us
  transfers between devices with their start and end apart: 29, of which 12 were waited for; matrix products, arithmetic and copies ran while one was open for 8% of the time, Pallas kernels for 24%

commit v1 on v0

--- a/solution.py
+++ b/solution.py
@@ -182,7 +182,7 @@
     for index in range(count):
         kv_s[index * cap : (index + 1) * cap, :half] = own[index][...]
         kv_s[index * cap : (index + 1) * cap, half:] = other[index][...]
-    chunk = 256
+    chunk = 512
     for first in range(0, out_s.shape[1], chunk):
         here = slice(first, first + chunk)
         total = lax.dot_general(
@@ -410,37 +410,46 @@
 
 
 def spread_kernel(order, target_ref, *refs):
-    parts, out_ref = refs[:-1], refs[-1]
+    parts, (out_ref, pick_ref) = refs[:2], refs[-2:]
     step = pl.program_id(0)
-    tokens, capacity = out_ref.shape[0], parts[0].shape[0]
-    token = lax.broadcasted_iota(jnp.int32, (tokens, capacity), 0)
-    pick = (token == target_ref[...]).astype(jnp.bfloat16)
+    tokens, capacity = pick_ref.shape
+
+    @pl.when(step == 0)
+    def _():
+        token = lax.broadcasted_iota(jnp.int32, (tokens, capacity), 0)
+        pick_ref[...] = (token == target_ref[...]).astype(jnp.bfloat16)
+
     for index, part in enumerate(parts):
 
         @pl.when(step == index)
         def _(part=part):
             out_ref[...] = lax.dot_general(
-                pick, part[...], ROWS_COLS, preferred_element_type=jnp.float32
+                pick_ref[...], part[...], ROWS_COLS, preferred_element_type=jnp.float32
             ).astype(jnp.bfloat16)
 
 
-def spread_rows(order, target, parts, tokens):
+def spread_rows(order, target, parts, shape, held=()):
     capacity, width = parts[0].shape
+    tokens = shape[0]
     whole = pl.BlockSpec((capacity, width), lambda s, order: (0, 0))
     return pl.pallas_call(
         spread_kernel,
         grid_spec=pltpu.PrefetchScalarGridSpec(
             num_scalar_prefetch=1,
             grid=(len(parts),),
-            in_specs=[pl.BlockSpec((1, capacity), lambda s, order: (0, 0))] + [whole] * len(parts),
+            in_specs=[pl.BlockSpec((1, capacity), lambda s, order: (0, 0))]
+            + [whole] * len(parts)
+            + [pl.BlockSpec(memory_space=pl.ANY)] * len(held),
             out_specs=pl.BlockSpec((tokens, width), lambda s, order: (0, order[s])),
-        ),
-        out_shape=jax.ShapeDtypeStruct((tokens, width * len(parts)), jnp.bfloat16),
+            scratch_shapes=[pltpu.VMEM((tokens, capacity), jnp.bfloat16)],
+        ),
+        out_shape=jax.ShapeDtypeStruct(shape, jnp.bfloat16),
+        input_output_aliases={2 + len(parts): 0} if held else {},
         cost_estimate=pl.CostEstimate(
-            flops=800_000_000, bytes_accessed=6_000_000, transcendentals=0
+            flops=400_000_000, bytes_accessed=3_000_000, transcendentals=0
         ),
         name="spread_rows",
-    )(order, target[None, :], *parts)
+    )(order, target[None, :], *parts, *held)
 
 
 def shards(hidden, kept, counts, queries, keys, values, out_grad, kv_weight):
@@ -494,12 +503,7 @@
     far = jnp.concatenate(
         [lax.dynamic_slice_in_dim(array[0], sent, group_columns, 1) for array in (queries, out_grad)], axis=1
     )
-    halves = kv_weight.reshape(rep_devices, part_rows, 2 * width)
-    kept_half = lax.dynamic_index_in_dim(halves, rep_index, 0, keepdims=False)
-    sent_half = lax.dynamic_index_in_dim(halves, 1 - rep_index, 0, keepdims=False)
-    kv_x, far, hidden, kept_half, sent_half = lax.optimization_barrier(
-        (kv_x, far, hidden, kept_half, sent_half)
-    )
+    kv_x, far, hidden = lax.optimization_barrier((kv_x, far, hidden))
     kv_y = [kv_x] + [shift_y(kv_x, step) for step in range(1, SIDE)]
 
     far = lax.ppermute(far, "seq", mirror)
@@ -507,12 +511,9 @@
     own_rows = lax.dynamic_index_in_dim(kept[0], seq_index, 0, keepdims=False)
     own_count = lax.dynamic_index_in_dim(counts[0], seq_index, 0, keepdims=False)
     columns = gather_columns(place, own_rows, hidden[0], dp_devices, rep_devices)
-    other_half = lax.ppermute(sent_half, "rep", swap)
     slot_index = jnp.arange(capacity, dtype=jnp.int32)
     target = jnp.where(slot_index < own_count, own_rows, tokens_local)
-    kv_y[1:], columns, kept_half, other_half, target = lax.optimization_barrier(
-        (kv_y[1:], columns, kept_half, other_half, target)
-    )
+    kv_y[1:], columns, target = lax.optimization_barrier((kv_y[1:], columns, target))
     columns = lax.all_to_all(columns, "dp", split_axis=0, concat_axis=0, tiled=True)
 
     grads = attention_backward(counts[0], place, queries[0], out_grad[0], far, kv_y)
@@ -520,11 +521,19 @@
     kv_back = [kv_back[0]] + [shift_y(kv_back[step], step) for step in range(1, SIDE)]
     dq_back = lax.ppermute(dq_far, "seq", mirror)
     columns_far = lax.ppermute(columns, "rep", swap)
-    kv_back[-1], columns_far = lax.optimization_barrier((kv_back[-1], columns_far))
+    dq_back, kv_weight = lax.optimization_barrier((dq_back, kv_weight))
+    halves = kv_weight.reshape(rep_devices, part_rows, 2 * width)
+    kept_half = lax.dynamic_index_in_dim(halves, rep_index, 0, keepdims=False)
+    sent_half = lax.dynamic_index_in_dim(halves, 1 - rep_index, 0, keepdims=False)
+    kv_back[-1], columns_far, kept_half, sent_half = lax.optimization_barrier(
+        (kv_back[-1], columns_far, kept_half, sent_half)
+    )
 
     pieces = y_sum(place, kv_back)
+    pieces, sent_half = lax.optimization_barrier((pieces, sent_half))
+    other_half = lax.ppermute(sent_half, "rep", swap)
     pieces = [pieces[0]] + [shift_x(pieces[step], step) for step in range(1, SIDE)]
-    pieces, dq_back = lax.optimization_barrier((pieces, dq_back))
+    pieces, dq_back, other_half = lax.optimization_barrier((pieces, dq_back, other_half))
     kv_grad = x_sum(place, pieces, local_groups)
     dq_first = jnp.where(group == 0, dq_own, dq_back)
     dq_last = jnp.where(group == 0, dq_back, dq_own)
@@ -532,7 +541,7 @@
 
     kv_all = [kv_grad] + [shift_dp(kv_grad, step) for step in range(1, dp_devices)]
     kv_far = [lax.ppermute(part, "rep", swap) for part in kv_all]
-    kv_all, kv_far[:-1], back_query = lax.optimization_barrier((kv_all, kv_far[:-1], back_query))
+    kv_all, kv_far, back_query = lax.optimization_barrier((kv_all, kv_far, back_query))
 
     terms = weight_terms(place, columns, columns_far, kv_all)
     terms = lax.all_to_all(
@@ -550,8 +559,12 @@
                 to_dp = (lane + step) % dp_devices
                 pairs.append((dp * rep_devices + rep, to_dp * rep_devices + dp // dp_per_rep))
         received.append(lax.ppermute(products[step], ("dp", "rep"), pairs))
-    order = jnp.stack([(dp_index - step) % dp_devices for step in range(dp_devices)]).astype(jnp.int32)
-    grad_hidden = spread_rows(order, target, received, tokens_local)
+    held = ()
+    for steps in ((0, 3), (1, 2)):
+        order = jnp.stack([(dp_index - step) % dp_devices for step in steps]).astype(jnp.int32)
+        parts = [received[step] for step in steps]
+        held = (spread_rows(order, target, parts, (tokens_local, dp_devices * part_rows), held),)
+    grad_hidden = held[0]
     return (back_query[None], grad_hidden[None], grad_weight)
 
 

time: 173 us -> 167 us (0.965); the launches traced: 170 us -> 166 us
  waiting for transfers between devices: 40.9 us -> 48.6 us
  Pallas kernels: 49.3 us -> 45 us
  other arithmetic: 6.47 us -> 3.26 us
  starting transfers between devices: 58.7 us -> 55.6 us
    ppermute x3, waiting for transfers between devices: 0.01 us -> 6.56 us  [shift_dp(): lax.ppermute(array, 'dp', [(i, (i + step) % dp_devices) for i in range(dp...]
    pallas_call x1, Pallas kernels: 22.9 us -> 16.3 us  [attention_backward(): pl.pallas_call(attention_kernel, out_shape=[jax.ShapeDtypeStruct((cap, wi...]
    ppermute x4, starting transfers between devices: 7.78 us -> 3.95 us  [shards(): kv_far = [lax.ppermute(part, 'rep', swap) for part in kv_all]]
    ppermute x4, waiting for transfers between devices: 12.3 us -> 9.31 us  [shards(): received.append(lax.ppermute(products[step], ('dp', 'rep'), pairs))]
    all_to_all x1, waiting for transfers between devices: 0.01 us -> 2.89 us  [shards(): lax.all_to_all(columns, 'dp', split_axis=0, concat_axis=0, tiled=True)]
    ppermute x6, waiting for transfers between devices: 2.96 us -> 5.79 us  [shift_x(): return lax.ppermute(array, 'seq', pairs)]
    ppermute x1, starting transfers between devices: 0.01 us -> 2.39 us  [shards(): far = lax.ppermute(far, 'seq', mirror)]
    ppermute x1, starting transfers between devices: 0.01 us -> 2.39 us  [shards(): dq_back = lax.ppermute(dq_far, 'seq', mirror)]
  transfers between devices with their start and end apart: 29 -> 29, of which waited for: 12 -> 16; matrix products, arithmetic and copies ran while one was open for 8% -> 7% of each run, Pallas kernels for 24% -> 21%
where the time goes in v1:
time: 167 us; the launch traced here: 166 us
  starting transfers between devices  55.6 us (33%)
  waiting for transfers between devices  48.6 us (29%)
  Pallas kernels  45 us (27%)
  local copies, waits for them, and re-layouts  12.1 us (7%)
  other arithmetic  3.26 us (2%)
    ppermute x6, waiting for transfers between devices, shift_y(): return lax.ppermute(array, 'seq', pairs)  22.4 us
    pallas_call x1, Pallas kernels, attention_backward(): pl.pallas_call(attention_kernel, out_shape=[jax.ShapeDtypeStruct((cap, wi...  16.3 us
    ppermute x6, starting transfers between devices, shift_y(): return lax.ppermute(array, 'seq', pairs)  12.2 us
    ppermute x4, starting transfers between devices, shards(): received.append(lax.ppermute(products[step], ('dp', 'rep'), pairs))  10.1 us
    ppermute x4, waiting for transfers between devices, shards(): received.append(lax.ppermute(products[step], ('dp', 'rep'), pairs))  9.31 us
    ppermute x6, starting transfers between devices, shift_x(): return lax.ppermute(array, 'seq', pairs)  8.46 us
    pallas_call x2, Pallas kernels, spread_rows(): pl.pallas_call(spread_kernel, grid_spec=pltpu.PrefetchScalarGridSpec(num_...  7.35 us
    ppermute x3, waiting for transfers between devices, shift_dp(): lax.ppermute(array, 'dp', [(i, (i + step) % dp_devices) for i in range(dp...  6.56 us
  transfers between devices with their start and end apart: 29, of which 16 were waited for; matrix products, arithmetic and copies ran while one was open for 7% of the time, Pallas kernels for 21%

profile of v1, /device:TPU:1, one launch (start us, length us, event | category | flops | bytes accessed | tf_op | source)
XLA Modules:
  0.0 165.6 jit_solution(182016468235000948)
XLA Ops:
  0.8 0.9 fusion
  1.7 2.1 %collective-permute-start = (bf16[192,256]{1,0:T(8,128)(2,1)S(1)}, bf16[192,256]{1,0:T(8,128)(2,1)S(1)}, u32[]{:S(2)}, u32[]{:S(2)}) collective-permute-start(bf16[192,256]{1,0:T(8,128)(2,1)S(1)} %get-tuple-element.118), channel_id=1, source_target_pairs={{0,32},{8,40},{16,48},{24,56},{32,64},{40,72},{48,80},{56,88},{64,... | collective-permute-start | bytes 294920 | tf_op jit(solution)/shard_map/ppermute | solution.py:482
  3.8 2.5 %collective-permute-start.1 = (bf16[192,256]{1,0:T(8,128)(2,1)S(1)}, bf16[192,256]{1,0:T(8,128)(2,1)S(1)}, u32[]{:S(2)}, u32[]{:S(2)}) collective-permute-start(bf16[192,256]{1,0:T(8,128)(2,1)S(1)} %get-tuple-element.119), channel_id=1, source_target_pairs={{0,64},{8,72},{16,80},{24,88},{32,96},{40,104},{48,112},{56,120},{... | collective-permute-start | bytes 294920 | tf_op jit(solution)/shard_map/ppermute | solution.py:482
  6.3 1.2 collective-permute-start.2
  7.5 1.2 constant_dynamic-slice_fusion
  8.8 1.2 dynamic-slice_bitcast_fusion.2
  10.4 2.9 %collective-permute-start.6 = (bf16[768,256]{1,0:T(8,128)(2,1)S(1)}, bf16[768,256]{1,0:T(8,128)(2,1)S(1)}, u32[]{:S(2)}, u32[]{:S(2)}) collective-permute-start(bf16[768,256]{1,0:T(8,128)(2,1)S(1)} %pad_maximum_fusion.2.kv0), channel_id=1, source_target_pairs={{0,24},{8,0},{16,8},{24,16},{32,56},{40,32},{48,40},{56,48},{64,88... | collective-permute-start | bytes 1179656 | tf_op jit(solution)/shard_map/ppermute | solution.py:486
  14.2 1.2 compare_select_fusion
  15.5 2.4 %collective-permute-start.3 = (bf16[192,2048]{1,0:T(8,128)(2,1)S(1)}, bf16[192,2048]{1,0:T(8,128)(2,1)S(1)}, u32[]{:S(2)}, u32[]{:S(2)}) collective-permute-start(bf16[192,2048]{1,0:T(8,128)(2,1)S(1)} %pad_maximum_fusion), channel_id=1, source_target_pairs={{0,96},{8,104},{16,112},{24,120},{32,64},{40,72},{48,80},{56,88},{... | collective-permute-start | bytes 2359304 | tf_op jit(solution)/shard_map/ppermute | solution.py:509
  19.3 5.6 %gather_columns.1 = bf16[4,192,1024]{2,1,0:T(8,128)(2,1)} custom-call(s32[6]{0:T(128)} %stack.45.place, s32[192,1]{1,0:T(8,128)} %copy.12.rows_ref, bf16[512,8192]{1,0:T(8,128)(2,1)} %bitcast.34), custom_call_target="tpu_custom_call" | custom-call | flops 800000000 | bytes 6000000 | tf_op jit(solution)/shard_map/gather_columns/pallas_call | solution.py:45
  24.9 9.3 %collective-permute-done.4.kv1 = bf16[768,256]{1,0:T(8,128)(2,1)S(1)} collective-permute-done((bf16[768,256]{1,0:T(8,128)(2,1)S(1)}, bf16[768,256]{1,0:T(8,128)(2,1)S(1)}, u32[]{:S(2)}, u32[]{:S(2)}) %collective-permute-start.4) | collective-permute-done | bytes 393248 | tf_op jit(solution)/shard_map/ppermute | solution.py:486
  34.2 5.0 %all-to-all-start = ((bf16[4,192,1024]{2,1,0:T(8,128)(2,1)}), bf16[4,192,1024]{2,1,0:T(8,128)(2,1)}, u32[]{:S(2)}, u32[]{:S(2)}) async-start(bf16[4,192,1024]{2,1,0:T(8,128)(2,1)} %gather_columns.1), calls=%async_computation | async-start | bytes 3145728 | tf_op jit(solution)/shard_map/all_to_all | solution.py:517
  40.1 16.3 %attention_backward.1 = (bf16[192,1024]{1,0:T(8,128)(2,1)}, bf16[192,1024]{1,0:T(8,128)(2,1)}, bf16[768,256]{1,0:T(8,128)(2,1)}, bf16[768,256]{1,0:T(8,128)(2,1)...) custom-call(s32[16]{0:T(128)} %bitcast.43, s32[6]{0:T(128)} %stack.45.place, bf16[192,2048]{1,0:T(8,128)(2,1)} %bitcast.36, ...), custom_call_target="tpu_custom_call" | custom-call | flops 6000000000 | bytes 6000000 | tf_op jit(solution)/shard_map/attention_backward/pallas_call | solution.py:384
  56.4 2.9 %all-to-all-done.own_ref = bf16[4,192,1024]{2,1,0:T(8,128)(2,1)} async-done(((bf16[4,192,1024]{2,1,0:T(8,128)(2,1)}), bf16[4,192,1024]{2,1,0:T(8,128)(2,1)}, u32[]{:S(2)}, u32[]{:S(2)}) %all-to-all-start) | async-done | bytes 1572896 | tf_op jit(solution)/shard_map/all_to_all | solution.py:517
  59.3 1.7 %collective-permute-start.10 = (bf16[4,192,1024]{2,1,0:T(8,128)(2,1)}, bf16[4,192,1024]{2,1,0:T(8,128)(2,1)}, u32[]{:S(2)}, u32[]{:S(2)}) collective-permute-start(bf16[4,192,1024]{2,1,0:T(8,128)(2,1)} %all-to-all-done.own_ref), channel_id=1, source_target_pairs={{0,1},{1,0},{2,3},{3,2},{4,5},{5,4},{6,7},{7,6},{8,9},{9,8},{10,11... | collective-permute-start | bytes 4718600 | tf_op jit(solution)/shard_map/ppermute | solution.py:523
  61.0 2.4 %collective-permute-start.11 = (bf16[192,1024]{1,0:T(8,128)(2,1)}, bf16[192,1024]{1,0:T(8,128)(2,1)S(1)}, u32[]{:S(2)}, u32[]{:S(2)}) collective-permute-start(bf16[192,1024]{1,0:T(8,128)(2,1)} %get-tuple-element.76), channel_id=1, source_target_pairs={{0,96},{8,104},{16,112},{24,120},{32,64},{40,72},{48,80},{56,88},{... | collective-permute-start | bytes 1179656 | tf_op jit(solution)/shard_map/ppermute | solution.py:522
  63.4 7.1 %collective-permute-start.9 = (bf16[768,256]{1,0:T(8,128)(2,1)}, bf16[768,256]{1,0:T(8,128)(2,1)}, u32[]{:S(2)}, u32[]{:S(2)}) collective-permute-start(bf16[768,256]{1,0:T(8,128)(2,1)} %get-tuple-element.74), channel_id=1, source_target_pairs={{0,24},{8,0},{16,8},{24,16},{32,56},{40,32},{48,40},{56,48},{64,88... | collective-permute-start | bytes 1179656 | tf_op jit(solution)/shard_map/ppermute | solution.py:486
  70.6 1.2 collective-permute-start.8
  71.8 1.4 collective-permute-done.11
  73.2 3.2 %reshape.22 = bf16[2,1024,512]{2,1,0:T(8,128)(2,1)S(1)} reshape(bf16[2048,2,256]{2,1,0:T(2,128)(2,1)} %param.15) | data formatting | bytes 4194304 | tf_op jit(solution)/shard_map/reshape | solution.py:525
  76.4 1.1 dynamic-slice_bitcast_fusion
  77.5 10.0 %collective-permute-done.9.refs_3_ = bf16[768,256]{1,0:T(8,128)(2,1)} collective-permute-done((bf16[768,256]{1,0:T(8,128)(2,1)}, bf16[768,256]{1,0:T(8,128)(2,1)}, u32[]{:S(2)}, u32[]{:S(2)}) %collective-permute-start.9) | collective-permute-done | bytes 393248 | tf_op jit(solution)/shard_map/ppermute | solution.py:486
  87.5 3.1 %collective-permute-done.7.refs_1_ = bf16[768,256]{1,0:T(8,128)(2,1)} collective-permute-done((bf16[768,256]{1,0:T(8,128)(2,1)}, bf16[768,256]{1,0:T(8,128)(2,1)}, u32[]{:S(2)}, u32[]{:S(2)}) %collective-permute-start.7) | collective-permute-done | bytes 393248 | tf_op jit(solution)/shard_map/ppermute | solution.py:486
  90.6 2.2 %y_sum.1 = (bf16[192,256]{1,0:T(8,128)(2,1)}, bf16[192,256]{1,0:T(8,128)(2,1)}, bf16[192,256]{1,0:T(8,128)(2,1)}, bf16[192,256]{1,0:T(8,128)(2,1)}) custom-call(s32[6]{0:T(128)} %stack.45.place, bf16[768,256]{1,0:T(8,128)(2,1)} %get-tuple-element.71.refs_0_, bf16[768,256]{1,0:T(8,128)(2,1)} %collective-permute-done.7.refs_1_, ...), custom_call_target="tpu_custom_call" | custom-call | flops 1000000 | bytes 2000000 | tf_op jit(solution)/shard_map/y_sum/pallas_call | solution.py:79
  92.8 1.5 collective-permute-start.15
  94.3 1.5 collective-permute-start.13
  95.8 1.2 collective-permute-start.14
  97.0 5.2 %collective-permute-done.12.refs_1_ = bf16[192,256]{1,0:T(8,128)(2,1)S(1)} collective-permute-done((bf16[192,256]{1,0:T(8,128)(2,1)}, bf16[192,256]{1,0:T(8,128)(2,1)S(1)}, u32[]{:S(2)}, u32[]{:S(2)}) %collective-permute-start.12) | collective-permute-done | bytes 98336 | tf_op jit(solution)/shard_map/ppermute | solution.py:482
  103.2 2.2 %x_sum.1.refs_0_ = bf16[192,512]{1,0:T(8,128)(2,1)} custom-call(s32[6]{0:T(128)} %stack.45.place, bf16[192,256]{1,0:T(8,128)(2,1)} %get-tuple-element.90.refs_0_, bf16[192,256]{1,0:T(8,128)(2,1)} %copy-done.9, bf16[192,256]{1,0:T(8,128)(2,1)} %copy-done.10, bf16[192,256]{1,0:T(8,128)(2,1)} %copy-done.11), custom_call_target="tpu_custom_call" | custom-call | flops 1000000 | bytes 1000000 | tf_op jit(solution)/shard_map/x_sum/pallas_call | solution.py:113
  105.4 1.1 collective-permute-start.19
  106.5 3.2 %collective-permute-start.17 = (bf16[192,512]{1,0:T(8,128)(2,1)}, bf16[192,512]{1,0:T(8,128)(2,1)S(1)}, u32[]{:S(2)}, u32[]{:S(2)}) collective-permute-start(bf16[192,512]{1,0:T(8,128)(2,1)} %x_sum.1.refs_0_), channel_id=1, source_target_pairs={{0,4},{2,6},{4,0},{6,2},{1,5},{3,7},{5,1},{7,3},{8,12},{10,14},{12... | collective-permute-start | bytes 589832 | tf_op jit(solution)/shard_map/ppermute | solution.py:478
  110.7 2.5 %collective-permute-done.18.refs_3_ = bf16[192,512]{1,0:T(8,128)(2,1)S(1)} collective-permute-done((bf16[192,512]{1,0:T(8,128)(2,1)}, bf16[192,512]{1,0:T(8,128)(2,1)S(1)}, u32[]{:S(2)}, u32[]{:S(2)}) %collective-permute-start.18) | collective-permute-done | bytes 196640 | tf_op jit(solution)/shard_map/ppermute | solution.py:478
  113.2 1.3 collective-permute-start.22
  115.1 1.0 collective-permute-start.21
  116.2 3.4 %collective-permute-done.16.refs_1_ = bf16[192,512]{1,0:T(8,128)(2,1)S(1)} collective-permute-done((bf16[192,512]{1,0:T(8,128)(2,1)}, bf16[192,512]{1,0:T(8,128)(2,1)S(1)}, u32[]{:S(2)}, u32[]{:S(2)}) %collective-permute-start.16) | collective-permute-done | bytes 196640 | tf_op jit(solution)/shard_map/ppermute | solution.py:478
  120.1 0.9 pad_maximum_fusion.1
  121.3 6.1 %weight_terms.1 = bf16[2048,512]{1,0:T(8,128)(2,1)} custom-call(s32[6]{0:T(128)} %stack.45.place, bf16[4,192,1024]{2,1,0:T(8,128)(2,1)} %all-to-all-done.own_ref, bf16[4,192,1024]{2,1,0:T(8,128)(2,1)} %collective-permute-done.10.other_ref, bf16[192,512]{1,0:T(8,128)(2,1)} %x_sum.1.refs_0_, bf16[192,512]{1,0:T(8,128)(2,1)} %copy-done.8, ...), custom_call_target="tpu_custom_call" | custom-call | flops 1600000000 | bytes 6000000 | tf_op jit(solution)/shard_map/weight_terms/pallas_call | solution.py:155
  127.4 3.7 %all-to-all-start.1 = ((bf16[16,128,512]{2,1,0:T(8,128)(2,1)}), bf16[16,128,512]{2,1,0:T(8,128)(2,1)S(1)}, u32[]{:S(2)}, u32[]{:S(2)}) async-start(bf16[16,128,512]{2,1,0:T(8,128)(2,1)} %bitcast.33), calls=%async_computation.1 | async-start | bytes 4194304 | tf_op jit(solution)/shard_map/all_to_all | solution.py:547
  131.1 5.2 %input_products.1 = (bf16[192,1024]{1,0:T(8,128)(2,1)}, bf16[192,1024]{1,0:T(8,128)(2,1)}, bf16[192,1024]{1,0:T(8,128)(2,1)}, bf16[192,1024]{1,0:T(8,128)(2,1)}) custom-call(s32[6]{0:T(128)} %stack.45.place, bf16[192,512]{1,0:T(8,128)(2,1)} %x_sum.1.refs_0_, bf16[192,512]{1,0:T(8,128)(2,1)} %copy-done.8, bf16[192,512]{1,0:T(8,128)(2,1)} %copy-done.7, ...), custom_call_target="tpu_custom_call" | custom-call | flops 1600000000 | bytes 6000000 | tf_op jit(solution)/shard_map/input_products/pallas_call | solution.py:208
  136.3 3.6 %collective-permute-start.25 = (bf16[192,1024]{1,0:T(8,128)(2,1)}, bf16[192,1024]{1,0:T(8,128)(2,1)S(1)}, u32[]{:S(2)}, u32[]{:S(2)}) collective-permute-start(bf16[192,1024]{1,0:T(8,128)(2,1)} %get-tuple-element.110), channel_id=1, source_target_pairs={{0,0},{1,2},{2,4},{3,6},{4,1},{5,3},{6,5},{7,7},{8,8},{9,10},{10,1... | collective-permute-start | bytes 1179656 | tf_op jit(solution)/shard_map/ppermute | solution.py:561
  139.9 1.9 %collective-permute-start.26 = (bf16[192,1024]{1,0:T(8,128)(2,1)}, bf16[192,1024]{1,0:T(8,128)(2,1)}, u32[]{:S(2)}, u32[]{:S(2)}) collective-permute-start(bf16[192,1024]{1,0:T(8,128)(2,1)} %get-tuple-element.111), channel_id=1, source_target_pairs={{0,6},{1,0},{2,2},{3,4},{4,7},{5,1},{6,3},{7,5},{8,14},{9,8},{10,1... | collective-permute-start | bytes 1179656 | tf_op jit(solution)/shard_map/ppermute | solution.py:561
  141.9 3.4 %collective-permute-start.23 = (bf16[192,1024]{1,0:T(8,128)(2,1)}, bf16[192,1024]{1,0:T(8,128)(2,1)S(1)}, u32[]{:S(2)}, u32[]{:S(2)}) collective-permute-start(bf16[192,1024]{1,0:T(8,128)(2,1)} %get-tuple-element.108), channel_id=1, source_target_pairs={{0,2},{1,4},{2,6},{3,0},{4,3},{5,5},{6,7},{7,1},{8,10},{9,12},{10,... | collective-permute-start | bytes 1179656 | tf_op jit(solution)/shard_map/ppermute | solution.py:561
  145.3 1.2 collective-permute-start.24
  147.0 1.4 collective-permute-done.25.refs_0_
  148.5 6.2 %collective-permute-done.26.refs_1_ = bf16[192,1024]{1,0:T(8,128)(2,1)} collective-permute-done((bf16[192,1024]{1,0:T(8,128)(2,1)}, bf16[192,1024]{1,0:T(8,128)(2,1)}, u32[]{:S(2)}, u32[]{:S(2)}) %collective-permute-start.26) | collective-permute-done | bytes 393248 | tf_op jit(solution)/shard_map/ppermute | solution.py:561
  154.7 3.7 %spread_rows.2.refs_2_ = bf16[512,4096]{1,0:T(8,128)(2,1)} custom-call(s32[2]{0:T(128)} %get-tuple-element.125.order, s32[1,192]{1,0:T(1,128)} %bitcast.40, bf16[192,1024]{1,0:T(8,128)(2,1)} %copy-done.3, bf16[192,1024]{1,0:T(8,128)(2,1)} %collective-permute-done.26.refs_1_), custom_call_target="tpu_custom_call" | custom-call | flops 400000000 | bytes 3000000 | tf_op jit(solution)/shard_map/spread_rows/pallas_call | solution.py:435
  160.8 3.7 %spread_rows.3 = bf16[512,4096]{1,0:T(8,128)(2,1)} custom-call(s32[2]{0:T(128)} %get-tuple-element.124.order, s32[1,192]{1,0:T(1,128)} %bitcast.41, bf16[192,1024]{1,0:T(8,128)(2,1)} %copy-done.1, bf16[192,1024]{1,0:T(8,128)(2,1)} %copy-done.2, bf16[512,4096]{1,0:T(8,128)(2,1)} %spread_rows.2.refs_2_), custom_call_target="tpu_custom_call", output_to_operand_aliasing={{}: (4, {})} | custom-call | flops 400000000 | bytes 3000000 | tf_op jit(solution)/shard_map/spread_rows/pallas_call | solution.py:435
  164.8 0.9 reshape.24
  (77 shorter events, 10.3 us)
Async XLA Ops:
  0.6 9.4 %copy-start = (s32[1,16,192]{2,1,0:T(8,128)S(1)}, s32[1,16,192]{2,1,0:T(8,128)}, u32[]{:S(2)}) copy-start(s32[1,16,192]{2,1,0:T(8,128)} %param.9) | copy-start | bytes 36868
  1.7 8.3 %collective-permute-start = (bf16[192,256]{1,0:T(8,128)(2,1)S(1)}, bf16[192,256]{1,0:T(8,128)(2,1)S(1)}, u32[]{:S(2)}, u32[]{:S(2)}) collective-permute-start(bf16[192,256]{1,0:T(8,128)(2,1)S(1)} %get-tuple-element.118), channel_id=1, source_target_pairs={{0,32},{8,40},{16,48},{24,56},{32,64},{40,72},{48,80},{56,88},{64,... | collective-permute-start | bytes 294920 | tf_op jit(solution)/shard_map/ppermute | solution.py:482
  3.8 6.5 %collective-permute-start.1 = (bf16[192,256]{1,0:T(8,128)(2,1)S(1)}, bf16[192,256]{1,0:T(8,128)(2,1)S(1)}, u32[]{:S(2)}, u32[]{:S(2)}) collective-permute-start(bf16[192,256]{1,0:T(8,128)(2,1)S(1)} %get-tuple-element.119), channel_id=1, source_target_pairs={{0,64},{8,72},{16,80},{24,88},{32,96},{40,104},{48,112},{56,120},{... | collective-permute-start | bytes 294920 | tf_op jit(solution)/shard_map/ppermute | solution.py:482
  6.3 4.0 %collective-permute-start.2 = (bf16[192,256]{1,0:T(8,128)(2,1)S(1)}, bf16[192,256]{1,0:T(8,128)(2,1)S(1)}, u32[]{:S(2)}, u32[]{:S(2)}) collective-permute-start(bf16[192,256]{1,0:T(8,128)(2,1)S(1)} %broadcast_select_fusion.2), channel_id=1, source_target_pairs={{0,96},{8,104},{16,112},{24,120},{32,0},{40,8},{48,16},{56,24},{64... | collective-permute-start | bytes 294920 | tf_op jit(solution)/shard_map/ppermute | solution.py:482
  10.3 14.5 %copy-start.4 = (bf16[768,256]{1,0:T(8,128)(2,1)}, bf16[768,256]{1,0:T(8,128)(2,1)S(1)}, u32[]{:S(2)}) copy-start(bf16[768,256]{1,0:T(8,128)(2,1)S(1)} %pad_maximum_fusion.2.kv0) | copy-start | bytes 1179652
  10.4 14.5 %collective-permute-start.6 = (bf16[768,256]{1,0:T(8,128)(2,1)S(1)}, bf16[768,256]{1,0:T(8,128)(2,1)S(1)}, u32[]{:S(2)}, u32[]{:S(2)}) collective-permute-start(bf16[768,256]{1,0:T(8,128)(2,1)S(1)} %pad_maximum_fusion.2.kv0), channel_id=1, source_target_pairs={{0,24},{8,0},{16,8},{24,16},{32,56},{40,32},{48,40},{56,48},{64,88... | collective-permute-start | bytes 1179656 | tf_op jit(solution)/shard_map/ppermute | solution.py:486
  13.2 11.6 %collective-permute-start.5 = (bf16[768,256]{1,0:T(8,128)(2,1)S(1)}, bf16[768,256]{1,0:T(8,128)(2,1)S(1)}, u32[]{:S(2)}, u32[]{:S(2)}) collective-permute-start(bf16[768,256]{1,0:T(8,128)(2,1)S(1)} %pad_maximum_fusion.2.kv0), channel_id=1, source_target_pairs={{0,16},{8,24},{16,0},{24,8},{32,48},{40,56},{48,32},{56,40},{64,80... | collective-permute-start | bytes 1179656 | tf_op jit(solution)/shard_map/ppermute | solution.py:486
  13.6 20.6 %collective-permute-start.4 = (bf16[768,256]{1,0:T(8,128)(2,1)S(1)}, bf16[768,256]{1,0:T(8,128)(2,1)S(1)}, u32[]{:S(2)}, u32[]{:S(2)}) collective-permute-start(bf16[768,256]{1,0:T(8,128)(2,1)S(1)} %pad_maximum_fusion.2.kv0), channel_id=1, source_target_pairs={{0,8},{8,16},{16,24},{24,0},{32,40},{40,48},{48,56},{56,32},{64,72... | collective-permute-start | bytes 1179656 | tf_op jit(solution)/shard_map/ppermute | solution.py:486
  15.5 23.7 %collective-permute-start.3 = (bf16[192,2048]{1,0:T(8,128)(2,1)S(1)}, bf16[192,2048]{1,0:T(8,128)(2,1)S(1)}, u32[]{:S(2)}, u32[]{:S(2)}) collective-permute-start(bf16[192,2048]{1,0:T(8,128)(2,1)S(1)} %pad_maximum_fusion), channel_id=1, source_target_pairs={{0,96},{8,104},{16,112},{24,120},{32,64},{40,72},{48,80},{56,88},{... | collective-permute-start | bytes 2359304 | tf_op jit(solution)/shard_map/ppermute | solution.py:509
  24.8 14.4 %copy-start.14 = (bf16[768,256]{1,0:T(8,128)(2,1)}, bf16[768,256]{1,0:T(8,128)(2,1)S(1)}, u32[]{:S(2)}) copy-start(bf16[768,256]{1,0:T(8,128)(2,1)S(1)} %collective-permute-done.6.kv3) | copy-start | bytes 1179652
  24.8 14.4 %copy-start.15 = (bf16[768,256]{1,0:T(8,128)(2,1)}, bf16[768,256]{1,0:T(8,128)(2,1)S(1)}, u32[]{:S(2)}) copy-start(bf16[768,256]{1,0:T(8,128)(2,1)S(1)} %collective-permute-done.5.kv2) | copy-start | bytes 1179652
  34.2 5.1 %copy-start.16 = (bf16[768,256]{1,0:T(8,128)(2,1)}, bf16[768,256]{1,0:T(8,128)(2,1)S(1)}, u32[]{:S(2)}) copy-start(bf16[768,256]{1,0:T(8,128)(2,1)S(1)} %collective-permute-done.4.kv1) | copy-start | bytes 1179652
  34.2 25.2 %all-to-all-start = ((bf16[4,192,1024]{2,1,0:T(8,128)(2,1)}), bf16[4,192,1024]{2,1,0:T(8,128)(2,1)}, u32[]{:S(2)}, u32[]{:S(2)}) async-start(bf16[4,192,1024]{2,1,0:T(8,128)(2,1)} %gather_columns.1), calls=%async_computation | async-start | bytes 3145728 | tf_op jit(solution)/shard_map/all_to_all | solution.py:517
  39.2 0.9 copy-start.13
  59.3 28.1 %collective-permute-start.10 = (bf16[4,192,1024]{2,1,0:T(8,128)(2,1)}, bf16[4,192,1024]{2,1,0:T(8,128)(2,1)}, u32[]{:S(2)}, u32[]{:S(2)}) collective-permute-start(bf16[4,192,1024]{2,1,0:T(8,128)(2,1)} %all-to-all-done.own_ref), channel_id=1, source_target_pairs={{0,1},{1,0},{2,3},{3,2},{4,5},{5,4},{6,7},{7,6},{8,9},{9,8},{10,11... | collective-permute-start | bytes 4718600 | tf_op jit(solution)/shard_map/ppermute | solution.py:523
  61.0 12.2 %collective-permute-start.11 = (bf16[192,1024]{1,0:T(8,128)(2,1)}, bf16[192,1024]{1,0:T(8,128)(2,1)S(1)}, u32[]{:S(2)}, u32[]{:S(2)}) collective-permute-start(bf16[192,1024]{1,0:T(8,128)(2,1)} %get-tuple-element.76), channel_id=1, source_target_pairs={{0,96},{8,104},{16,112},{24,120},{32,64},{40,72},{48,80},{56,88},{... | collective-permute-start | bytes 1179656 | tf_op jit(solution)/shard_map/ppermute | solution.py:522
  63.4 24.0 %collective-permute-start.9 = (bf16[768,256]{1,0:T(8,128)(2,1)}, bf16[768,256]{1,0:T(8,128)(2,1)}, u32[]{:S(2)}, u32[]{:S(2)}) collective-permute-start(bf16[768,256]{1,0:T(8,128)(2,1)} %get-tuple-element.74), channel_id=1, source_target_pairs={{0,24},{8,0},{16,8},{24,16},{32,56},{40,32},{48,40},{56,48},{64,88... | collective-permute-start | bytes 1179656 | tf_op jit(solution)/shard_map/ppermute | solution.py:486
  70.6 20.0 %collective-permute-start.7 = (bf16[768,256]{1,0:T(8,128)(2,1)}, bf16[768,256]{1,0:T(8,128)(2,1)}, u32[]{:S(2)}, u32[]{:S(2)}) collective-permute-start(bf16[768,256]{1,0:T(8,128)(2,1)} %get-tuple-element.72), channel_id=1, source_target_pairs={{0,8},{8,16},{16,24},{24,0},{32,40},{40,48},{48,56},{56,32},{64,72... | collective-permute-start | bytes 1179656 | tf_op jit(solution)/shard_map/ppermute | solution.py:486
  70.6 20.0 %collective-permute-start.8 = (bf16[768,256]{1,0:T(8,128)(2,1)}, bf16[768,256]{1,0:T(8,128)(2,1)}, u32[]{:S(2)}, u32[]{:S(2)}) collective-permute-start(bf16[768,256]{1,0:T(8,128)(2,1)} %get-tuple-element.73), channel_id=1, source_target_pairs={{0,16},{8,24},{16,0},{24,8},{32,48},{40,56},{48,32},{56,40},{64,80... | collective-permute-start | bytes 1179656 | tf_op jit(solution)/shard_map/ppermute | solution.py:486
  77.5 33.1 %copy-start.5 = (bf16[192,1024]{1,0:T(8,128)(2,1)S(1)}, bf16[192,1024]{1,0:T(8,128)(2,1)}, u32[]{:S(2)}) copy-start(bf16[192,1024]{1,0:T(8,128)(2,1)} %get-tuple-element.94) | copy-start | bytes 1179652
  92.8 9.7 %collective-permute-start.15 = (bf16[1024,512]{1,0:T(8,128)(2,1)S(1)}, bf16[1024,512]{1,0:T(8,128)(2,1)S(1)}, u32[]{:S(2)}, u32[]{:S(2)}) collective-permute-start(bf16[1024,512]{1,0:T(8,128)(2,1)S(1)} %get-tuple-element.89), channel_id=1, source_target_pairs={{0,1},{1,0},{2,3},{3,2},{4,5},{5,4},{6,7},{7,6},{8,9},{9,8},{10,11... | collective-permute-start | bytes 3145736 | tf_op jit(solution)/shard_map/ppermute | solution.py:534
  94.3 7.9 %collective-permute-start.12 = (bf16[192,256]{1,0:T(8,128)(2,1)}, bf16[192,256]{1,0:T(8,128)(2,1)S(1)}, u32[]{:S(2)}, u32[]{:S(2)}) collective-permute-start(bf16[192,256]{1,0:T(8,128)(2,1)} %get-tuple-element.85), channel_id=1, source_target_pairs={{0,32},{8,40},{16,48},{24,56},{32,64},{40,72},{48,80},{56,88},{64,... | collective-permute-start | bytes 294920 | tf_op jit(solution)/shard_map/ppermute | solution.py:482
  94.3 7.9 %collective-permute-start.13 = (bf16[192,256]{1,0:T(8,128)(2,1)}, bf16[192,256]{1,0:T(8,128)(2,1)S(1)}, u32[]{:S(2)}, u32[]{:S(2)}) collective-permute-start(bf16[192,256]{1,0:T(8,128)(2,1)} %get-tuple-element.86), channel_id=1, source_target_pairs={{0,64},{8,72},{16,80},{24,88},{32,96},{40,104},{48,112},{56,120},{... | collective-permute-start | bytes 294920 | tf_op jit(solution)/shard_map/ppermute | solution.py:482
  95.8 6.7 %collective-permute-start.14 = (bf16[192,256]{1,0:T(8,128)(2,1)}, bf16[192,256]{1,0:T(8,128)(2,1)S(1)}, u32[]{:S(2)}, u32[]{:S(2)}) collective-permute-start(bf16[192,256]{1,0:T(8,128)(2,1)} %get-tuple-element.87), channel_id=1, source_target_pairs={{0,96},{8,104},{16,112},{24,120},{32,0},{40,8},{48,16},{56,24},{64... | collective-permute-start | bytes 294920 | tf_op jit(solution)/shard_map/ppermute | solution.py:482
  102.2 0.7 copy-start.10
  102.5 0.6 copy-start.11
  103.2 2.2 %copy-start.12 = (bf16[1024,512]{1,0:T(8,128)(2,1)}, bf16[1024,512]{1,0:T(8,128)(2,1)S(1)}, u32[]{:S(2)}) copy-start(bf16[1024,512]{1,0:T(8,128)(2,1)S(1)} %collective-permute-done.15.refs_9_) | copy-start | bytes 3145732
  105.4 15.6 %collective-permute-start.19 = (bf16[192,512]{1,0:T(8,128)(2,1)}, bf16[192,512]{1,0:T(8,128)(2,1)S(1)}, u32[]{:S(2)}, u32[]{:S(2)}) collective-permute-start(bf16[192,512]{1,0:T(8,128)(2,1)} %x_sum.1.refs_0_), channel_id=1, source_target_pairs={{0,1},{1,0},{2,3},{3,2},{4,5},{5,4},{6,7},{7,6},{8,9},{9,8},{10,11... | collective-permute-start | bytes 589832 | tf_op jit(solution)/shard_map/ppermute | solution.py:543
  106.5 6.7 %collective-permute-start.18 = (bf16[192,512]{1,0:T(8,128)(2,1)}, bf16[192,512]{1,0:T(8,128)(2,1)S(1)}, u32[]{:S(2)}, u32[]{:S(2)}) collective-permute-start(bf16[192,512]{1,0:T(8,128)(2,1)} %x_sum.1.refs_0_), channel_id=1, source_target_pairs={{0,6},{2,0},{4,2},{6,4},{1,7},{3,1},{5,3},{7,5},{8,14},{10,8},{12,... | collective-permute-start | bytes 589832 | tf_op jit(solution)/shard_map/ppermute | solution.py:478
  106.5 8.6 %collective-permute-start.17 = (bf16[192,512]{1,0:T(8,128)(2,1)}, bf16[192,512]{1,0:T(8,128)(2,1)S(1)}, u32[]{:S(2)}, u32[]{:S(2)}) collective-permute-start(bf16[192,512]{1,0:T(8,128)(2,1)} %x_sum.1.refs_0_), channel_id=1, source_target_pairs={{0,4},{2,6},{4,0},{6,2},{1,5},{3,7},{5,1},{7,3},{8,12},{10,14},{12... | collective-permute-start | bytes 589832 | tf_op jit(solution)/shard_map/ppermute | solution.py:478
  109.8 9.8 %collective-permute-start.16 = (bf16[192,512]{1,0:T(8,128)(2,1)}, bf16[192,512]{1,0:T(8,128)(2,1)S(1)}, u32[]{:S(2)}, u32[]{:S(2)}) collective-permute-start(bf16[192,512]{1,0:T(8,128)(2,1)} %x_sum.1.refs_0_), channel_id=1, source_target_pairs={{0,2},{2,4},{4,6},{6,0},{1,3},{3,5},{5,7},{7,1},{8,10},{10,12},{12... | collective-permute-start | bytes 589832 | tf_op jit(solution)/shard_map/ppermute | solution.py:478
  113.2 8.1 %copy-start.6 = (bf16[192,512]{1,0:T(8,128)(2,1)}, bf16[192,512]{1,0:T(8,128)(2,1)S(1)}, u32[]{:S(2)}) copy-start(bf16[192,512]{1,0:T(8,128)(2,1)S(1)} %collective-permute-done.18.refs_3_) | copy-start | bytes 589828
  113.2 7.8 %collective-permute-start.22 = (bf16[192,512]{1,0:T(8,128)(2,1)S(1)}, bf16[192,512]{1,0:T(8,128)(2,1)S(1)}, u32[]{:S(2)}, u32[]{:S(2)}) collective-permute-start(bf16[192,512]{1,0:T(8,128)(2,1)S(1)} %collective-permute-done.18.refs_3_), channel_id=1, source_target_pairs={{0,1},{1,0},{2,3},{3,2},{4,5},{5,4},{6,7},{7,6},{8,9},{9,8},{10,11... | collective-permute-start | bytes 589832 | tf_op jit(solution)/shard_map/ppermute | solution.py:543
  115.1 6.1 %copy-start.7 = (bf16[192,512]{1,0:T(8,128)(2,1)}, bf16[192,512]{1,0:T(8,128)(2,1)S(1)}, u32[]{:S(2)}) copy-start(bf16[192,512]{1,0:T(8,128)(2,1)S(1)} %collective-permute-done.17.refs_2_) | copy-start | bytes 589828
  115.1 5.9 %collective-permute-start.21 = (bf16[192,512]{1,0:T(8,128)(2,1)S(1)}, bf16[192,512]{1,0:T(8,128)(2,1)S(1)}, u32[]{:S(2)}, u32[]{:S(2)}) collective-permute-start(bf16[192,512]{1,0:T(8,128)(2,1)S(1)} %collective-permute-done.17.refs_2_), channel_id=1, source_target_pairs={{0,1},{1,0},{2,3},{3,2},{4,5},{5,4},{6,7},{7,6},{8,9},{9,8},{10,11... | collective-permute-start | bytes 589832 | tf_op jit(solution)/shard_map/ppermute | solution.py:543
  119.6 1.7 %copy-start.8 = (bf16[192,512]{1,0:T(8,128)(2,1)}, bf16[192,512]{1,0:T(8,128)(2,1)S(1)}, u32[]{:S(2)}) copy-start(bf16[192,512]{1,0:T(8,128)(2,1)S(1)} %collective-permute-done.16.refs_1_) | copy-start | bytes 589828
  119.6 1.7 %collective-permute-start.20 = (bf16[192,512]{1,0:T(8,128)(2,1)S(1)}, bf16[192,512]{1,0:T(8,128)(2,1)}, u32[]{:S(2)}, u32[]{:S(2)}) collective-permute-start(bf16[192,512]{1,0:T(8,128)(2,1)S(1)} %collective-permute-done.16.refs_1_), channel_id=1, source_target_pairs={{0,1},{1,0},{2,3},{3,2},{4,5},{5,4},{6,7},{7,6},{8,9},{9,8},{10,11... | collective-permute-start | bytes 589832 | tf_op jit(solution)/shard_map/ppermute | solution.py:543
  121.0 6.4 %copy-start.17 = (bf16[192,512]{1,0:T(8,128)(2,1)}, bf16[192,512]{1,0:T(8,128)(2,1)S(1)}, u32[]{:S(2)}) copy-start(bf16[192,512]{1,0:T(8,128)(2,1)S(1)} %collective-permute-done.19.refs_4_) | copy-start | bytes 589828
  121.0 6.4 %copy-start.18 = (bf16[192,512]{1,0:T(8,128)(2,1)}, bf16[192,512]{1,0:T(8,128)(2,1)S(1)}, u32[]{:S(2)}) copy-start(bf16[192,512]{1,0:T(8,128)(2,1)S(1)} %collective-permute-done.22.refs_7_) | copy-start | bytes 589828
  121.0 6.3 %copy-start.19 = (bf16[192,512]{1,0:T(8,128)(2,1)}, bf16[192,512]{1,0:T(8,128)(2,1)S(1)}, u32[]{:S(2)}) copy-start(bf16[192,512]{1,0:T(8,128)(2,1)S(1)} %collective-permute-done.21.refs_6_) | copy-start | bytes 589828
  127.4 37.1 %all-to-all-start.1 = ((bf16[16,128,512]{2,1,0:T(8,128)(2,1)}), bf16[16,128,512]{2,1,0:T(8,128)(2,1)S(1)}, u32[]{:S(2)}, u32[]{:S(2)}) async-start(bf16[16,128,512]{2,1,0:T(8,128)(2,1)} %bitcast.33), calls=%async_computation.1 | async-start | bytes 4194304 | tf_op jit(solution)/shard_map/all_to_all | solution.py:547
  136.3 12.2 %collective-permute-start.25 = (bf16[192,1024]{1,0:T(8,128)(2,1)}, bf16[192,1024]{1,0:T(8,128)(2,1)S(1)}, u32[]{:S(2)}, u32[]{:S(2)}) collective-permute-start(bf16[192,1024]{1,0:T(8,128)(2,1)} %get-tuple-element.110), channel_id=1, source_target_pairs={{0,0},{1,2},{2,4},{3,6},{4,1},{5,3},{6,5},{7,7},{8,8},{9,10},{10,1... | collective-permute-start | bytes 1179656 | tf_op jit(solution)/shard_map/ppermute | solution.py:561
  139.9 14.8 %collective-permute-start.26 = (bf16[192,1024]{1,0:T(8,128)(2,1)}, bf16[192,1024]{1,0:T(8,128)(2,1)}, u32[]{:S(2)}, u32[]{:S(2)}) collective-permute-start(bf16[192,1024]{1,0:T(8,128)(2,1)} %get-tuple-element.111), channel_id=1, source_target_pairs={{0,6},{1,0},{2,2},{3,4},{4,7},{5,1},{6,3},{7,5},{8,14},{9,8},{10,1... | collective-permute-start | bytes 1179656 | tf_op jit(solution)/shard_map/ppermute | solution.py:561
  141.9 17.3 %collective-permute-start.23 = (bf16[192,1024]{1,0:T(8,128)(2,1)}, bf16[192,1024]{1,0:T(8,128)(2,1)S(1)}, u32[]{:S(2)}, u32[]{:S(2)}) collective-permute-start(bf16[192,1024]{1,0:T(8,128)(2,1)} %get-tuple-element.108), channel_id=1, source_target_pairs={{0,2},{1,4},{2,6},{3,0},{4,3},{5,5},{6,7},{7,1},{8,10},{9,12},{10,... | collective-permute-start | bytes 1179656 | tf_op jit(solution)/shard_map/ppermute | solution.py:561
  145.3 14.7 %collective-permute-start.24 = (bf16[192,1024]{1,0:T(8,128)(2,1)}, bf16[192,1024]{1,0:T(8,128)(2,1)S(1)}, u32[]{:S(2)}, u32[]{:S(2)}) collective-permute-start(bf16[192,1024]{1,0:T(8,128)(2,1)} %get-tuple-element.109), channel_id=1, source_target_pairs={{0,4},{1,6},{2,0},{3,2},{4,5},{5,7},{6,1},{7,3},{8,12},{9,14},{10,... | collective-permute-start | bytes 1179656 | tf_op jit(solution)/shard_map/ppermute | solution.py:561
  148.5 6.3 %copy-start.3 = (bf16[192,1024]{1,0:T(8,128)(2,1)}, bf16[192,1024]{1,0:T(8,128)(2,1)S(1)}, u32[]{:S(2)}) copy-start(bf16[192,1024]{1,0:T(8,128)(2,1)S(1)} %collective-permute-done.25.refs_0_) | copy-start | bytes 1179652
  159.2 0.9 copy-start.1
  160.0 0.8 copy-start.2
  (1 other events, 0.6 us)

commit v2 on v1

--- a/solution.py
+++ b/solution.py
@@ -13,6 +13,7 @@
 ROWS_ROWS = (((1,), (1,)), ((), ()))
 ROWS_COLS = (((1,), (0,)), ((), ()))
 QT = 512
+WIDE = 1024
 KT = 512
 VMEM_BYTES = 56 * 1024 * 1024
 SIDE = 4
@@ -269,13 +270,10 @@
         return carry
 
     lax.fori_loop(0, (total + cap + KT - 1) // KT, prepare, 0)
-    one_lane = lax.broadcasted_iota(jnp.int32, (QT, HEAD), 1)
-    ones = jnp.where(one_lane == 0, 1.0, 0.0).astype(bf)
     slot = lax.broadcasted_iota(jnp.int32, (cap, 2 * HEAD), 0)
     key_slot = lax.broadcasted_iota(jnp.int32, (cap, 2 * HEAD), 1)
     later = jnp.where(key_slot > slot, MASKED, 0.0).astype(bf)
     same = jnp.where(key_slot == slot, 1.0, 0.0).astype(bf)
-    key_row = lax.broadcasted_iota(jnp.int32, (KT, QT), 0)
 
     def one_shard(shard, q_ref, do_ref, q_first, do_first, dq_ref):
         count = counts[shard]
@@ -296,10 +294,14 @@
         own = pl.ds(before, cap)
         full = before // KT
         rest = before - full * KT
-        tiles = (far_heads * rows + QT - 1) // QT
-
-        def query_step(i, carry):
-            q_at = pl.ds(pl.multiple_of(i * QT, QT), QT)
+        wide = (far_heads * rows + QT - 1) // WIDE
+        narrow = (far_heads * rows > wide * WIDE).astype(jnp.int32)
+
+        def query_step(i, carry, size):
+            q_at = pl.ds(pl.multiple_of(i * WIDE, WIDE), size)
+            one_lane = lax.broadcasted_iota(jnp.int32, (size, HEAD), 1)
+            ones = jnp.where(one_lane == 0, 1.0, 0.0).astype(bf)
+            key_row = lax.broadcasted_iota(jnp.int32, (KT, size), 0)
             q = q_s[q_at, :]
             do = do_s[q_at, :]
             q_one = jnp.concatenate([q, ones], axis=1)
@@ -307,8 +309,8 @@
             scores = lax.dot_general(own_k, q, ROWS_ROWS, preferred_element_type=f32) * (scale * LOG2E)
             scores = scores + lax.dot_general(same, tri_s[q_at, :], ROWS_ROWS, preferred_element_type=f32)
             grads = lax.dot_general(v_s[own, :], do, ROWS_ROWS, preferred_element_type=f32)
-            so_s[...] = scores
-            go_s[...] = grads
+            so_s[:, :size] = scores
+            go_s[:, :size] = grads
             high = jnp.max(scores, axis=0, keepdims=True)
             e = jnp.exp2(scores - high)
             state = (high, jnp.sum(e, axis=0, keepdims=True), jnp.sum(e * grads, axis=0, keepdims=True))
@@ -321,8 +323,8 @@
                 scores = scores * (scale * LOG2E)
                 if partial:
                     scores = jnp.where(key_row < rest, scores, MASKED)
-                s_s[at, :] = scores
-                g_s[at, :] = grads
+                s_s[at, :size] = scores
+                g_s[at, :size] = grads
                 new = jnp.maximum(high, jnp.max(scores, axis=0, keepdims=True))
                 e = jnp.exp2(scores - new)
                 shrink = jnp.exp2(high - new)
@@ -345,14 +347,15 @@
                 dk_s[at, :] += lax.dot_general(dscore, q, ROWS_COLS, preferred_element_type=f32)
                 return lax.dot_general(key_t, dscore, ROWS_COLS, preferred_element_type=f32)
 
-            dq = spread(own, own_k.T, so_s[...], go_s[...])
+            dq = spread(own, own_k.T, so_s[:, :size], go_s[:, :size])
             dq = lax.fori_loop(
-                0, ends, lambda j, dq: dq + spread(k_at(j), kt_s[:, k_at(j)], s_s[k_at(j), :], g_s[k_at(j), :]), dq
+                0, ends, lambda j, dq: dq + spread(k_at(j), kt_s[:, k_at(j)], s_s[k_at(j), :size], g_s[k_at(j), :size]), dq
             )
             dq_s[q_at, :] = (dq * scale).T.astype(bf)
             return carry
 
-        lax.fori_loop(0, tiles, query_step, 0)
+        lax.fori_loop(0, wide, functools.partial(query_step, size=WIDE), 0)
+        lax.fori_loop(wide, wide + narrow, functools.partial(query_step, size=QT), 0)
         for h in range(far_heads):
             at = pl.ds(pl.multiple_of(h * rows, 16), cap)
             dq_ref[:, h * HEAD : (h + 1) * HEAD] = jnp.where(live, dq_s[at, :], zero)
@@ -394,10 +397,10 @@
             pltpu.VMEM((queries, HEAD), bf),
             pltpu.VMEM((queries, HEAD), bf),
             pltpu.VMEM((queries, 2 * HEAD), bf),
-            pltpu.VMEM((keys, QT), f32),
-            pltpu.VMEM((keys, QT), f32),
-            pltpu.VMEM((cap, QT), f32),
-            pltpu.VMEM((cap, QT), f32),
+            pltpu.VMEM((keys, WIDE), f32),
+            pltpu.VMEM((keys, WIDE), f32),
+            pltpu.VMEM((cap, WIDE), f32),
+            pltpu.VMEM((cap, WIDE), f32),
             pltpu.VMEM((queries, HEAD), bf),
             pltpu.VMEM((keys, HEAD), f32),
             pltpu.VMEM((keys, HEAD), f32),

time: 167 us -> 166 us (level)
  starting transfers between devices: 55.6 us -> 51.5 us
  waiting for transfers between devices: 48.6 us -> 51.8 us
    ppermute x1, waiting for transfers between devices: 1.44 us -> 4.19 us  [shards(): dq_back = lax.ppermute(dq_far, 'seq', mirror)]
    ppermute x6, waiting for transfers between devices: 22.4 us -> 19.6 us  [shift_y(): return lax.ppermute(array, 'seq', pairs)]
    ppermute x6, starting transfers between devices: 12.2 us -> 9.58 us  [shift_y(): return lax.ppermute(array, 'seq', pairs)]
    ppermute x3, starting transfers between devices: 4.11 us -> 2.16 us  [shift_dp(): lax.ppermute(array, 'dp', [(i, (i + step) % dp_devices) for i in range(dp...]
    ppermute x3, waiting for transfers between devices: 6.56 us -> 8.23 us  [shift_dp(): lax.ppermute(array, 'dp', [(i, (i + step) % dp_devices) for i in range(dp...]
  transfers between devices with their start and end apart: 29 -> 29, of which waited for: 16 -> 16; matrix products, arithmetic and copies ran while one was open for 7% -> 7% of each run, Pallas kernels for 21% -> 20%
where the time goes in v2:
time: 166 us; the launch traced here: 164 us
  waiting for transfers between devices  51.8 us (31%)
  starting transfers between devices  51.5 us (31%)
  Pallas kernels  44 us (27%)
  local copies, waits for them, and re-layouts  12.2 us (7%)
  other arithmetic  3.26 us (2%)
    ppermute x6, waiting for transfers between devices, shift_y(): return lax.ppermute(array, 'seq', pairs)  19.6 us
    pallas_call x1, Pallas kernels, attention_backward(): pl.pallas_call(attention_kernel, out_shape=[jax.ShapeDtypeStruct((cap, wi...  15.3 us
    ppermute x4, waiting for transfers between devices, shards(): received.append(lax.ppermute(products[step], ('dp', 'rep'), pairs))  9.84 us
    ppermute x4, starting transfers between devices, shards(): received.append(lax.ppermute(products[step], ('dp', 'rep'), pairs))  9.61 us
    ppermute x6, starting transfers between devices, shift_y(): return lax.ppermute(array, 'seq', pairs)  9.58 us
    ppermute x6, starting transfers between devices, shift_x(): return lax.ppermute(array, 'seq', pairs)  8.46 us
    ppermute x3, waiting for transfers between devices, shift_dp(): lax.ppermute(array, 'dp', [(i, (i + step) % dp_devices) for i in range(dp...  8.23 us
    pallas_call x2, Pallas kernels, spread_rows(): pl.pallas_call(spread_kernel, grid_spec=pltpu.PrefetchScalarGridSpec(num_...  7.35 us
  transfers between devices with their start and end apart: 29, of which 16 were waited for; matrix products, arithmetic and copies ran while one was open for 7% of the time, Pallas kernels for 20%

profile of v2, /device:TPU:1, one launch (start us, length us, event | category | flops | bytes accessed | tf_op | source)
XLA Modules:
  0.0 163.7 jit_solution(3834343678800137913)
XLA Ops:
  0.8 0.9 fusion
  1.7 2.1 %collective-permute-start = (bf16[192,256]{1,0:T(8,128)(2,1)S(1)}, bf16[192,256]{1,0:T(8,128)(2,1)S(1)}, u32[]{:S(2)}, u32[]{:S(2)}) collective-permute-start(bf16[192,256]{1,0:T(8,128)(2,1)S(1)} %get-tuple-element.118), channel_id=1, source_target_pairs={{0,32},{8,40},{16,48},{24,56},{32,64},{40,72},{48,80},{56,88},{64,... | collective-permute-start | bytes 294920 | tf_op jit(solution)/shard_map/ppermute | solution.py:485
  3.8 2.5 %collective-permute-start.1 = (bf16[192,256]{1,0:T(8,128)(2,1)S(1)}, bf16[192,256]{1,0:T(8,128)(2,1)S(1)}, u32[]{:S(2)}, u32[]{:S(2)}) collective-permute-start(bf16[192,256]{1,0:T(8,128)(2,1)S(1)} %get-tuple-element.119), channel_id=1, source_target_pairs={{0,64},{8,72},{16,80},{24,88},{32,96},{40,104},{48,112},{56,120},{... | collective-permute-start | bytes 294920 | tf_op jit(solution)/shard_map/ppermute | solution.py:485
  6.3 1.2 collective-permute-start.2
  7.5 1.2 constant_dynamic-slice_fusion
  8.8 1.2 dynamic-slice_bitcast_fusion.2
  10.4 2.9 %collective-permute-start.6 = (bf16[768,256]{1,0:T(8,128)(2,1)S(1)}, bf16[768,256]{1,0:T(8,128)(2,1)S(1)}, u32[]{:S(2)}, u32[]{:S(2)}) collective-permute-start(bf16[768,256]{1,0:T(8,128)(2,1)S(1)} %pad_maximum_fusion.2.kv0), channel_id=1, source_target_pairs={{0,24},{8,0},{16,8},{24,16},{32,56},{40,32},{48,40},{56,48},{64,88... | collective-permute-start | bytes 1179656 | tf_op jit(solution)/shard_map/ppermute | solution.py:489
  14.2 1.2 compare_select_fusion
  15.5 2.4 %collective-permute-start.3 = (bf16[192,2048]{1,0:T(8,128)(2,1)S(1)}, bf16[192,2048]{1,0:T(8,128)(2,1)S(1)}, u32[]{:S(2)}, u32[]{:S(2)}) collective-permute-start(bf16[192,2048]{1,0:T(8,128)(2,1)S(1)} %pad_maximum_fusion), channel_id=1, source_target_pairs={{0,96},{8,104},{16,112},{24,120},{32,64},{40,72},{48,80},{56,88},{... | collective-permute-start | bytes 2359304 | tf_op jit(solution)/shard_map/ppermute | solution.py:512
  19.3 5.6 %gather_columns.1 = bf16[4,192,1024]{2,1,0:T(8,128)(2,1)} custom-call(s32[6]{0:T(128)} %stack.45.place, s32[192,1]{1,0:T(8,128)} %copy.12.rows_ref, bf16[512,8192]{1,0:T(8,128)(2,1)} %bitcast.34), custom_call_target="tpu_custom_call" | custom-call | flops 800000000 | bytes 6000000 | tf_op jit(solution)/shard_map/gather_columns/pallas_call | solution.py:46
  24.9 9.3 %collective-permute-done.4.kv1 = bf16[768,256]{1,0:T(8,128)(2,1)S(1)} collective-permute-done((bf16[768,256]{1,0:T(8,128)(2,1)S(1)}, bf16[768,256]{1,0:T(8,128)(2,1)S(1)}, u32[]{:S(2)}, u32[]{:S(2)}) %collective-permute-start.4) | collective-permute-done | bytes 393248 | tf_op jit(solution)/shard_map/ppermute | solution.py:489
  34.2 5.0 %all-to-all-start = ((bf16[4,192,1024]{2,1,0:T(8,128)(2,1)}), bf16[4,192,1024]{2,1,0:T(8,128)(2,1)}, u32[]{:S(2)}, u32[]{:S(2)}) async-start(bf16[4,192,1024]{2,1,0:T(8,128)(2,1)} %gather_columns.1), calls=%async_computation | async-start | bytes 3145728 | tf_op jit(solution)/shard_map/all_to_all | solution.py:520
  40.1 15.3 %attention_backward.1 = (bf16[192,1024]{1,0:T(8,128)(2,1)}, bf16[192,1024]{1,0:T(8,128)(2,1)}, bf16[768,256]{1,0:T(8,128)(2,1)}, bf16[768,256]{1,0:T(8,128)(2,1)...) custom-call(s32[16]{0:T(128)} %bitcast.43, s32[6]{0:T(128)} %stack.45.place, bf16[192,2048]{1,0:T(8,128)(2,1)} %bitcast.36, ...), custom_call_target="tpu_custom_call" | custom-call | flops 6000000000 | bytes 6000000 | tf_op jit(solution)/shard_map/attention_backward/pallas_call | solution.py:387
  55.4 3.9 %all-to-all-done.own_ref = bf16[4,192,1024]{2,1,0:T(8,128)(2,1)} async-done(((bf16[4,192,1024]{2,1,0:T(8,128)(2,1)}), bf16[4,192,1024]{2,1,0:T(8,128)(2,1)}, u32[]{:S(2)}, u32[]{:S(2)}) %all-to-all-start) | async-done | bytes 1572896 | tf_op jit(solution)/shard_map/all_to_all | solution.py:520
  59.3 1.7 %collective-permute-start.10 = (bf16[4,192,1024]{2,1,0:T(8,128)(2,1)}, bf16[4,192,1024]{2,1,0:T(8,128)(2,1)}, u32[]{:S(2)}, u32[]{:S(2)}) collective-permute-start(bf16[4,192,1024]{2,1,0:T(8,128)(2,1)} %all-to-all-done.own_ref), channel_id=1, source_target_pairs={{0,1},{1,0},{2,3},{3,2},{4,5},{5,4},{6,7},{7,6},{8,9},{9,8},{10,11... | collective-permute-start | bytes 4718600 | tf_op jit(solution)/shard_map/ppermute | solution.py:526
  61.0 2.4 %collective-permute-start.11 = (bf16[192,1024]{1,0:T(8,128)(2,1)}, bf16[192,1024]{1,0:T(8,128)(2,1)S(1)}, u32[]{:S(2)}, u32[]{:S(2)}) collective-permute-start(bf16[192,1024]{1,0:T(8,128)(2,1)} %get-tuple-element.76), channel_id=1, source_target_pairs={{0,96},{8,104},{16,112},{24,120},{32,64},{40,72},{48,80},{56,88},{... | collective-permute-start | bytes 1179656 | tf_op jit(solution)/shard_map/ppermute | solution.py:525
  63.4 4.5 %collective-permute-start.9 = (bf16[768,256]{1,0:T(8,128)(2,1)}, bf16[768,256]{1,0:T(8,128)(2,1)}, u32[]{:S(2)}, u32[]{:S(2)}) collective-permute-start(bf16[768,256]{1,0:T(8,128)(2,1)} %get-tuple-element.74), channel_id=1, source_target_pairs={{0,24},{8,0},{16,8},{24,16},{32,56},{40,32},{48,40},{56,48},{64,88... | collective-permute-start | bytes 1179656 | tf_op jit(solution)/shard_map/ppermute | solution.py:489
  67.9 1.2 collective-permute-start.8
  69.1 4.2 %collective-permute-done.11 = bf16[192,1024]{1,0:T(8,128)(2,1)S(1)} collective-permute-done((bf16[192,1024]{1,0:T(8,128)(2,1)}, bf16[192,1024]{1,0:T(8,128)(2,1)S(1)}, u32[]{:S(2)}, u32[]{:S(2)}) %collective-permute-start.11) | collective-permute-done | bytes 393248 | tf_op jit(solution)/shard_map/ppermute | solution.py:525
  73.3 3.2 %reshape.22 = bf16[2,1024,512]{2,1,0:T(8,128)(2,1)S(1)} reshape(bf16[2048,2,256]{2,1,0:T(2,128)(2,1)} %param.15) | data formatting | bytes 4194304 | tf_op jit(solution)/shard_map/reshape | solution.py:528
  76.5 1.1 dynamic-slice_bitcast_fusion
  77.6 7.2 %collective-permute-done.9.refs_3_ = bf16[768,256]{1,0:T(8,128)(2,1)} collective-permute-done((bf16[768,256]{1,0:T(8,128)(2,1)}, bf16[768,256]{1,0:T(8,128)(2,1)}, u32[]{:S(2)}, u32[]{:S(2)}) %collective-permute-start.9) | collective-permute-done | bytes 393248 | tf_op jit(solution)/shard_map/ppermute | solution.py:489
  84.8 3.1 %collective-permute-done.7.refs_1_ = bf16[768,256]{1,0:T(8,128)(2,1)} collective-permute-done((bf16[768,256]{1,0:T(8,128)(2,1)}, bf16[768,256]{1,0:T(8,128)(2,1)}, u32[]{:S(2)}, u32[]{:S(2)}) %collective-permute-start.7) | collective-permute-done | bytes 393248 | tf_op jit(solution)/shard_map/ppermute | solution.py:489
  87.9 2.2 %y_sum.1 = (bf16[192,256]{1,0:T(8,128)(2,1)}, bf16[192,256]{1,0:T(8,128)(2,1)}, bf16[192,256]{1,0:T(8,128)(2,1)}, bf16[192,256]{1,0:T(8,128)(2,1)}) custom-call(s32[6]{0:T(128)} %stack.45.place, bf16[768,256]{1,0:T(8,128)(2,1)} %get-tuple-element.71.refs_0_, bf16[768,256]{1,0:T(8,128)(2,1)} %collective-permute-done.7.refs_1_, ...), custom_call_target="tpu_custom_call" | custom-call | flops 1000000 | bytes 2000000 | tf_op jit(solution)/shard_map/y_sum/pallas_call | solution.py:80
  90.1 1.5 collective-permute-start.15
  91.7 1.5 collective-permute-start.13
  93.1 1.2 collective-permute-start.14
  94.3 5.3 %collective-permute-done.12.refs_1_ = bf16[192,256]{1,0:T(8,128)(2,1)S(1)} collective-permute-done((bf16[192,256]{1,0:T(8,128)(2,1)}, bf16[192,256]{1,0:T(8,128)(2,1)S(1)}, u32[]{:S(2)}, u32[]{:S(2)}) %collective-permute-start.12) | collective-permute-done | bytes 98336 | tf_op jit(solution)/shard_map/ppermute | solution.py:485
  100.5 2.2 %x_sum.1.refs_0_ = bf16[192,512]{1,0:T(8,128)(2,1)} custom-call(s32[6]{0:T(128)} %stack.45.place, bf16[192,256]{1,0:T(8,128)(2,1)} %get-tuple-element.90.refs_0_, bf16[192,256]{1,0:T(8,128)(2,1)} %copy-done.9, bf16[192,256]{1,0:T(8,128)(2,1)} %copy-done.10, bf16[192,256]{1,0:T(8,128)(2,1)} %copy-done.11), custom_call_target="tpu_custom_call" | custom-call | flops 1000000 | bytes 1000000 | tf_op jit(solution)/shard_map/x_sum/pallas_call | solution.py:114
  102.7 1.1 collective-permute-start.19
  103.9 1.0 collective-permute-start.18
  106.1 4.4 %collective-permute-done.18.refs_3_ = bf16[192,512]{1,0:T(8,128)(2,1)S(1)} collective-permute-done((bf16[192,512]{1,0:T(8,128)(2,1)}, bf16[192,512]{1,0:T(8,128)(2,1)S(1)}, u32[]{:S(2)}, u32[]{:S(2)}) %collective-permute-start.18) | collective-permute-done | bytes 196640 | tf_op jit(solution)/shard_map/ppermute | solution.py:481
  110.5 1.3 collective-permute-start.22
  111.9 0.9 collective-permute-done.17.refs_2_
  112.7 1.9 %collective-permute-start.21 = (bf16[192,512]{1,0:T(8,128)(2,1)S(1)}, bf16[192,512]{1,0:T(8,128)(2,1)S(1)}, u32[]{:S(2)}, u32[]{:S(2)}) collective-permute-start(bf16[192,512]{1,0:T(8,128)(2,1)S(1)} %collective-permute-done.17.refs_2_), channel_id=1, source_target_pairs={{0,1},{1,0},{2,3},{3,2},{4,5},{5,4},{6,7},{7,6},{8,9},{9,8},{10,11... | collective-permute-start | bytes 589832 | tf_op jit(solution)/shard_map/ppermute | solution.py:546
  114.7 2.9 %collective-permute-done.16.refs_1_ = bf16[192,512]{1,0:T(8,128)(2,1)S(1)} collective-permute-done((bf16[192,512]{1,0:T(8,128)(2,1)}, bf16[192,512]{1,0:T(8,128)(2,1)S(1)}, u32[]{:S(2)}, u32[]{:S(2)}) %collective-permute-start.16) | collective-permute-done | bytes 196640 | tf_op jit(solution)/shard_map/ppermute | solution.py:481
  118.1 0.9 pad_maximum_fusion.1
  119.3 6.1 %weight_terms.1 = bf16[2048,512]{1,0:T(8,128)(2,1)} custom-call(s32[6]{0:T(128)} %stack.45.place, bf16[4,192,1024]{2,1,0:T(8,128)(2,1)} %all-to-all-done.own_ref, bf16[4,192,1024]{2,1,0:T(8,128)(2,1)} %collective-permute-done.10.other_ref, bf16[192,512]{1,0:T(8,128)(2,1)} %x_sum.1.refs_0_, bf16[192,512]{1,0:T(8,128)(2,1)} %copy-done.8, ...), custom_call_target="tpu_custom_call" | custom-call | flops 1600000000 | bytes 6000000 | tf_op jit(solution)/shard_map/weight_terms/pallas_call | solution.py:156
  125.4 3.7 %all-to-all-start.1 = ((bf16[16,128,512]{2,1,0:T(8,128)(2,1)}), bf16[16,128,512]{2,1,0:T(8,128)(2,1)S(1)}, u32[]{:S(2)}, u32[]{:S(2)}) async-start(bf16[16,128,512]{2,1,0:T(8,128)(2,1)} %bitcast.33), calls=%async_computation.1 | async-start | bytes 4194304 | tf_op jit(solution)/shard_map/all_to_all | solution.py:550
  129.2 5.2 %input_products.1 = (bf16[192,1024]{1,0:T(8,128)(2,1)}, bf16[192,1024]{1,0:T(8,128)(2,1)}, bf16[192,1024]{1,0:T(8,128)(2,1)}, bf16[192,1024]{1,0:T(8,128)(2,1)}) custom-call(s32[6]{0:T(128)} %stack.45.place, bf16[192,512]{1,0:T(8,128)(2,1)} %x_sum.1.refs_0_, bf16[192,512]{1,0:T(8,128)(2,1)} %copy-done.8, bf16[192,512]{1,0:T(8,128)(2,1)} %copy-done.7, ...), custom_call_target="tpu_custom_call" | custom-call | flops 1600000000 | bytes 6000000 | tf_op jit(solution)/shard_map/input_products/pallas_call | solution.py:209
  134.3 1.9 %collective-permute-start.25 = (bf16[192,1024]{1,0:T(8,128)(2,1)}, bf16[192,1024]{1,0:T(8,128)(2,1)S(1)}, u32[]{:S(2)}, u32[]{:S(2)}) collective-permute-start(bf16[192,1024]{1,0:T(8,128)(2,1)} %get-tuple-element.110), channel_id=1, source_target_pairs={{0,0},{1,2},{2,4},{3,6},{4,1},{5,3},{6,5},{7,7},{8,8},{9,10},{10,1... | collective-permute-start | bytes 1179656 | tf_op jit(solution)/shard_map/ppermute | solution.py:564
  136.2 2.0 %collective-permute-start.26 = (bf16[192,1024]{1,0:T(8,128)(2,1)}, bf16[192,1024]{1,0:T(8,128)(2,1)}, u32[]{:S(2)}, u32[]{:S(2)}) collective-permute-start(bf16[192,1024]{1,0:T(8,128)(2,1)} %get-tuple-element.111), channel_id=1, source_target_pairs={{0,6},{1,0},{2,2},{3,4},{4,7},{5,1},{6,3},{7,5},{8,14},{9,8},{10,1... | collective-permute-start | bytes 1179656 | tf_op jit(solution)/shard_map/ppermute | solution.py:564
  138.2 5.1 %collective-permute-start.23 = (bf16[192,1024]{1,0:T(8,128)(2,1)}, bf16[192,1024]{1,0:T(8,128)(2,1)S(1)}, u32[]{:S(2)}, u32[]{:S(2)}) collective-permute-start(bf16[192,1024]{1,0:T(8,128)(2,1)} %get-tuple-element.108), channel_id=1, source_target_pairs={{0,2},{1,4},{2,6},{3,0},{4,3},{5,5},{6,7},{7,1},{8,10},{9,12},{10,... | collective-permute-start | bytes 1179656 | tf_op jit(solution)/shard_map/ppermute | solution.py:564
  144.5 3.7 %collective-permute-done.25.refs_0_ = bf16[192,1024]{1,0:T(8,128)(2,1)S(1)} collective-permute-done((bf16[192,1024]{1,0:T(8,128)(2,1)}, bf16[192,1024]{1,0:T(8,128)(2,1)S(1)}, u32[]{:S(2)}, u32[]{:S(2)}) %collective-permute-start.25) | collective-permute-done | bytes 393248 | tf_op jit(solution)/shard_map/ppermute | solution.py:564
  148.3 2.8 %collective-permute-done.26.refs_1_ = bf16[192,1024]{1,0:T(8,128)(2,1)} collective-permute-done((bf16[192,1024]{1,0:T(8,128)(2,1)}, bf16[192,1024]{1,0:T(8,128)(2,1)}, u32[]{:S(2)}, u32[]{:S(2)}) %collective-permute-start.26) | collective-permute-done | bytes 393248 | tf_op jit(solution)/shard_map/ppermute | solution.py:564
  151.1 3.7 %spread_rows.2.refs_2_ = bf16[512,4096]{1,0:T(8,128)(2,1)} custom-call(s32[2]{0:T(128)} %get-tuple-element.125.order, s32[1,192]{1,0:T(1,128)} %bitcast.40, bf16[192,1024]{1,0:T(8,128)(2,1)} %copy-done.3, bf16[192,1024]{1,0:T(8,128)(2,1)} %collective-permute-done.26.refs_1_), custom_call_target="tpu_custom_call" | custom-call | flops 400000000 | bytes 3000000 | tf_op jit(solution)/shard_map/spread_rows/pallas_call | solution.py:438
  154.8 3.2 %collective-permute-done.23.refs_0_ = bf16[192,1024]{1,0:T(8,128)(2,1)S(1)} collective-permute-done((bf16[192,1024]{1,0:T(8,128)(2,1)}, bf16[192,1024]{1,0:T(8,128)(2,1)S(1)}, u32[]{:S(2)}, u32[]{:S(2)}) %collective-permute-start.23) | collective-permute-done | bytes 393248 | tf_op jit(solution)/shard_map/ppermute | solution.py:564
  158.9 3.7 %spread_rows.3 = bf16[512,4096]{1,0:T(8,128)(2,1)} custom-call(s32[2]{0:T(128)} %get-tuple-element.124.order, s32[1,192]{1,0:T(1,128)} %bitcast.41, bf16[192,1024]{1,0:T(8,128)(2,1)} %copy-done.1, bf16[192,1024]{1,0:T(8,128)(2,1)} %copy-done.2, bf16[512,4096]{1,0:T(8,128)(2,1)} %spread_rows.2.refs_2_), custom_call_target="tpu_custom_call", output_to_operand_aliasing={{}: (4, {})} | custom-call | flops 400000000 | bytes 3000000 | tf_op jit(solution)/shard_map/spread_rows/pallas_call | solution.py:438
  (77 shorter events, 10.0 us)
Async XLA Ops:
  0.6 9.4 %copy-start = (s32[1,16,192]{2,1,0:T(8,128)S(1)}, s32[1,16,192]{2,1,0:T(8,128)}, u32[]{:S(2)}) copy-start(s32[1,16,192]{2,1,0:T(8,128)} %param.9) | copy-start | bytes 36868
  1.7 8.3 %collective-permute-start = (bf16[192,256]{1,0:T(8,128)(2,1)S(1)}, bf16[192,256]{1,0:T(8,128)(2,1)S(1)}, u32[]{:S(2)}, u32[]{:S(2)}) collective-permute-start(bf16[192,256]{1,0:T(8,128)(2,1)S(1)} %get-tuple-element.118), channel_id=1, source_target_pairs={{0,32},{8,40},{16,48},{24,56},{32,64},{40,72},{48,80},{56,88},{64,... | collective-permute-start | bytes 294920 | tf_op jit(solution)/shard_map/ppermute | solution.py:485
  3.8 6.5 %collective-permute-start.1 = (bf16[192,256]{1,0:T(8,128)(2,1)S(1)}, bf16[192,256]{1,0:T(8,128)(2,1)S(1)}, u32[]{:S(2)}, u32[]{:S(2)}) collective-permute-start(bf16[192,256]{1,0:T(8,128)(2,1)S(1)} %get-tuple-element.119), channel_id=1, source_target_pairs={{0,64},{8,72},{16,80},{24,88},{32,96},{40,104},{48,112},{56,120},{... | collective-permute-start | bytes 294920 | tf_op jit(solution)/shard_map/ppermute | solution.py:485
  6.3 4.0 %collective-permute-start.2 = (bf16[192,256]{1,0:T(8,128)(2,1)S(1)}, bf16[192,256]{1,0:T(8,128)(2,1)S(1)}, u32[]{:S(2)}, u32[]{:S(2)}) collective-permute-start(bf16[192,256]{1,0:T(8,128)(2,1)S(1)} %broadcast_select_fusion.2), channel_id=1, source_target_pairs={{0,96},{8,104},{16,112},{24,120},{32,0},{40,8},{48,16},{56,24},{64... | collective-permute-start | bytes 294920 | tf_op jit(solution)/shard_map/ppermute | solution.py:485
  10.3 14.5 %copy-start.4 = (bf16[768,256]{1,0:T(8,128)(2,1)}, bf16[768,256]{1,0:T(8,128)(2,1)S(1)}, u32[]{:S(2)}) copy-start(bf16[768,256]{1,0:T(8,128)(2,1)S(1)} %pad_maximum_fusion.2.kv0) | copy-start | bytes 1179652
  10.4 14.5 %collective-permute-start.6 = (bf16[768,256]{1,0:T(8,128)(2,1)S(1)}, bf16[768,256]{1,0:T(8,128)(2,1)S(1)}, u32[]{:S(2)}, u32[]{:S(2)}) collective-permute-start(bf16[768,256]{1,0:T(8,128)(2,1)S(1)} %pad_maximum_fusion.2.kv0), channel_id=1, source_target_pairs={{0,24},{8,0},{16,8},{24,16},{32,56},{40,32},{48,40},{56,48},{64,88... | collective-permute-start | bytes 1179656 | tf_op jit(solution)/shard_map/ppermute | solution.py:489
  13.2 11.6 %collective-permute-start.5 = (bf16[768,256]{1,0:T(8,128)(2,1)S(1)}, bf16[768,256]{1,0:T(8,128)(2,1)S(1)}, u32[]{:S(2)}, u32[]{:S(2)}) collective-permute-start(bf16[768,256]{1,0:T(8,128)(2,1)S(1)} %pad_maximum_fusion.2.kv0), channel_id=1, source_target_pairs={{0,16},{8,24},{16,0},{24,8},{32,48},{40,56},{48,32},{56,40},{64,80... | collective-permute-start | bytes 1179656 | tf_op jit(solution)/shard_map/ppermute | solution.py:489
  13.6 20.6 %collective-permute-start.4 = (bf16[768,256]{1,0:T(8,128)(2,1)S(1)}, bf16[768,256]{1,0:T(8,128)(2,1)S(1)}, u32[]{:S(2)}, u32[]{:S(2)}) collective-permute-start(bf16[768,256]{1,0:T(8,128)(2,1)S(1)} %pad_maximum_fusion.2.kv0), channel_id=1, source_target_pairs={{0,8},{8,16},{16,24},{24,0},{32,40},{40,48},{48,56},{56,32},{64,72... | collective-permute-start | bytes 1179656 | tf_op jit(solution)/shard_map/ppermute | solution.py:489
  15.5 23.7 %collective-permute-start.3 = (bf16[192,2048]{1,0:T(8,128)(2,1)S(1)}, bf16[192,2048]{1,0:T(8,128)(2,1)S(1)}, u32[]{:S(2)}, u32[]{:S(2)}) collective-permute-start(bf16[192,2048]{1,0:T(8,128)(2,1)S(1)} %pad_maximum_fusion), channel_id=1, source_target_pairs={{0,96},{8,104},{16,112},{24,120},{32,64},{40,72},{48,80},{56,88},{... | collective-permute-start | bytes 2359304 | tf_op jit(solution)/shard_map/ppermute | solution.py:512
  24.8 14.4 %copy-start.14 = (bf16[768,256]{1,0:T(8,128)(2,1)}, bf16[768,256]{1,0:T(8,128)(2,1)S(1)}, u32[]{:S(2)}) copy-start(bf16[768,256]{1,0:T(8,128)(2,1)S(1)} %collective-permute-done.6.kv3) | copy-start | bytes 1179652
  24.8 14.4 %copy-start.15 = (bf16[768,256]{1,0:T(8,128)(2,1)}, bf16[768,256]{1,0:T(8,128)(2,1)S(1)}, u32[]{:S(2)}) copy-start(bf16[768,256]{1,0:T(8,128)(2,1)S(1)} %collective-permute-done.5.kv2) | copy-start | bytes 1179652
  34.2 5.1 %copy-start.16 = (bf16[768,256]{1,0:T(8,128)(2,1)}, bf16[768,256]{1,0:T(8,128)(2,1)S(1)}, u32[]{:S(2)}) copy-start(bf16[768,256]{1,0:T(8,128)(2,1)S(1)} %collective-permute-done.4.kv1) | copy-start | bytes 1179652
  34.2 25.2 %all-to-all-start = ((bf16[4,192,1024]{2,1,0:T(8,128)(2,1)}), bf16[4,192,1024]{2,1,0:T(8,128)(2,1)}, u32[]{:S(2)}, u32[]{:S(2)}) async-start(bf16[4,192,1024]{2,1,0:T(8,128)(2,1)} %gather_columns.1), calls=%async_computation | async-start | bytes 3145728 | tf_op jit(solution)/shard_map/all_to_all | solution.py:520
  39.2 0.9 copy-start.13
  59.3 25.5 %collective-permute-start.10 = (bf16[4,192,1024]{2,1,0:T(8,128)(2,1)}, bf16[4,192,1024]{2,1,0:T(8,128)(2,1)}, u32[]{:S(2)}, u32[]{:S(2)}) collective-permute-start(bf16[4,192,1024]{2,1,0:T(8,128)(2,1)} %all-to-all-done.own_ref), channel_id=1, source_target_pairs={{0,1},{1,0},{2,3},{3,2},{4,5},{5,4},{6,7},{7,6},{8,9},{9,8},{10,11... | collective-permute-start | bytes 4718600 | tf_op jit(solution)/shard_map/ppermute | solution.py:526
  61.0 12.3 %collective-permute-start.11 = (bf16[192,1024]{1,0:T(8,128)(2,1)}, bf16[192,1024]{1,0:T(8,128)(2,1)S(1)}, u32[]{:S(2)}, u32[]{:S(2)}) collective-permute-start(bf16[192,1024]{1,0:T(8,128)(2,1)} %get-tuple-element.76), channel_id=1, source_target_pairs={{0,96},{8,104},{16,112},{24,120},{32,64},{40,72},{48,80},{56,88},{... | collective-permute-start | bytes 1179656 | tf_op jit(solution)/shard_map/ppermute | solution.py:525
  63.4 21.4 %collective-permute-start.9 = (bf16[768,256]{1,0:T(8,128)(2,1)}, bf16[768,256]{1,0:T(8,128)(2,1)}, u32[]{:S(2)}, u32[]{:S(2)}) collective-permute-start(bf16[768,256]{1,0:T(8,128)(2,1)} %get-tuple-element.74), channel_id=1, source_target_pairs={{0,24},{8,0},{16,8},{24,16},{32,56},{40,32},{48,40},{56,48},{64,88... | collective-permute-start | bytes 1179656 | tf_op jit(solution)/shard_map/ppermute | solution.py:489
  67.9 20.0 %collective-permute-start.7 = (bf16[768,256]{1,0:T(8,128)(2,1)}, bf16[768,256]{1,0:T(8,128)(2,1)}, u32[]{:S(2)}, u32[]{:S(2)}) collective-permute-start(bf16[768,256]{1,0:T(8,128)(2,1)} %get-tuple-element.72), channel_id=1, source_target_pairs={{0,8},{8,16},{16,24},{24,0},{32,40},{40,48},{48,56},{56,32},{64,72... | collective-permute-start | bytes 1179656 | tf_op jit(solution)/shard_map/ppermute | solution.py:489
  67.9 20.0 %collective-permute-start.8 = (bf16[768,256]{1,0:T(8,128)(2,1)}, bf16[768,256]{1,0:T(8,128)(2,1)}, u32[]{:S(2)}, u32[]{:S(2)}) collective-permute-start(bf16[768,256]{1,0:T(8,128)(2,1)} %get-tuple-element.73), channel_id=1, source_target_pairs={{0,16},{8,24},{16,0},{24,8},{32,48},{40,56},{48,32},{56,40},{64,80... | collective-permute-start | bytes 1179656 | tf_op jit(solution)/shard_map/ppermute | solution.py:489
  77.6 28.4 %copy-start.5 = (bf16[192,1024]{1,0:T(8,128)(2,1)S(1)}, bf16[192,1024]{1,0:T(8,128)(2,1)}, u32[]{:S(2)}) copy-start(bf16[192,1024]{1,0:T(8,128)(2,1)} %get-tuple-element.94) | copy-start | bytes 1179652
  90.1 9.7 %collective-permute-start.15 = (bf16[1024,512]{1,0:T(8,128)(2,1)S(1)}, bf16[1024,512]{1,0:T(8,128)(2,1)S(1)}, u32[]{:S(2)}, u32[]{:S(2)}) collective-permute-start(bf16[1024,512]{1,0:T(8,128)(2,1)S(1)} %get-tuple-element.89), channel_id=1, source_target_pairs={{0,1},{1,0},{2,3},{3,2},{4,5},{5,4},{6,7},{7,6},{8,9},{9,8},{10,11... | collective-permute-start | bytes 3145736 | tf_op jit(solution)/shard_map/ppermute | solution.py:537
  91.7 7.9 %collective-permute-start.12 = (bf16[192,256]{1,0:T(8,128)(2,1)}, bf16[192,256]{1,0:T(8,128)(2,1)S(1)}, u32[]{:S(2)}, u32[]{:S(2)}) collective-permute-start(bf16[192,256]{1,0:T(8,128)(2,1)} %get-tuple-element.85), channel_id=1, source_target_pairs={{0,32},{8,40},{16,48},{24,56},{32,64},{40,72},{48,80},{56,88},{64,... | collective-permute-start | bytes 294920 | tf_op jit(solution)/shard_map/ppermute | solution.py:485
  91.7 7.9 %collective-permute-start.13 = (bf16[192,256]{1,0:T(8,128)(2,1)}, bf16[192,256]{1,0:T(8,128)(2,1)S(1)}, u32[]{:S(2)}, u32[]{:S(2)}) collective-permute-start(bf16[192,256]{1,0:T(8,128)(2,1)} %get-tuple-element.86), channel_id=1, source_target_pairs={{0,64},{8,72},{16,80},{24,88},{32,96},{40,104},{48,112},{56,120},{... | collective-permute-start | bytes 294920 | tf_op jit(solution)/shard_map/ppermute | solution.py:485
  93.1 6.8 %collective-permute-start.14 = (bf16[192,256]{1,0:T(8,128)(2,1)}, bf16[192,256]{1,0:T(8,128)(2,1)S(1)}, u32[]{:S(2)}, u32[]{:S(2)}) collective-permute-start(bf16[192,256]{1,0:T(8,128)(2,1)} %get-tuple-element.87), channel_id=1, source_target_pairs={{0,96},{8,104},{16,112},{24,120},{32,0},{40,8},{48,16},{56,24},{64... | collective-permute-start | bytes 294920 | tf_op jit(solution)/shard_map/ppermute | solution.py:485
  99.6 0.7 copy-start.10
  99.9 0.6 copy-start.11
  100.5 2.2 %copy-start.12 = (bf16[1024,512]{1,0:T(8,128)(2,1)}, bf16[1024,512]{1,0:T(8,128)(2,1)S(1)}, u32[]{:S(2)}) copy-start(bf16[1024,512]{1,0:T(8,128)(2,1)S(1)} %collective-permute-done.15.refs_9_) | copy-start | bytes 3145732
  102.7 16.3 %collective-permute-start.19 = (bf16[192,512]{1,0:T(8,128)(2,1)}, bf16[192,512]{1,0:T(8,128)(2,1)S(1)}, u32[]{:S(2)}, u32[]{:S(2)}) collective-permute-start(bf16[192,512]{1,0:T(8,128)(2,1)} %x_sum.1.refs_0_), channel_id=1, source_target_pairs={{0,1},{1,0},{2,3},{3,2},{4,5},{5,4},{6,7},{7,6},{8,9},{9,8},{10,11... | collective-permute-start | bytes 589832 | tf_op jit(solution)/shard_map/ppermute | solution.py:546
  103.9 6.7 %collective-permute-start.18 = (bf16[192,512]{1,0:T(8,128)(2,1)}, bf16[192,512]{1,0:T(8,128)(2,1)S(1)}, u32[]{:S(2)}, u32[]{:S(2)}) collective-permute-start(bf16[192,512]{1,0:T(8,128)(2,1)} %x_sum.1.refs_0_), channel_id=1, source_target_pairs={{0,6},{2,0},{4,2},{6,4},{1,7},{3,1},{5,3},{7,5},{8,14},{10,8},{12,... | collective-permute-start | bytes 589832 | tf_op jit(solution)/shard_map/ppermute | solution.py:481
  104.8 7.9 %collective-permute-start.17 = (bf16[192,512]{1,0:T(8,128)(2,1)}, bf16[192,512]{1,0:T(8,128)(2,1)S(1)}, u32[]{:S(2)}, u32[]{:S(2)}) collective-permute-start(bf16[192,512]{1,0:T(8,128)(2,1)} %x_sum.1.refs_0_), channel_id=1, source_target_pairs={{0,4},{2,6},{4,0},{6,2},{1,5},{3,7},{5,1},{7,3},{8,12},{10,14},{12... | collective-permute-start | bytes 589832 | tf_op jit(solution)/shard_map/ppermute | solution.py:481
  105.4 12.2 %collective-permute-start.16 = (bf16[192,512]{1,0:T(8,128)(2,1)}, bf16[192,512]{1,0:T(8,128)(2,1)S(1)}, u32[]{:S(2)}, u32[]{:S(2)}) collective-permute-start(bf16[192,512]{1,0:T(8,128)(2,1)} %x_sum.1.refs_0_), channel_id=1, source_target_pairs={{0,2},{2,4},{4,6},{6,0},{1,3},{3,5},{5,7},{7,1},{8,10},{10,12},{12... | collective-permute-start | bytes 589832 | tf_op jit(solution)/shard_map/ppermute | solution.py:481
  110.5 8.8 %copy-start.6 = (bf16[192,512]{1,0:T(8,128)(2,1)}, bf16[192,512]{1,0:T(8,128)(2,1)S(1)}, u32[]{:S(2)}) copy-start(bf16[192,512]{1,0:T(8,128)(2,1)S(1)} %collective-permute-done.18.refs_3_) | copy-start | bytes 589828
  110.5 8.5 %collective-permute-start.22 = (bf16[192,512]{1,0:T(8,128)(2,1)S(1)}, bf16[192,512]{1,0:T(8,128)(2,1)S(1)}, u32[]{:S(2)}, u32[]{:S(2)}) collective-permute-start(bf16[192,512]{1,0:T(8,128)(2,1)S(1)} %collective-permute-done.18.refs_3_), channel_id=1, source_target_pairs={{0,1},{1,0},{2,3},{3,2},{4,5},{5,4},{6,7},{7,6},{8,9},{9,8},{10,11... | collective-permute-start | bytes 589832 | tf_op jit(solution)/shard_map/ppermute | solution.py:546
  112.7 6.6 %copy-start.7 = (bf16[192,512]{1,0:T(8,128)(2,1)}, bf16[192,512]{1,0:T(8,128)(2,1)S(1)}, u32[]{:S(2)}) copy-start(bf16[192,512]{1,0:T(8,128)(2,1)S(1)} %collective-permute-done.17.refs_2_) | copy-start | bytes 589828
  112.7 6.3 %collective-permute-start.21 = (bf16[192,512]{1,0:T(8,128)(2,1)S(1)}, bf16[192,512]{1,0:T(8,128)(2,1)S(1)}, u32[]{:S(2)}, u32[]{:S(2)}) collective-permute-start(bf16[192,512]{1,0:T(8,128)(2,1)S(1)} %collective-permute-done.17.refs_2_), channel_id=1, source_target_pairs={{0,1},{1,0},{2,3},{3,2},{4,5},{5,4},{6,7},{7,6},{8,9},{9,8},{10,11... | collective-permute-start | bytes 589832 | tf_op jit(solution)/shard_map/ppermute | solution.py:546
  117.6 1.7 %copy-start.8 = (bf16[192,512]{1,0:T(8,128)(2,1)}, bf16[192,512]{1,0:T(8,128)(2,1)S(1)}, u32[]{:S(2)}) copy-start(bf16[192,512]{1,0:T(8,128)(2,1)S(1)} %collective-permute-done.16.refs_1_) | copy-start | bytes 589828
  117.6 1.7 %collective-permute-start.20 = (bf16[192,512]{1,0:T(8,128)(2,1)S(1)}, bf16[192,512]{1,0:T(8,128)(2,1)}, u32[]{:S(2)}, u32[]{:S(2)}) collective-permute-start(bf16[192,512]{1,0:T(8,128)(2,1)S(1)} %collective-permute-done.16.refs_1_), channel_id=1, source_target_pairs={{0,1},{1,0},{2,3},{3,2},{4,5},{5,4},{6,7},{7,6},{8,9},{9,8},{10,11... | collective-permute-start | bytes 589832 | tf_op jit(solution)/shard_map/ppermute | solution.py:546
  119.0 6.4 %copy-start.17 = (bf16[192,512]{1,0:T(8,128)(2,1)}, bf16[192,512]{1,0:T(8,128)(2,1)S(1)}, u32[]{:S(2)}) copy-start(bf16[192,512]{1,0:T(8,128)(2,1)S(1)} %collective-permute-done.19.refs_4_) | copy-start | bytes 589828
  119.0 6.4 %copy-start.18 = (bf16[192,512]{1,0:T(8,128)(2,1)}, bf16[192,512]{1,0:T(8,128)(2,1)S(1)}, u32[]{:S(2)}) copy-start(bf16[192,512]{1,0:T(8,128)(2,1)S(1)} %collective-permute-done.22.refs_7_) | copy-start | bytes 589828
  119.1 6.3 %copy-start.19 = (bf16[192,512]{1,0:T(8,128)(2,1)}, bf16[192,512]{1,0:T(8,128)(2,1)S(1)}, u32[]{:S(2)}) copy-start(bf16[192,512]{1,0:T(8,128)(2,1)S(1)} %collective-permute-done.21.refs_6_) | copy-start | bytes 589828
  125.4 37.1 %all-to-all-start.1 = ((bf16[16,128,512]{2,1,0:T(8,128)(2,1)}), bf16[16,128,512]{2,1,0:T(8,128)(2,1)S(1)}, u32[]{:S(2)}, u32[]{:S(2)}) async-start(bf16[16,128,512]{2,1,0:T(8,128)(2,1)} %bitcast.33), calls=%async_computation.1 | async-start | bytes 4194304 | tf_op jit(solution)/shard_map/all_to_all | solution.py:550
  134.3 13.9 %collective-permute-start.25 = (bf16[192,1024]{1,0:T(8,128)(2,1)}, bf16[192,1024]{1,0:T(8,128)(2,1)S(1)}, u32[]{:S(2)}, u32[]{:S(2)}) collective-permute-start(bf16[192,1024]{1,0:T(8,128)(2,1)} %get-tuple-element.110), channel_id=1, source_target_pairs={{0,0},{1,2},{2,4},{3,6},{4,1},{5,3},{6,5},{7,7},{8,8},{9,10},{10,1... | collective-permute-start | bytes 1179656 | tf_op jit(solution)/shard_map/ppermute | solution.py:564
  136.2 14.8 %collective-permute-start.26 = (bf16[192,1024]{1,0:T(8,128)(2,1)}, bf16[192,1024]{1,0:T(8,128)(2,1)}, u32[]{:S(2)}, u32[]{:S(2)}) collective-permute-start(bf16[192,1024]{1,0:T(8,128)(2,1)} %get-tuple-element.111), channel_id=1, source_target_pairs={{0,6},{1,0},{2,2},{3,4},{4,7},{5,1},{6,3},{7,5},{8,14},{9,8},{10,1... | collective-permute-start | bytes 1179656 | tf_op jit(solution)/shard_map/ppermute | solution.py:564
  138.2 19.7 %collective-permute-start.23 = (bf16[192,1024]{1,0:T(8,128)(2,1)}, bf16[192,1024]{1,0:T(8,128)(2,1)S(1)}, u32[]{:S(2)}, u32[]{:S(2)}) collective-permute-start(bf16[192,1024]{1,0:T(8,128)(2,1)} %get-tuple-element.108), channel_id=1, source_target_pairs={{0,2},{1,4},{2,6},{3,0},{4,3},{5,5},{6,7},{7,1},{8,10},{9,12},{10,... | collective-permute-start | bytes 1179656 | tf_op jit(solution)/shard_map/ppermute | solution.py:564
  143.3 14.7 %collective-permute-start.24 = (bf16[192,1024]{1,0:T(8,128)(2,1)}, bf16[192,1024]{1,0:T(8,128)(2,1)S(1)}, u32[]{:S(2)}, u32[]{:S(2)}) collective-permute-start(bf16[192,1024]{1,0:T(8,128)(2,1)} %get-tuple-element.109), channel_id=1, source_target_pairs={{0,4},{1,6},{2,0},{3,2},{4,5},{5,7},{6,1},{7,3},{8,12},{9,14},{10,... | collective-permute-start | bytes 1179656 | tf_op jit(solution)/shard_map/ppermute | solution.py:564
  148.3 2.8 %copy-start.3 = (bf16[192,1024]{1,0:T(8,128)(2,1)}, bf16[192,1024]{1,0:T(8,128)(2,1)S(1)}, u32[]{:S(2)}) copy-start(bf16[192,1024]{1,0:T(8,128)(2,1)S(1)} %collective-permute-done.25.refs_0_) | copy-start | bytes 1179652
  158.0 0.8 copy-start.1
  158.1 0.8 copy-start.2
  (1 other events, 0.6 us)

commit v3 on v2

--- a/solution.py
+++ b/solution.py
@@ -315,14 +315,14 @@
             e = jnp.exp2(scores - high)
             state = (high, jnp.sum(e, axis=0, keepdims=True), jnp.sum(e * grads, axis=0, keepdims=True))
 
-            def scan(j, state, partial):
+            def scan(j, state, tile, partial):
                 high, total_e, total_w = state
-                at = k_at(j)
+                at = pl.ds(pl.multiple_of(j * KT, KT), tile)
                 scores = lax.dot_general(k_s[at, :], q_one, ROWS_ROWS, preferred_element_type=f32)
                 grads = lax.dot_general(v_s[at, :], do, ROWS_ROWS, preferred_element_type=f32)
                 scores = scores * (scale * LOG2E)
                 if partial:
-                    scores = jnp.where(key_row < rest, scores, MASKED)
+                    scores = jnp.where(key_row[:tile] < rest, scores, MASKED)
                 s_s[at, :size] = scores
                 g_s[at, :size] = grads
                 new = jnp.maximum(high, jnp.max(scores, axis=0, keepdims=True))
@@ -334,9 +334,13 @@
                     total_w * shrink + jnp.sum(e * grads, axis=0, keepdims=True),
                 )
 
-            state = lax.fori_loop(0, full, functools.partial(scan, partial=False), state)
-            ends = full + (rest > 0).astype(jnp.int32)
-            high, total_e, total_w = lax.fori_loop(full, ends, functools.partial(scan, partial=True), state)
+            state = lax.fori_loop(0, full, functools.partial(scan, tile=KT, partial=False), state)
+            ends = full + (rest > KT // 2).astype(jnp.int32)
+            small = ((rest > 0) & (rest <= KT // 2)).astype(jnp.int32)
+            state = lax.fori_loop(full, ends, functools.partial(scan, tile=KT, partial=True), state)
+            high, total_e, total_w = lax.fori_loop(
+                full, full + small, functools.partial(scan, tile=KT // 2, partial=True), state
+            )
             delta = total_w / total_e
             log_total = high + jnp.log2(total_e)
 
@@ -348,9 +352,12 @@
                 return lax.dot_general(key_t, dscore, ROWS_COLS, preferred_element_type=f32)
 
             dq = spread(own, own_k.T, so_s[:, :size], go_s[:, :size])
-            dq = lax.fori_loop(
-                0, ends, lambda j, dq: dq + spread(k_at(j), kt_s[:, k_at(j)], s_s[k_at(j), :size], g_s[k_at(j), :size]), dq
-            )
+            def spread_tile(j, dq, tile):
+                at = pl.ds(pl.multiple_of(j * KT, KT), tile)
+                return dq + spread(at, kt_s[:, at], s_s[at, :size], g_s[at, :size])
+
+            dq = lax.fori_loop(0, ends, functools.partial(spread_tile, tile=KT), dq)
+            dq = lax.fori_loop(full, full + small, functools.partial(spread_tile, tile=KT // 2), dq)
             dq_s[q_at, :] = (dq * scale).T.astype(bf)
             return carry
 

time: 166 us -> 163 us (0.982); the launches traced: 164 us -> 163 us
    ppermute x3, starting transfers between devices: 2.16 us -> 5.9 us  [shift_dp(): lax.ppermute(array, 'dp', [(i, (i + step) % dp_devices) for i in range(dp...]
    ppermute x6, waiting for transfers between devices: 19.6 us -> 17.8 us  [shift_y(): return lax.ppermute(array, 'seq', pairs)]
    ppermute x6, starting transfers between devices: 9.58 us -> 7.71 us  [shift_y(): return lax.ppermute(array, 'seq', pairs)]
    ppermute x1, waiting for transfers between devices: 4.19 us -> 6.06 us  [shards(): dq_back = lax.ppermute(dq_far, 'seq', mirror)]
where the time goes in v3:
time: 163 us
  starting transfers between devices  52.6 us (32%)
  waiting for transfers between devices  51 us (31%)
  Pallas kernels  43.5 us (27%)
  local copies, waits for them, and re-layouts  12.1 us (7%)
  other arithmetic  3.26 us (2%)
    ppermute x6, waiting for transfers between devices, shift_y(): return lax.ppermute(array, 'seq', pairs)  17.8 us
    pallas_call x1, Pallas kernels, attention_backward(): pl.pallas_call(attention_kernel, out_shape=[jax.ShapeDtypeStruct((cap, wi...  14.8 us
    ppermute x4, starting transfers between devices, shards(): received.append(lax.ppermute(products[step], ('dp', 'rep'), pairs))  9.84 us
    ppermute x4, waiting for transfers between devices, shards(): received.append(lax.ppermute(products[step], ('dp', 'rep'), pairs))  9.61 us
    ppermute x6, starting transfers between devices, shift_x(): return lax.ppermute(array, 'seq', pairs)  8.46 us
    ppermute x6, starting transfers between devices, shift_y(): return lax.ppermute(array, 'seq', pairs)  7.71 us
    pallas_call x2, Pallas kernels, spread_rows(): pl.pallas_call(spread_kernel, grid_spec=pltpu.PrefetchScalarGridSpec(num_...  7.35 us
    ppermute x3, waiting for transfers between devices, shift_dp(): lax.ppermute(array, 'dp', [(i, (i + step) % dp_devices) for i in range(dp...  7.1 us
  transfers between devices with their start and end apart: 29, of which 16 were waited for; matrix products, arithmetic and copies ran while one was open for 7% of the time, Pallas kernels for 20%

profile of v3, /device:TPU:1, one launch (start us, length us, event | category | flops | bytes accessed | tf_op | source)
XLA Modules:
  0.0 163.4 jit_solution(14139602630715266345)
XLA Ops:
  0.8 0.9 fusion
  1.7 2.1 %collective-permute-start = (bf16[192,256]{1,0:T(8,128)(2,1)S(1)}, bf16[192,256]{1,0:T(8,128)(2,1)S(1)}, u32[]{:S(2)}, u32[]{:S(2)}) collective-permute-start(bf16[192,256]{1,0:T(8,128)(2,1)S(1)} %get-tuple-element.118), channel_id=1, source_target_pairs={{0,32},{8,40},{16,48},{24,56},{32,64},{40,72},{48,80},{56,88},{64,... | collective-permute-start | bytes 294920 | tf_op jit(solution)/shard_map/ppermute | solution.py:492
  3.8 2.5 %collective-permute-start.1 = (bf16[192,256]{1,0:T(8,128)(2,1)S(1)}, bf16[192,256]{1,0:T(8,128)(2,1)S(1)}, u32[]{:S(2)}, u32[]{:S(2)}) collective-permute-start(bf16[192,256]{1,0:T(8,128)(2,1)S(1)} %get-tuple-element.119), channel_id=1, source_target_pairs={{0,64},{8,72},{16,80},{24,88},{32,96},{40,104},{48,112},{56,120},{... | collective-permute-start | bytes 294920 | tf_op jit(solution)/shard_map/ppermute | solution.py:492
  6.3 1.2 collective-permute-start.2
  7.5 1.2 constant_dynamic-slice_fusion
  8.8 1.2 dynamic-slice_bitcast_fusion.2
  10.4 2.9 %collective-permute-start.6 = (bf16[768,256]{1,0:T(8,128)(2,1)S(1)}, bf16[768,256]{1,0:T(8,128)(2,1)S(1)}, u32[]{:S(2)}, u32[]{:S(2)}) collective-permute-start(bf16[768,256]{1,0:T(8,128)(2,1)S(1)} %pad_maximum_fusion.2.kv0), channel_id=1, source_target_pairs={{0,24},{8,0},{16,8},{24,16},{32,56},{40,32},{48,40},{56,48},{64,88... | collective-permute-start | bytes 1179656 | tf_op jit(solution)/shard_map/ppermute | solution.py:496
  14.2 1.2 compare_select_fusion
  15.5 2.4 %collective-permute-start.3 = (bf16[192,2048]{1,0:T(8,128)(2,1)S(1)}, bf16[192,2048]{1,0:T(8,128)(2,1)S(1)}, u32[]{:S(2)}, u32[]{:S(2)}) collective-permute-start(bf16[192,2048]{1,0:T(8,128)(2,1)S(1)} %pad_maximum_fusion), channel_id=1, source_target_pairs={{0,96},{8,104},{16,112},{24,120},{32,64},{40,72},{48,80},{56,88},{... | collective-permute-start | bytes 2359304 | tf_op jit(solution)/shard_map/ppermute | solution.py:519
  19.3 5.6 %gather_columns.1 = bf16[4,192,1024]{2,1,0:T(8,128)(2,1)} custom-call(s32[6]{0:T(128)} %stack.45.place, s32[192,1]{1,0:T(8,128)} %copy.12.rows_ref, bf16[512,8192]{1,0:T(8,128)(2,1)} %bitcast.34), custom_call_target="tpu_custom_call" | custom-call | flops 800000000 | bytes 6000000 | tf_op jit(solution)/shard_map/gather_columns/pallas_call | solution.py:46
  24.9 9.3 %collective-permute-done.4.kv1 = bf16[768,256]{1,0:T(8,128)(2,1)S(1)} collective-permute-done((bf16[768,256]{1,0:T(8,128)(2,1)S(1)}, bf16[768,256]{1,0:T(8,128)(2,1)S(1)}, u32[]{:S(2)}, u32[]{:S(2)}) %collective-permute-start.4) | collective-permute-done | bytes 393248 | tf_op jit(solution)/shard_map/ppermute | solution.py:496
  34.2 5.0 %all-to-all-start = ((bf16[4,192,1024]{2,1,0:T(8,128)(2,1)}), bf16[4,192,1024]{2,1,0:T(8,128)(2,1)}, u32[]{:S(2)}, u32[]{:S(2)}) async-start(bf16[4,192,1024]{2,1,0:T(8,128)(2,1)} %gather_columns.1), calls=%async_computation | async-start | bytes 3145728 | tf_op jit(solution)/shard_map/all_to_all | solution.py:527
  40.1 14.8 %attention_backward.1 = (bf16[192,1024]{1,0:T(8,128)(2,1)}, bf16[192,1024]{1,0:T(8,128)(2,1)}, bf16[768,256]{1,0:T(8,128)(2,1)}, bf16[768,256]{1,0:T(8,128)(2,1)...) custom-call(s32[16]{0:T(128)} %bitcast.43, s32[6]{0:T(128)} %stack.45.place, bf16[192,2048]{1,0:T(8,128)(2,1)} %bitcast.36, ...), custom_call_target="tpu_custom_call" | custom-call | flops 6000000000 | bytes 6000000 | tf_op jit(solution)/shard_map/attention_backward/pallas_call | solution.py:394
  54.9 4.4 %all-to-all-done.own_ref = bf16[4,192,1024]{2,1,0:T(8,128)(2,1)} async-done(((bf16[4,192,1024]{2,1,0:T(8,128)(2,1)}), bf16[4,192,1024]{2,1,0:T(8,128)(2,1)}, u32[]{:S(2)}, u32[]{:S(2)}) %all-to-all-start) | async-done | bytes 1572896 | tf_op jit(solution)/shard_map/all_to_all | solution.py:527
  59.3 1.7 %collective-permute-start.10 = (bf16[4,192,1024]{2,1,0:T(8,128)(2,1)}, bf16[4,192,1024]{2,1,0:T(8,128)(2,1)}, u32[]{:S(2)}, u32[]{:S(2)}) collective-permute-start(bf16[4,192,1024]{2,1,0:T(8,128)(2,1)} %all-to-all-done.own_ref), channel_id=1, source_target_pairs={{0,1},{1,0},{2,3},{3,2},{4,5},{5,4},{6,7},{7,6},{8,9},{9,8},{10,11... | collective-permute-start | bytes 4718600 | tf_op jit(solution)/shard_map/ppermute | solution.py:533
  61.0 2.4 %collective-permute-start.11 = (bf16[192,1024]{1,0:T(8,128)(2,1)}, bf16[192,1024]{1,0:T(8,128)(2,1)S(1)}, u32[]{:S(2)}, u32[]{:S(2)}) collective-permute-start(bf16[192,1024]{1,0:T(8,128)(2,1)} %get-tuple-element.76), channel_id=1, source_target_pairs={{0,96},{8,104},{16,112},{24,120},{32,64},{40,72},{48,80},{56,88},{... | collective-permute-start | bytes 1179656 | tf_op jit(solution)/shard_map/ppermute | solution.py:532
  63.4 2.6 %collective-permute-start.9 = (bf16[768,256]{1,0:T(8,128)(2,1)}, bf16[768,256]{1,0:T(8,128)(2,1)}, u32[]{:S(2)}, u32[]{:S(2)}) collective-permute-start(bf16[768,256]{1,0:T(8,128)(2,1)} %get-tuple-element.74), channel_id=1, source_target_pairs={{0,24},{8,0},{16,8},{24,16},{32,56},{40,32},{48,40},{56,48},{64,88... | collective-permute-start | bytes 1179656 | tf_op jit(solution)/shard_map/ppermute | solution.py:496
  66.1 1.2 collective-permute-start.8
  67.3 6.1 %collective-permute-done.11 = bf16[192,1024]{1,0:T(8,128)(2,1)S(1)} collective-permute-done((bf16[192,1024]{1,0:T(8,128)(2,1)}, bf16[192,1024]{1,0:T(8,128)(2,1)S(1)}, u32[]{:S(2)}, u32[]{:S(2)}) %collective-permute-start.11) | collective-permute-done | bytes 393248 | tf_op jit(solution)/shard_map/ppermute | solution.py:532
  73.3 3.2 %reshape.22 = bf16[2,1024,512]{2,1,0:T(8,128)(2,1)S(1)} reshape(bf16[2048,2,256]{2,1,0:T(2,128)(2,1)} %param.15) | data formatting | bytes 4194304 | tf_op jit(solution)/shard_map/reshape | solution.py:535
  76.5 1.1 dynamic-slice_bitcast_fusion
  77.6 5.2 %collective-permute-done.9.refs_3_ = bf16[768,256]{1,0:T(8,128)(2,1)} collective-permute-done((bf16[768,256]{1,0:T(8,128)(2,1)}, bf16[768,256]{1,0:T(8,128)(2,1)}, u32[]{:S(2)}, u32[]{:S(2)}) %collective-permute-start.9) | collective-permute-done | bytes 393248 | tf_op jit(solution)/shard_map/ppermute | solution.py:496
  82.8 3.2 %collective-permute-done.7.refs_1_ = bf16[768,256]{1,0:T(8,128)(2,1)} collective-permute-done((bf16[768,256]{1,0:T(8,128)(2,1)}, bf16[768,256]{1,0:T(8,128)(2,1)}, u32[]{:S(2)}, u32[]{:S(2)}) %collective-permute-start.7) | collective-permute-done | bytes 393248 | tf_op jit(solution)/shard_map/ppermute | solution.py:496
  86.0 2.2 %y_sum.1 = (bf16[192,256]{1,0:T(8,128)(2,1)}, bf16[192,256]{1,0:T(8,128)(2,1)}, bf16[192,256]{1,0:T(8,128)(2,1)}, bf16[192,256]{1,0:T(8,128)(2,1)}) custom-call(s32[6]{0:T(128)} %stack.45.place, bf16[768,256]{1,0:T(8,128)(2,1)} %get-tuple-element.71.refs_0_, bf16[768,256]{1,0:T(8,128)(2,1)} %collective-permute-done.7.refs_1_, ...), custom_call_target="tpu_custom_call" | custom-call | flops 1000000 | bytes 2000000 | tf_op jit(solution)/shard_map/y_sum/pallas_call | solution.py:80
  88.3 1.5 collective-permute-start.15
  89.8 1.5 collective-permute-start.13
  91.3 1.2 collective-permute-start.14
  92.5 5.2 %collective-permute-done.12.refs_1_ = bf16[192,256]{1,0:T(8,128)(2,1)S(1)} collective-permute-done((bf16[192,256]{1,0:T(8,128)(2,1)}, bf16[192,256]{1,0:T(8,128)(2,1)S(1)}, u32[]{:S(2)}, u32[]{:S(2)}) %collective-permute-start.12) | collective-permute-done | bytes 98336 | tf_op jit(solution)/shard_map/ppermute | solution.py:492
  98.6 2.2 %x_sum.1.refs_0_ = bf16[192,512]{1,0:T(8,128)(2,1)} custom-call(s32[6]{0:T(128)} %stack.45.place, bf16[192,256]{1,0:T(8,128)(2,1)} %get-tuple-element.90.refs_0_, bf16[192,256]{1,0:T(8,128)(2,1)} %copy-done.9, bf16[192,256]{1,0:T(8,128)(2,1)} %copy-done.10, bf16[192,256]{1,0:T(8,128)(2,1)} %copy-done.11), custom_call_target="tpu_custom_call" | custom-call | flops 1000000 | bytes 1000000 | tf_op jit(solution)/shard_map/x_sum/pallas_call | solution.py:114
  100.9 1.1 collective-permute-start.19
  102.0 1.7 %collective-permute-start.18 = (bf16[192,512]{1,0:T(8,128)(2,1)}, bf16[192,512]{1,0:T(8,128)(2,1)S(1)}, u32[]{:S(2)}, u32[]{:S(2)}) collective-permute-start(bf16[192,512]{1,0:T(8,128)(2,1)} %x_sum.1.refs_0_), channel_id=1, source_target_pairs={{0,6},{2,0},{4,2},{6,4},{1,7},{3,1},{5,3},{7,5},{8,14},{10,8},{12,... | collective-permute-start | bytes 589832 | tf_op jit(solution)/shard_map/ppermute | solution.py:488
  103.6 3.4 %collective-permute-start.17 = (bf16[192,512]{1,0:T(8,128)(2,1)}, bf16[192,512]{1,0:T(8,128)(2,1)S(1)}, u32[]{:S(2)}, u32[]{:S(2)}) collective-permute-start(bf16[192,512]{1,0:T(8,128)(2,1)} %x_sum.1.refs_0_), channel_id=1, source_target_pairs={{0,4},{2,6},{4,0},{6,2},{1,5},{3,7},{5,1},{7,3},{8,12},{10,14},{12... | collective-permute-start | bytes 589832 | tf_op jit(solution)/shard_map/ppermute | solution.py:488
  108.7 0.9 collective-permute-start.22
  109.5 2.9 %collective-permute-done.17.refs_2_ = bf16[192,512]{1,0:T(8,128)(2,1)S(1)} collective-permute-done((bf16[192,512]{1,0:T(8,128)(2,1)}, bf16[192,512]{1,0:T(8,128)(2,1)S(1)}, u32[]{:S(2)}, u32[]{:S(2)}) %collective-permute-start.17) | collective-permute-done | bytes 196640 | tf_op jit(solution)/shard_map/ppermute | solution.py:488
  112.5 0.9 collective-permute-start.21
  113.4 3.5 %collective-permute-done.16.refs_1_ = bf16[192,512]{1,0:T(8,128)(2,1)S(1)} collective-permute-done((bf16[192,512]{1,0:T(8,128)(2,1)}, bf16[192,512]{1,0:T(8,128)(2,1)S(1)}, u32[]{:S(2)}, u32[]{:S(2)}) %collective-permute-start.16) | collective-permute-done | bytes 196640 | tf_op jit(solution)/shard_map/ppermute | solution.py:488
  117.3 0.9 pad_maximum_fusion.1
  118.6 6.1 %weight_terms.1 = bf16[2048,512]{1,0:T(8,128)(2,1)} custom-call(s32[6]{0:T(128)} %stack.45.place, bf16[4,192,1024]{2,1,0:T(8,128)(2,1)} %all-to-all-done.own_ref, bf16[4,192,1024]{2,1,0:T(8,128)(2,1)} %collective-permute-done.10.other_ref, bf16[192,512]{1,0:T(8,128)(2,1)} %x_sum.1.refs_0_, bf16[192,512]{1,0:T(8,128)(2,1)} %copy-done.8, ...), custom_call_target="tpu_custom_call" | custom-call | flops 1600000000 | bytes 6000000 | tf_op jit(solution)/shard_map/weight_terms/pallas_call | solution.py:156
  124.7 4.2 %all-to-all-start.1 = ((bf16[16,128,512]{2,1,0:T(8,128)(2,1)}), bf16[16,128,512]{2,1,0:T(8,128)(2,1)S(1)}, u32[]{:S(2)}, u32[]{:S(2)}) async-start(bf16[16,128,512]{2,1,0:T(8,128)(2,1)} %bitcast.33), calls=%async_computation.1 | async-start | bytes 4194304 | tf_op jit(solution)/shard_map/all_to_all | solution.py:557
  128.9 5.2 %input_products.1 = (bf16[192,1024]{1,0:T(8,128)(2,1)}, bf16[192,1024]{1,0:T(8,128)(2,1)}, bf16[192,1024]{1,0:T(8,128)(2,1)}, bf16[192,1024]{1,0:T(8,128)(2,1)}) custom-call(s32[6]{0:T(128)} %stack.45.place, bf16[192,512]{1,0:T(8,128)(2,1)} %x_sum.1.refs_0_, bf16[192,512]{1,0:T(8,128)(2,1)} %copy-done.8, bf16[192,512]{1,0:T(8,128)(2,1)} %copy-done.7, ...), custom_call_target="tpu_custom_call" | custom-call | flops 1600000000 | bytes 6000000 | tf_op jit(solution)/shard_map/input_products/pallas_call | solution.py:209
  134.1 3.6 %collective-permute-start.25 = (bf16[192,1024]{1,0:T(8,128)(2,1)}, bf16[192,1024]{1,0:T(8,128)(2,1)S(1)}, u32[]{:S(2)}, u32[]{:S(2)}) collective-permute-start(bf16[192,1024]{1,0:T(8,128)(2,1)} %get-tuple-element.110), channel_id=1, source_target_pairs={{0,0},{1,2},{2,4},{3,6},{4,1},{5,3},{6,5},{7,7},{8,8},{9,10},{10,1... | collective-permute-start | bytes 1179656 | tf_op jit(solution)/shard_map/ppermute | solution.py:571
  137.6 1.9 %collective-permute-start.26 = (bf16[192,1024]{1,0:T(8,128)(2,1)}, bf16[192,1024]{1,0:T(8,128)(2,1)}, u32[]{:S(2)}, u32[]{:S(2)}) collective-permute-start(bf16[192,1024]{1,0:T(8,128)(2,1)} %get-tuple-element.111), channel_id=1, source_target_pairs={{0,6},{1,0},{2,2},{3,4},{4,7},{5,1},{6,3},{7,5},{8,14},{9,8},{10,1... | collective-permute-start | bytes 1179656 | tf_op jit(solution)/shard_map/ppermute | solution.py:571
  139.6 3.5 %collective-permute-start.23 = (bf16[192,1024]{1,0:T(8,128)(2,1)}, bf16[192,1024]{1,0:T(8,128)(2,1)S(1)}, u32[]{:S(2)}, u32[]{:S(2)}) collective-permute-start(bf16[192,1024]{1,0:T(8,128)(2,1)} %get-tuple-element.108), channel_id=1, source_target_pairs={{0,2},{1,4},{2,6},{3,0},{4,3},{5,5},{6,7},{7,1},{8,10},{9,12},{10,... | collective-permute-start | bytes 1179656 | tf_op jit(solution)/shard_map/ppermute | solution.py:571
  144.5 1.8 %collective-permute-done.25.refs_0_ = bf16[192,1024]{1,0:T(8,128)(2,1)S(1)} collective-permute-done((bf16[192,1024]{1,0:T(8,128)(2,1)}, bf16[192,1024]{1,0:T(8,128)(2,1)S(1)}, u32[]{:S(2)}, u32[]{:S(2)}) %collective-permute-start.25) | collective-permute-done | bytes 393248 | tf_op jit(solution)/shard_map/ppermute | solution.py:571
  146.3 6.1 %collective-permute-done.26.refs_1_ = bf16[192,1024]{1,0:T(8,128)(2,1)} collective-permute-done((bf16[192,1024]{1,0:T(8,128)(2,1)}, bf16[192,1024]{1,0:T(8,128)(2,1)}, u32[]{:S(2)}, u32[]{:S(2)}) %collective-permute-start.26) | collective-permute-done | bytes 393248 | tf_op jit(solution)/shard_map/ppermute | solution.py:571
  152.4 3.7 %spread_rows.2.refs_2_ = bf16[512,4096]{1,0:T(8,128)(2,1)} custom-call(s32[2]{0:T(128)} %get-tuple-element.125.order, s32[1,192]{1,0:T(1,128)} %bitcast.40, bf16[192,1024]{1,0:T(8,128)(2,1)} %copy-done.3, bf16[192,1024]{1,0:T(8,128)(2,1)} %collective-permute-done.26.refs_1_), custom_call_target="tpu_custom_call" | custom-call | flops 400000000 | bytes 3000000 | tf_op jit(solution)/shard_map/spread_rows/pallas_call | solution.py:445
  158.6 3.7 %spread_rows.3 = bf16[512,4096]{1,0:T(8,128)(2,1)} custom-call(s32[2]{0:T(128)} %get-tuple-element.124.order, s32[1,192]{1,0:T(1,128)} %bitcast.41, bf16[192,1024]{1,0:T(8,128)(2,1)} %copy-done.1, bf16[192,1024]{1,0:T(8,128)(2,1)} %copy-done.2, bf16[512,4096]{1,0:T(8,128)(2,1)} %spread_rows.2.refs_2_), custom_call_target="tpu_custom_call", output_to_operand_aliasing={{}: (4, {})} | custom-call | flops 400000000 | bytes 3000000 | tf_op jit(solution)/shard_map/spread_rows/pallas_call | solution.py:445
  162.5 0.9 reshape.24
  (77 shorter events, 11.2 us)
Async XLA Ops:
  0.6 9.4 %copy-start = (s32[1,16,192]{2,1,0:T(8,128)S(1)}, s32[1,16,192]{2,1,0:T(8,128)}, u32[]{:S(2)}) copy-start(s32[1,16,192]{2,1,0:T(8,128)} %param.9) | copy-start | bytes 36868
  1.7 8.3 %collective-permute-start = (bf16[192,256]{1,0:T(8,128)(2,1)S(1)}, bf16[192,256]{1,0:T(8,128)(2,1)S(1)}, u32[]{:S(2)}, u32[]{:S(2)}) collective-permute-start(bf16[192,256]{1,0:T(8,128)(2,1)S(1)} %get-tuple-element.118), channel_id=1, source_target_pairs={{0,32},{8,40},{16,48},{24,56},{32,64},{40,72},{48,80},{56,88},{64,... | collective-permute-start | bytes 294920 | tf_op jit(solution)/shard_map/ppermute | solution.py:492
  3.8 6.5 %collective-permute-start.1 = (bf16[192,256]{1,0:T(8,128)(2,1)S(1)}, bf16[192,256]{1,0:T(8,128)(2,1)S(1)}, u32[]{:S(2)}, u32[]{:S(2)}) collective-permute-start(bf16[192,256]{1,0:T(8,128)(2,1)S(1)} %get-tuple-element.119), channel_id=1, source_target_pairs={{0,64},{8,72},{16,80},{24,88},{32,96},{40,104},{48,112},{56,120},{... | collective-permute-start | bytes 294920 | tf_op jit(solution)/shard_map/ppermute | solution.py:492
  6.3 4.0 %collective-permute-start.2 = (bf16[192,256]{1,0:T(8,128)(2,1)S(1)}, bf16[192,256]{1,0:T(8,128)(2,1)S(1)}, u32[]{:S(2)}, u32[]{:S(2)}) collective-permute-start(bf16[192,256]{1,0:T(8,128)(2,1)S(1)} %broadcast_select_fusion.2), channel_id=1, source_target_pairs={{0,96},{8,104},{16,112},{24,120},{32,0},{40,8},{48,16},{56,24},{64... | collective-permute-start | bytes 294920 | tf_op jit(solution)/shard_map/ppermute | solution.py:492
  10.3 14.5 %copy-start.4 = (bf16[768,256]{1,0:T(8,128)(2,1)}, bf16[768,256]{1,0:T(8,128)(2,1)S(1)}, u32[]{:S(2)}) copy-start(bf16[768,256]{1,0:T(8,128)(2,1)S(1)} %pad_maximum_fusion.2.kv0) | copy-start | bytes 1179652
  10.4 14.5 %collective-permute-start.6 = (bf16[768,256]{1,0:T(8,128)(2,1)S(1)}, bf16[768,256]{1,0:T(8,128)(2,1)S(1)}, u32[]{:S(2)}, u32[]{:S(2)}) collective-permute-start(bf16[768,256]{1,0:T(8,128)(2,1)S(1)} %pad_maximum_fusion.2.kv0), channel_id=1, source_target_pairs={{0,24},{8,0},{16,8},{24,16},{32,56},{40,32},{48,40},{56,48},{64,88... | collective-permute-start | bytes 1179656 | tf_op jit(solution)/shard_map/ppermute | solution.py:496
  13.2 11.6 %collective-permute-start.5 = (bf16[768,256]{1,0:T(8,128)(2,1)S(1)}, bf16[768,256]{1,0:T(8,128)(2,1)S(1)}, u32[]{:S(2)}, u32[]{:S(2)}) collective-permute-start(bf16[768,256]{1,0:T(8,128)(2,1)S(1)} %pad_maximum_fusion.2.kv0), channel_id=1, source_target_pairs={{0,16},{8,24},{16,0},{24,8},{32,48},{40,56},{48,32},{56,40},{64,80... | collective-permute-start | bytes 1179656 | tf_op jit(solution)/shard_map/ppermute | solution.py:496
  13.6 20.6 %collective-permute-start.4 = (bf16[768,256]{1,0:T(8,128)(2,1)S(1)}, bf16[768,256]{1,0:T(8,128)(2,1)S(1)}, u32[]{:S(2)}, u32[]{:S(2)}) collective-permute-start(bf16[768,256]{1,0:T(8,128)(2,1)S(1)} %pad_maximum_fusion.2.kv0), channel_id=1, source_target_pairs={{0,8},{8,16},{16,24},{24,0},{32,40},{40,48},{48,56},{56,32},{64,72... | collective-permute-start | bytes 1179656 | tf_op jit(solution)/shard_map/ppermute | solution.py:496
  15.5 23.7 %collective-permute-start.3 = (bf16[192,2048]{1,0:T(8,128)(2,1)S(1)}, bf16[192,2048]{1,0:T(8,128)(2,1)S(1)}, u32[]{:S(2)}, u32[]{:S(2)}) collective-permute-start(bf16[192,2048]{1,0:T(8,128)(2,1)S(1)} %pad_maximum_fusion), channel_id=1, source_target_pairs={{0,96},{8,104},{16,112},{24,120},{32,64},{40,72},{48,80},{56,88},{... | collective-permute-start | bytes 2359304 | tf_op jit(solution)/shard_map/ppermute | solution.py:519
  24.8 14.4 %copy-start.14 = (bf16[768,256]{1,0:T(8,128)(2,1)}, bf16[768,256]{1,0:T(8,128)(2,1)S(1)}, u32[]{:S(2)}) copy-start(bf16[768,256]{1,0:T(8,128)(2,1)S(1)} %collective-permute-done.6.kv3) | copy-start | bytes 1179652
  24.8 14.4 %copy-start.15 = (bf16[768,256]{1,0:T(8,128)(2,1)}, bf16[768,256]{1,0:T(8,128)(2,1)S(1)}, u32[]{:S(2)}) copy-start(bf16[768,256]{1,0:T(8,128)(2,1)S(1)} %collective-permute-done.5.kv2) | copy-start | bytes 1179652
  34.2 5.1 %copy-start.16 = (bf16[768,256]{1,0:T(8,128)(2,1)}, bf16[768,256]{1,0:T(8,128)(2,1)S(1)}, u32[]{:S(2)}) copy-start(bf16[768,256]{1,0:T(8,128)(2,1)S(1)} %collective-permute-done.4.kv1) | copy-start | bytes 1179652
  34.2 25.2 %all-to-all-start = ((bf16[4,192,1024]{2,1,0:T(8,128)(2,1)}), bf16[4,192,1024]{2,1,0:T(8,128)(2,1)}, u32[]{:S(2)}, u32[]{:S(2)}) async-start(bf16[4,192,1024]{2,1,0:T(8,128)(2,1)} %gather_columns.1), calls=%async_computation | async-start | bytes 3145728 | tf_op jit(solution)/shard_map/all_to_all | solution.py:527
  39.2 0.9 copy-start.13
  59.3 23.5 %collective-permute-start.10 = (bf16[4,192,1024]{2,1,0:T(8,128)(2,1)}, bf16[4,192,1024]{2,1,0:T(8,128)(2,1)}, u32[]{:S(2)}, u32[]{:S(2)}) collective-permute-start(bf16[4,192,1024]{2,1,0:T(8,128)(2,1)} %all-to-all-done.own_ref), channel_id=1, source_target_pairs={{0,1},{1,0},{2,3},{3,2},{4,5},{5,4},{6,7},{7,6},{8,9},{9,8},{10,11... | collective-permute-start | bytes 4718600 | tf_op jit(solution)/shard_map/ppermute | solution.py:533
  61.0 12.3 %collective-permute-start.11 = (bf16[192,1024]{1,0:T(8,128)(2,1)}, bf16[192,1024]{1,0:T(8,128)(2,1)S(1)}, u32[]{:S(2)}, u32[]{:S(2)}) collective-permute-start(bf16[192,1024]{1,0:T(8,128)(2,1)} %get-tuple-element.76), channel_id=1, source_target_pairs={{0,96},{8,104},{16,112},{24,120},{32,64},{40,72},{48,80},{56,88},{... | collective-permute-start | bytes 1179656 | tf_op jit(solution)/shard_map/ppermute | solution.py:532
  63.4 19.4 %collective-permute-start.9 = (bf16[768,256]{1,0:T(8,128)(2,1)}, bf16[768,256]{1,0:T(8,128)(2,1)}, u32[]{:S(2)}, u32[]{:S(2)}) collective-permute-start(bf16[768,256]{1,0:T(8,128)(2,1)} %get-tuple-element.74), channel_id=1, source_target_pairs={{0,24},{8,0},{16,8},{24,16},{32,56},{40,32},{48,40},{56,48},{64,88... | collective-permute-start | bytes 1179656 | tf_op jit(solution)/shard_map/ppermute | solution.py:496
  66.1 20.0 %collective-permute-start.7 = (bf16[768,256]{1,0:T(8,128)(2,1)}, bf16[768,256]{1,0:T(8,128)(2,1)}, u32[]{:S(2)}, u32[]{:S(2)}) collective-permute-start(bf16[768,256]{1,0:T(8,128)(2,1)} %get-tuple-element.72), channel_id=1, source_target_pairs={{0,8},{8,16},{16,24},{24,0},{32,40},{40,48},{48,56},{56,32},{64,72... | collective-permute-start | bytes 1179656 | tf_op jit(solution)/shard_map/ppermute | solution.py:496
  66.1 20.0 %collective-permute-start.8 = (bf16[768,256]{1,0:T(8,128)(2,1)}, bf16[768,256]{1,0:T(8,128)(2,1)}, u32[]{:S(2)}, u32[]{:S(2)}) collective-permute-start(bf16[768,256]{1,0:T(8,128)(2,1)} %get-tuple-element.73), channel_id=1, source_target_pairs={{0,16},{8,24},{16,0},{24,8},{32,48},{40,56},{48,32},{56,40},{64,80... | collective-permute-start | bytes 1179656 | tf_op jit(solution)/shard_map/ppermute | solution.py:496
  77.6 30.3 %copy-start.5 = (bf16[192,1024]{1,0:T(8,128)(2,1)S(1)}, bf16[192,1024]{1,0:T(8,128)(2,1)}, u32[]{:S(2)}) copy-start(bf16[192,1024]{1,0:T(8,128)(2,1)} %get-tuple-element.94) | copy-start | bytes 1179652
  88.3 9.7 %collective-permute-start.15 = (bf16[1024,512]{1,0:T(8,128)(2,1)S(1)}, bf16[1024,512]{1,0:T(8,128)(2,1)S(1)}, u32[]{:S(2)}, u32[]{:S(2)}) collective-permute-start(bf16[1024,512]{1,0:T(8,128)(2,1)S(1)} %get-tuple-element.89), channel_id=1, source_target_pairs={{0,1},{1,0},{2,3},{3,2},{4,5},{5,4},{6,7},{7,6},{8,9},{9,8},{10,11... | collective-permute-start | bytes 3145736 | tf_op jit(solution)/shard_map/ppermute | solution.py:544
  89.8 7.9 %collective-permute-start.12 = (bf16[192,256]{1,0:T(8,128)(2,1)}, bf16[192,256]{1,0:T(8,128)(2,1)S(1)}, u32[]{:S(2)}, u32[]{:S(2)}) collective-permute-start(bf16[192,256]{1,0:T(8,128)(2,1)} %get-tuple-element.85), channel_id=1, source_target_pairs={{0,32},{8,40},{16,48},{24,56},{32,64},{40,72},{48,80},{56,88},{64,... | collective-permute-start | bytes 294920 | tf_op jit(solution)/shard_map/ppermute | solution.py:492
  89.8 7.9 %collective-permute-start.13 = (bf16[192,256]{1,0:T(8,128)(2,1)}, bf16[192,256]{1,0:T(8,128)(2,1)S(1)}, u32[]{:S(2)}, u32[]{:S(2)}) collective-permute-start(bf16[192,256]{1,0:T(8,128)(2,1)} %get-tuple-element.86), channel_id=1, source_target_pairs={{0,64},{8,72},{16,80},{24,88},{32,96},{40,104},{48,112},{56,120},{... | collective-permute-start | bytes 294920 | tf_op jit(solution)/shard_map/ppermute | solution.py:492
  91.3 6.7 %collective-permute-start.14 = (bf16[192,256]{1,0:T(8,128)(2,1)}, bf16[192,256]{1,0:T(8,128)(2,1)S(1)}, u32[]{:S(2)}, u32[]{:S(2)}) collective-permute-start(bf16[192,256]{1,0:T(8,128)(2,1)} %get-tuple-element.87), channel_id=1, source_target_pairs={{0,96},{8,104},{16,112},{24,120},{32,0},{40,8},{48,16},{56,24},{64... | collective-permute-start | bytes 294920 | tf_op jit(solution)/shard_map/ppermute | solution.py:492
  97.7 0.7 copy-start.10
  98.0 0.6 copy-start.11
  98.6 2.2 %copy-start.12 = (bf16[1024,512]{1,0:T(8,128)(2,1)}, bf16[1024,512]{1,0:T(8,128)(2,1)S(1)}, u32[]{:S(2)}) copy-start(bf16[1024,512]{1,0:T(8,128)(2,1)S(1)} %collective-permute-done.15.refs_9_) | copy-start | bytes 3145732
  100.9 17.4 %collective-permute-start.19 = (bf16[192,512]{1,0:T(8,128)(2,1)}, bf16[192,512]{1,0:T(8,128)(2,1)S(1)}, u32[]{:S(2)}, u32[]{:S(2)}) collective-permute-start(bf16[192,512]{1,0:T(8,128)(2,1)} %x_sum.1.refs_0_), channel_id=1, source_target_pairs={{0,1},{1,0},{2,3},{3,2},{4,5},{5,4},{6,7},{7,6},{8,9},{9,8},{10,11... | collective-permute-start | bytes 589832 | tf_op jit(solution)/shard_map/ppermute | solution.py:553
  102.0 6.7 %collective-permute-start.18 = (bf16[192,512]{1,0:T(8,128)(2,1)}, bf16[192,512]{1,0:T(8,128)(2,1)S(1)}, u32[]{:S(2)}, u32[]{:S(2)}) collective-permute-start(bf16[192,512]{1,0:T(8,128)(2,1)} %x_sum.1.refs_0_), channel_id=1, source_target_pairs={{0,6},{2,0},{4,2},{6,4},{1,7},{3,1},{5,3},{7,5},{8,14},{10,8},{12,... | collective-permute-start | bytes 589832 | tf_op jit(solution)/shard_map/ppermute | solution.py:488
  103.6 8.8 %collective-permute-start.17 = (bf16[192,512]{1,0:T(8,128)(2,1)}, bf16[192,512]{1,0:T(8,128)(2,1)S(1)}, u32[]{:S(2)}, u32[]{:S(2)}) collective-permute-start(bf16[192,512]{1,0:T(8,128)(2,1)} %x_sum.1.refs_0_), channel_id=1, source_target_pairs={{0,4},{2,6},{4,0},{6,2},{1,5},{3,7},{5,1},{7,3},{8,12},{10,14},{12... | collective-permute-start | bytes 589832 | tf_op jit(solution)/shard_map/ppermute | solution.py:488
  107.0 9.8 %collective-permute-start.16 = (bf16[192,512]{1,0:T(8,128)(2,1)}, bf16[192,512]{1,0:T(8,128)(2,1)S(1)}, u32[]{:S(2)}, u32[]{:S(2)}) collective-permute-start(bf16[192,512]{1,0:T(8,128)(2,1)} %x_sum.1.refs_0_), channel_id=1, source_target_pairs={{0,2},{2,4},{4,6},{6,0},{1,3},{3,5},{5,7},{7,1},{8,10},{10,12},{12... | collective-permute-start | bytes 589832 | tf_op jit(solution)/shard_map/ppermute | solution.py:488
  108.6 9.9 %copy-start.6 = (bf16[192,512]{1,0:T(8,128)(2,1)}, bf16[192,512]{1,0:T(8,128)(2,1)S(1)}, u32[]{:S(2)}) copy-start(bf16[192,512]{1,0:T(8,128)(2,1)S(1)} %collective-permute-done.18.refs_3_) | copy-start | bytes 589828
  108.7 9.6 %collective-permute-start.22 = (bf16[192,512]{1,0:T(8,128)(2,1)S(1)}, bf16[192,512]{1,0:T(8,128)(2,1)S(1)}, u32[]{:S(2)}, u32[]{:S(2)}) collective-permute-start(bf16[192,512]{1,0:T(8,128)(2,1)S(1)} %collective-permute-done.18.refs_3_), channel_id=1, source_target_pairs={{0,1},{1,0},{2,3},{3,2},{4,5},{5,4},{6,7},{7,6},{8,9},{9,8},{10,11... | collective-permute-start | bytes 589832 | tf_op jit(solution)/shard_map/ppermute | solution.py:553
  112.5 6.1 %copy-start.7 = (bf16[192,512]{1,0:T(8,128)(2,1)}, bf16[192,512]{1,0:T(8,128)(2,1)S(1)}, u32[]{:S(2)}) copy-start(bf16[192,512]{1,0:T(8,128)(2,1)S(1)} %collective-permute-done.17.refs_2_) | copy-start | bytes 589828
  112.5 5.8 %collective-permute-start.21 = (bf16[192,512]{1,0:T(8,128)(2,1)S(1)}, bf16[192,512]{1,0:T(8,128)(2,1)S(1)}, u32[]{:S(2)}, u32[]{:S(2)}) collective-permute-start(bf16[192,512]{1,0:T(8,128)(2,1)S(1)} %collective-permute-done.17.refs_2_), channel_id=1, source_target_pairs={{0,1},{1,0},{2,3},{3,2},{4,5},{5,4},{6,7},{7,6},{8,9},{9,8},{10,11... | collective-permute-start | bytes 589832 | tf_op jit(solution)/shard_map/ppermute | solution.py:553
  116.9 1.7 %copy-start.8 = (bf16[192,512]{1,0:T(8,128)(2,1)}, bf16[192,512]{1,0:T(8,128)(2,1)S(1)}, u32[]{:S(2)}) copy-start(bf16[192,512]{1,0:T(8,128)(2,1)S(1)} %collective-permute-done.16.refs_1_) | copy-start | bytes 589828
  116.9 1.7 %collective-permute-start.20 = (bf16[192,512]{1,0:T(8,128)(2,1)S(1)}, bf16[192,512]{1,0:T(8,128)(2,1)}, u32[]{:S(2)}, u32[]{:S(2)}) collective-permute-start(bf16[192,512]{1,0:T(8,128)(2,1)S(1)} %collective-permute-done.16.refs_1_), channel_id=1, source_target_pairs={{0,1},{1,0},{2,3},{3,2},{4,5},{5,4},{6,7},{7,6},{8,9},{9,8},{10,11... | collective-permute-start | bytes 589832 | tf_op jit(solution)/shard_map/ppermute | solution.py:553
  118.3 6.4 %copy-start.17 = (bf16[192,512]{1,0:T(8,128)(2,1)}, bf16[192,512]{1,0:T(8,128)(2,1)S(1)}, u32[]{:S(2)}) copy-start(bf16[192,512]{1,0:T(8,128)(2,1)S(1)} %collective-permute-done.19.refs_4_) | copy-start | bytes 589828
  118.3 6.4 %copy-start.18 = (bf16[192,512]{1,0:T(8,128)(2,1)}, bf16[192,512]{1,0:T(8,128)(2,1)S(1)}, u32[]{:S(2)}) copy-start(bf16[192,512]{1,0:T(8,128)(2,1)S(1)} %collective-permute-done.22.refs_7_) | copy-start | bytes 589828
  118.3 6.3 %copy-start.19 = (bf16[192,512]{1,0:T(8,128)(2,1)}, bf16[192,512]{1,0:T(8,128)(2,1)S(1)}, u32[]{:S(2)}) copy-start(bf16[192,512]{1,0:T(8,128)(2,1)S(1)} %collective-permute-done.21.refs_6_) | copy-start | bytes 589828
  124.7 37.6 %all-to-all-start.1 = ((bf16[16,128,512]{2,1,0:T(8,128)(2,1)}), bf16[16,128,512]{2,1,0:T(8,128)(2,1)S(1)}, u32[]{:S(2)}, u32[]{:S(2)}) async-start(bf16[16,128,512]{2,1,0:T(8,128)(2,1)} %bitcast.33), calls=%async_computation.1 | async-start | bytes 4194304 | tf_op jit(solution)/shard_map/all_to_all | solution.py:557
  134.1 12.2 %collective-permute-start.25 = (bf16[192,1024]{1,0:T(8,128)(2,1)}, bf16[192,1024]{1,0:T(8,128)(2,1)S(1)}, u32[]{:S(2)}, u32[]{:S(2)}) collective-permute-start(bf16[192,1024]{1,0:T(8,128)(2,1)} %get-tuple-element.110), channel_id=1, source_target_pairs={{0,0},{1,2},{2,4},{3,6},{4,1},{5,3},{6,5},{7,7},{8,8},{9,10},{10,1... | collective-permute-start | bytes 1179656 | tf_op jit(solution)/shard_map/ppermute | solution.py:571
  137.6 14.8 %collective-permute-start.26 = (bf16[192,1024]{1,0:T(8,128)(2,1)}, bf16[192,1024]{1,0:T(8,128)(2,1)}, u32[]{:S(2)}, u32[]{:S(2)}) collective-permute-start(bf16[192,1024]{1,0:T(8,128)(2,1)} %get-tuple-element.111), channel_id=1, source_target_pairs={{0,6},{1,0},{2,2},{3,4},{4,7},{5,1},{6,3},{7,5},{8,14},{9,8},{10,1... | collective-permute-start | bytes 1179656 | tf_op jit(solution)/shard_map/ppermute | solution.py:571
  139.6 17.4 %collective-permute-start.23 = (bf16[192,1024]{1,0:T(8,128)(2,1)}, bf16[192,1024]{1,0:T(8,128)(2,1)S(1)}, u32[]{:S(2)}, u32[]{:S(2)}) collective-permute-start(bf16[192,1024]{1,0:T(8,128)(2,1)} %get-tuple-element.108), channel_id=1, source_target_pairs={{0,2},{1,4},{2,6},{3,0},{4,3},{5,5},{6,7},{7,1},{8,10},{9,12},{10,... | collective-permute-start | bytes 1179656 | tf_op jit(solution)/shard_map/ppermute | solution.py:571
  143.1 14.7 %collective-permute-start.24 = (bf16[192,1024]{1,0:T(8,128)(2,1)}, bf16[192,1024]{1,0:T(8,128)(2,1)S(1)}, u32[]{:S(2)}, u32[]{:S(2)}) collective-permute-start(bf16[192,1024]{1,0:T(8,128)(2,1)} %get-tuple-element.109), channel_id=1, source_target_pairs={{0,4},{1,6},{2,0},{3,2},{4,5},{5,7},{6,1},{7,3},{8,12},{9,14},{10,... | collective-permute-start | bytes 1179656 | tf_op jit(solution)/shard_map/ppermute | solution.py:571
  146.3 6.1 %copy-start.3 = (bf16[192,1024]{1,0:T(8,128)(2,1)}, bf16[192,1024]{1,0:T(8,128)(2,1)S(1)}, u32[]{:S(2)}) copy-start(bf16[192,1024]{1,0:T(8,128)(2,1)S(1)} %collective-permute-done.25.refs_0_) | copy-start | bytes 1179652
  157.0 0.8 copy-start.1
  157.8 0.8 copy-start.2
  (1 other events, 0.6 us)
